TPU v7x, 256 devices: a whole 4x4x8 slice. The times are simulated.
256 devices in a mesh: tok: 64 (over y, z, core), head: 4 (over x).
Axes of the slice: x: 4, y: 4, z: 8, core: 2. Of those that a mesh axis runs over, the one named last changes fastest.
Arguments:
- keys: bfloat16 [32768, 3072], P('tok', 'head'), may hold values from -6 to 6
- values: bfloat16 [32768, 3072], P('tok', 'head'), may hold values from -6 to 6
- rates: float32 [32768, 4], P('tok', 'head'), may hold values from 0.01 to 1
- fast_weights: bfloat16 [4, 3, 768, 768], P('head'), may hold values from -0.109375 to 0.109375
- queries: bfloat16 [16384, 3072], P('tok', 'head'), may hold values from -6 to 6
- out_proj: bfloat16 [3072, 3072], P('head'), may hold values from -0.109375 to 0.109375
Outputs:
- mixed: bfloat16 [3072, 16384], P('head', 'tok')
All inputs are finite; a program needn't handle non-finite values.
Results may differ from a plain program's by a relative error of at most 0.015.
Values may be sent and summed in bfloat16 or wider, within the bound.
No kernel may reach another device: no remote copies, remote signals or barrier semaphores. Data moves between devices by JAX's collectives and lax.ppermute only.
A program may use at most 128 MiB of HBM per device.

v0:
```python
import jax
import jax.numpy as jnp
from jax import lax
from jax.sharding import PartitionSpec as P

NS_ITERS = 2


ns_a = 3.4445
ns_b = -4.775
ns_c = 2.0315
step_scale = 1.0
eps = 1e-07


def silu_slope(pre):
    sig = jax.nn.sigmoid(pre)
    return sig * (1.0 + pre * (1.0 - sig))


def on_device(keys, values, rates, fast_weights, queries, out_proj):
    weights = fast_weights[0]
    h1 = jnp.dot(keys, weights[0], preferred_element_type=jnp.float32)
    h3 = jnp.dot(keys, weights[1], preferred_element_type=jnp.float32)
    act = jax.nn.silu(h1)
    hidden = (act * h3).astype(jnp.bfloat16)
    errors = (-rates * values.astype(jnp.float32)).astype(jnp.bfloat16)
    grad_two = lax.dot_general(
        hidden, errors, (((0,), (0,)), ((), ())), preferred_element_type=jnp.float32
    )
    dz = lax.dot_general(
        errors, weights[2], (((1,), (1,)), ((), ())), preferred_element_type=jnp.float32
    )
    grad_pre1 = (dz * h3 * silu_slope(h1)).astype(jnp.bfloat16)
    grad_pre3 = (dz * act).astype(jnp.bfloat16)
    grad_one = lax.dot_general(
        keys, grad_pre1, (((0,), (0,)), ((), ())), preferred_element_type=jnp.float32
    )
    grad_three = lax.dot_general(
        keys, grad_pre3, (((0,), (0,)), ((), ())), preferred_element_type=jnp.float32
    )
    grads = jnp.stack([grad_one, grad_three, grad_two])
    width = grads.shape[1]
    owned = width // lax.axis_size("tok")
    start_row = lax.axis_index("tok") * owned
    summed = lax.psum(grads, "tok")
    norms = jnp.sqrt(jnp.sum(summed * summed, axis=(1, 2)))
    full_iterate = (summed / (norms[:, None, None] + eps)).astype(jnp.bfloat16)
    iterate_rows = lax.dynamic_slice_in_dim(full_iterate, start_row, owned, 1)
    for turn in range(NS_ITERS):
        gram_part = jnp.einsum(
            "mij,mkj->mik", iterate_rows, full_iterate, preferred_element_type=jnp.float32
        ).astype(jnp.bfloat16)
        full_gram = lax.all_gather(gram_part, "tok", axis=1, tiled=True)
        squared = jnp.einsum(
            "mij,mjk->mik", gram_part, full_gram, preferred_element_type=jnp.float32
        )
        poly = (ns_b * gram_part.astype(jnp.float32) + ns_c * squared).astype(jnp.bfloat16)
        applied = jnp.einsum("mij,mjk->mik", poly, full_iterate, preferred_element_type=jnp.float32)
        iterate_rows = (ns_a * iterate_rows.astype(jnp.float32) + applied).astype(jnp.bfloat16)
        full_iterate = lax.all_gather(iterate_rows, "tok", axis=1, tiled=True)
    fresh = (weights.astype(jnp.float32) - step_scale * full_iterate.astype(jnp.float32)).astype(
        jnp.bfloat16
    )
    q1 = jnp.dot(queries, fresh[0], preferred_element_type=jnp.float32)
    q3 = jnp.dot(queries, fresh[1], preferred_element_type=jnp.float32)
    gated = (jax.nn.silu(q1) * q3).astype(jnp.bfloat16)
    outputs = jnp.dot(gated, fresh[2], preferred_element_type=jnp.float32).astype(jnp.bfloat16)
    mixed_rows = lax.psum_scatter(
        lax.dot_general(
            out_proj, outputs, (((0,), (1,)), ((), ())), preferred_element_type=jnp.float32
        ),
        "head",
        scatter_dimension=0,
        tiled=True,
    )
    return mixed_rows.astype(jnp.bfloat16)


def solution(mesh):
    in_specs = (
        P("tok", "head"),
        P("tok", "head"),
        P("tok", "head"),
        P("head", None, None, None),
        P("tok", "head"),
        P("head", None),
    )
    out_specs = P("head", "tok")
    return jax.shard_map(
        on_device, mesh=mesh, in_specs=in_specs, out_specs=out_specs, check_vma=False
    )
```

profile of v0, /device:TPU:1, one launch (start us, length us, event | category | flops | bytes accessed | tf_op | source)
XLA Modules:
  0.0 621.8 jit_solution(5913213091456241787)
XLA Ops:
  6.5 1.1 copy-done
  7.7 2.2 fusion.12
  12.0 1.0 convolution_bitcast_fusion.1
  13.0 1.1 convolution_bitcast_fusion.3
  15.1 3.4 pad_maximum_fusion
  18.5 204.7 %all-reduce.2.cloned.1.call-done = f32[3,768,768]{2,1,0:T(8,128)} async-done(((f32[3,768,768]{2,1,0:T(8,128)}), f32[3,768,768]{2,1,0:T(8,128)}) %all-reduce.2.cloned.1.call-update) | async-done | bytes 7077904 | tf_op jit(solution)/shard_map/psum | solution.py:46
  223.2 3.9 multiply_reduce_fusion
  227.1 1.1 copy-done.2
  229.0 1.0 convolution_convert_fusion.1
  231.4 80.2 %all-gather.5.cloned.1.call-done = bf16[3,768,768]{2,0,1:T(4,128)(2,1)} async-done(((bf16[3,12,768]{2,0,1:T(4,128)(2,1)}), bf16[3,768,768]{2,0,1:T(4,128)(2,1)}) %all-gather.5.cloned.1.call-update) | async-done | bytes 3538960 | tf_op jit(solution)/shard_map/all_gather | solution.py:54
  311.6 4.0 fusion.36
  315.6 1.6 copy.54
  317.3 76.8 %all-gather.7.cloned.1.call-done = bf16[3,768,768]{2,0,1:T(4,128)(2,1)} async-done(((bf16[3,12,768]{2,0,1:T(4,128)(2,1)}), bf16[3,768,768]{2,0,1:T(4,128)(2,1)}) %all-gather.7.cloned.1.call-update) | async-done | bytes 3538960 | tf_op jit(solution)/shard_map/all_gather | solution.py:61
  394.1 3.4 fusion.46
  398.9 76.8 %all-gather.9.cloned.1.call-done = bf16[3,768,768]{2,0,1:T(4,128)(2,1)} async-done(((bf16[3,12,768]{2,0,1:T(4,128)(2,1)}), bf16[3,768,768]{2,0,1:T(4,128)(2,1)}) %all-gather.9.cloned.1.call-update) | async-done | bytes 3538960 | tf_op jit(solution)/shard_map/all_gather | solution.py:54
  475.8 5.4 fusion.43
  481.2 1.6 copy.59
  483.0 76.7 %all-gather.11.cloned.1.call-done = bf16[3,768,768]{2,0,1:T(4,128)(2,1)} async-done(((bf16[3,12,768]{2,0,1:T(4,128)(2,1)}), bf16[3,768,768]{2,0,1:T(4,128)(2,1)}) %all-gather.11.cloned.1.call-update) | async-done | bytes 3538960 | tf_op jit(solution)/shard_map/all_gather | solution.py:61
  559.7 5.0 fusion
  564.7 1.8 convolution_bitcast_fusion.5
  566.5 3.1 convolution_convert_fusion
  569.7 5.4 convolution_bitcast_fusion
  575.1 37.8 %reduce-scatter.2.cloned.1.call-done = f32[768,256]{0,1:T(8,128)} async-done(((f32[3072,256]{0,1:T(8,128)}), f32[768,256]{0,1:T(8,128)}) %reduce-scatter.2.cloned.1.call-update) | async-done | bytes 786448 | tf_op jit(solution)/shard_map/reduce_scatter | solution.py:69
  612.8 1.2 convert_element_type.91
  (41 shorter events, 7.9 us)
Async XLA Ops:
  6.5 1.1 copy-start
  6.5 216.7 %all-reduce.2.cloned.1.call-start = ((), (), s32[]{:S(2)}) async-start(), calls=%async_computation.1 | async-start | bytes 14155776 | tf_op jit(solution)/shard_map/psum | solution.py:46
  7.7 2.4 copy-start.3
  10.0 0.8 copy-start.7
  10.0 1.1 copy-start.8
  18.5 293.1 %all-gather.5.cloned.1.call-start = ((), (), s32[]{:S(2)}) async-start(), calls=%async_computation.2 | async-start | bytes 4792320 | tf_op jit(solution)/shard_map/all_gather | solution.py:54
  223.2 5.0 copy-start.2
  230.0 0.7 copy-start.5
  231.4 162.7 %all-gather.7.cloned.1.call-start = ((), (), s32[]{:S(2)}) async-start(), calls=%async_computation.3 | async-start | bytes 4792320 | tf_op jit(solution)/shard_map/all_gather | solution.py:61
  317.2 158.5 %all-gather.9.cloned.1.call-start = ((), (), s32[]{:S(2)}) async-start(), calls=%async_computation.4 | async-start | bytes 4792320 | tf_op jit(solution)/shard_map/all_gather | solution.py:54
  397.5 0.7 copy-start.6
  398.9 160.8 %copy-start.4 = (bf16[1,3,768,768]{3,2,1,0:T(8,128)(2,1)S(1)}, bf16[1,3,768,768]{3,2,1,0:T(8,128)(2,1)}, u32[]{:S(2)}) copy-start(bf16[1,3,768,768]{3,2,1,0:T(8,128)(2,1)} %param.9) | copy-start | bytes 10616836
  398.9 160.8 %all-gather.11.cloned.1.call-start = ((), (), s32[]{:S(2)}) async-start(), calls=%async_computation.5 | async-start | bytes 4792320 | tf_op jit(solution)/shard_map/all_gather | solution.py:61
  482.8 130.0 %reduce-scatter.2.cloned.1.call-start = ((), (), s32[]{:S(2)}) async-start(), calls=%async_computation.6 | async-start | bytes 3932160 | tf_op jit(solution)/shard_map/reduce_scatter | solution.py:69
  559.7 5.0 copy-start.9
  564.7 1.8 copy-start.10
  575.0 39.9 %copy-start.1 = (bf16[512,768]{1,0:T(8,128)(2,1)S(1)}, bf16[512,768]{1,0:T(8,128)(2,1)}, u32[]{:S(2)}) copy-start(bf16[512,768]{1,0:T(8,128)(2,1)} %param.6) | copy-start | bytes 2359300
Sparse Core Ops, SparseCore 0:
  18.6 204.5 all-reduce.1
  231.5 80.0 all-gather.4
  317.3 76.7 all-gather.6
  399.0 76.7 all-gather.8
  482.9 76.7 all-gather.10
  575.2 37.5 reduce-scatter.1
where the time goes:
time: 622 us
  waiting for transfers between devices  553 us (89%)
  matrix products  31.1 us (5%)
  other arithmetic  14.2 us (2%)
  between operations  13.6 us (2%)
  local copies, waits for them, and re-layouts  9.48 us (2%)
    psum x1, waiting for transfers between devices, on_device(): summed = lax.psum(grads, 'tok')  205 us
    all_gather x2, waiting for transfers between devices, on_device(): full_gram = lax.all_gather(gram_part, 'tok', axis=1, tiled=True)  157 us
    all_gather x2, waiting for transfers between devices, on_device(): full_iterate = lax.all_gather(iterate_rows, 'tok', axis=1, tiled=True)  153 us
    reduce_scatter x1, waiting for transfers between devices, on_device(): lax.psum_scatter(lax.dot_general(out_proj, outputs, (((0,), (1,)), ((), (...  37.8 us
  transfers between devices with their start and end apart: 6, of which 6 were waited for; matrix products, arithmetic and copies ran while one was open for 0% of the time, Pallas kernels for 0%

commit v1 on v0

v1 whole, which is shorter than its diff:
```python
import jax
import jax.numpy as jnp
from jax import lax
from jax.sharding import PartitionSpec as P

NS_ITERS = 2


ns_a = 3.4445
ns_b = -4.775
ns_c = 2.0315
step_scale = 1.0
eps = 1e-07

f32 = jnp.float32
bf16 = jnp.bfloat16

NY, NZ, NC = 4, 8, 2


def chip_index(y, z, core):
    return (y * NZ + z) * NC + core


Y_GROUPS = [
    [chip_index(y, z, core) for y in range(NY)] for z in range(NZ) for core in range(NC)
]
Z_GROUPS = [
    [chip_index(y, z, core) for z in range(NZ)] for y in range(NY) for core in range(NC)
]
CORE_SWAP = [(device, device ^ 1) for device in range(NY * NZ * NC)]


def silu_slope(pre):
    sig = jax.nn.sigmoid(pre)
    return sig * (1.0 + pre * (1.0 - sig))


def swap_cores(array):
    return lax.ppermute(array, "tok", CORE_SWAP)


def exchange(blocks, groups):
    return lax.all_to_all(blocks, "tok", 0, 0, axis_index_groups=groups)


def sum_shares(blocks, groups):
    return jnp.sum(exchange(blocks, groups).astype(f32), axis=0).astype(bf16)


def gather_rows(rows, groups):
    size = len(groups[0])
    gathered = exchange(jnp.broadcast_to(rows[None], (size,) + rows.shape), groups)
    return gathered.reshape(-1, rows.shape[1])


def outer(left, right):
    return lax.dot_general(left, right, (((1,), (1,)), ((), ())), preferred_element_type=f32)


def orthogonal(parts):
    square_sum = sum(jnp.sum(part.astype(f32) * part.astype(f32)) for part in parts)
    scale = 1.0 / (jnp.sqrt(square_sum) + eps)
    for turn in range(NS_ITERS):
        gram = sum(outer(part, part) for part in parts)
        if turn == 0:
            gram = gram * (scale * scale)
        gram = gram.astype(bf16)
        squared = jnp.dot(gram, gram, preferred_element_type=f32)
        poly = (ns_b * gram.astype(f32) + ns_c * squared).astype(bf16)
        new = []
        for part in parts:
            applied = jnp.dot(poly, part, preferred_element_type=f32)
            applied = ns_a * part.astype(f32) + applied
            if turn == 0:
                applied = applied * scale
            new.append(applied.astype(bf16))
        parts = new
    return parts


def on_device(keys, values, rates, fast_weights, queries, out_proj):
    weights = fast_weights[0]
    width = weights.shape[1]
    half = width // 2
    core = lax.axis_index("tok") % NC
    head = lax.axis_index("head")
    first = core == 0

    h1 = jnp.dot(keys, weights[0], preferred_element_type=f32)
    h3 = jnp.dot(keys, weights[1], preferred_element_type=f32)
    act = jax.nn.silu(h1)
    hidden = (act * h3).astype(bf16)
    errors = (-rates * values.astype(f32)).astype(bf16)

    def token_sum(left, right):
        return lax.dot_general(left, right, (((0,), (0,)), ((), ())), preferred_element_type=f32)

    errors_keep = lax.dynamic_slice_in_dim(errors, core * half, half, 1)
    errors_send = lax.dynamic_slice_in_dim(errors, (1 - core) * half, half, 1)
    shared_got = swap_cores(token_sum(hidden, errors_send).astype(bf16))
    shared_keep = token_sum(hidden, errors_keep)
    dz = outer(errors, weights[2])
    grad_pre1 = (dz * h3 * silu_slope(h1)).astype(bf16)
    grad_pre3 = (dz * act).astype(bf16)
    own_got = swap_cores(token_sum(keys, jnp.where(first, grad_pre3, grad_pre1)).astype(bf16))
    own_keep = token_sum(keys, jnp.where(first, grad_pre1, grad_pre3))
    chip_sum = jnp.concatenate(
        [own_keep + own_got.astype(f32), shared_keep + shared_got.astype(f32)], axis=1
    ).astype(bf16)

    y_sum = sum_shares(chip_sum.reshape(NY, width // NY, -1), Y_GROUPS)
    z_sum = sum_shares(y_sum.reshape(NZ, width // NY // NZ, -1), Z_GROUPS)
    summed = gather_rows(gather_rows(z_sum, Z_GROUPS), Y_GROUPS)

    shared_part = summed[:, width:]
    shared_other = swap_cores(shared_part)
    (own_update,) = orthogonal([summed[:, :width]])
    own_weights = jnp.where(first, weights[0], weights[1])
    own_fresh = (own_weights.astype(f32) - step_scale * own_update.astype(f32)).astype(bf16)
    other_fresh = swap_cores(own_fresh)
    left = jnp.where(first, shared_part, shared_other)
    right = jnp.where(first, shared_other, shared_part)
    (shared_update,) = orthogonal([jnp.concatenate([left, right], axis=1)])
    shared_fresh = (weights[2].astype(f32) - step_scale * shared_update.astype(f32)).astype(bf16)

    q_own = jnp.dot(queries, own_fresh, preferred_element_type=f32)
    q_other = jnp.dot(queries, other_fresh, preferred_element_type=f32)
    q1 = jnp.where(first, q_own, q_other)
    q3 = jnp.where(first, q_other, q_own)
    gated = (jax.nn.silu(q1) * q3).astype(bf16)
    outputs = jnp.dot(gated, shared_fresh, preferred_element_type=f32).astype(bf16)

    heads = lax.axis_size("head")

    def contribution(target):
        columns = lax.dynamic_slice_in_dim(out_proj, target * width, width, 1)
        return lax.dot_general(columns, outputs, (((0,), (1,)), ((), ())), preferred_element_type=f32)

    got = []
    for step in (2, 1, 3):
        part = contribution((head + step) % heads).astype(bf16)
        got.append(
            lax.ppermute(part, "head", [(i, (i + step) % heads) for i in range(heads)])
        )
    mixed = contribution(head)
    for part in got:
        mixed = mixed + part.astype(f32)
    return mixed.astype(bf16)


def solution(mesh):
    in_specs = (
        P("tok", "head"),
        P("tok", "head"),
        P("tok", "head"),
        P("head", None, None, None),
        P("tok", "head"),
        P("head", None),
    )
    out_specs = P("head", "tok")
    return jax.shard_map(
        on_device, mesh=mesh, in_specs=in_specs, out_specs=out_specs, check_vma=False
    )
```

time: 622 us -> 179 us (0.29)
  waiting for transfers between devices: 553 us -> 32.1 us
  blocking collectives: 0 us -> 61.3 us
  matrix products: 31.1 us -> 54.3 us
  starting transfers between devices: 0.39 us -> 18.1 us
  between operations: 13.6 us -> 1.75 us
  other arithmetic: 14.2 us -> 6.35 us
    all_gather x4 -> x0, waiting for transfers between devices: 310 us -> none  [the longest x2 157 us: on_device(): full_gram = lax.all_gather(gram_part, 'tok', axis=1, tiled=True)]
    psum x1 -> x0, waiting for transfers between devices: 205 us -> none  [on_device(): summed = lax.psum(grads, 'tok')]
    all_to_all x0 -> x3, blocking collectives: none -> 61.3 us  [exchange(): return lax.all_to_all(blocks, 'tok', 0, 0, axis_index_groups=groups)]
    reduce_scatter x1 -> x0, waiting for transfers between devices: 37.8 us -> none  [on_device(): lax.psum_scatter(lax.dot_general(out_proj, outputs, (((0,), (1,)), ((), (...]
    dot_general x13 -> x21, matrix products: 31.1 us -> 54.3 us  [the longest x3 16.3 us: orthogonal(): applied = jnp.dot(poly, part, preferred_element_type=f32)]
    all_to_all x0 -> x1, waiting for transfers between devices: none -> 18.1 us  [exchange(): return lax.all_to_all(blocks, 'tok', 0, 0, axis_index_groups=groups)]
    ppermute x0 -> x7, starting transfers between devices: none -> 14.6 us  [the longest x4 8.89 us: swap_cores(): return lax.ppermute(array, 'tok', CORE_SWAP)]
    ppermute x0 -> x7, waiting for transfers between devices: none -> 14 us  [the longest x3 11.8 us: on_device(): lax.ppermute(part, 'head', [(i, (i + step) % heads) for i in range(heads)])]
  transfers between devices with their start and end apart: 6 -> 8, of which waited for: 6 -> 4; matrix products, arithmetic and copies ran while one was open for 0% -> 16% of each run, Pallas kernels for 0% -> 0%
where the time goes in v1:
time: 179 us; the launch traced here: 178 us
  blocking collectives  61.3 us (34%)
  matrix products  54.3 us (30%)
  waiting for transfers between devices  32.1 us (18%)
  starting transfers between devices  18.1 us (10%)
  other arithmetic  6.35 us (4%)
  local copies, waits for them, and re-layouts  4.28 us (2%)
    all_to_all x3, blocking collectives, exchange(): return lax.all_to_all(blocks, 'tok', 0, 0, axis_index_groups=groups)  61.3 us
    all_to_all x1, waiting for transfers between devices, exchange(): return lax.all_to_all(blocks, 'tok', 0, 0, axis_index_groups=groups)  18.1 us
    dot_general x3, matrix products, orthogonal(): applied = jnp.dot(poly, part, preferred_element_type=f32)  16.3 us
    dot_general x5, matrix products, outer(): lax.dot_general(left, right, (((1,), (1,)), ((), ())), preferred_element_...  12.7 us
    ppermute x3, waiting for transfers between devices, on_device(): lax.ppermute(part, 'head', [(i, (i + step) % heads) for i in range(heads)])  11.8 us
    ppermute x4, starting transfers between devices, swap_cores(): return lax.ppermute(array, 'tok', CORE_SWAP)  8.89 us
    dot_general x4, matrix products, contribution(): lax.dot_general(columns, outputs, (((0,), (1,)), ((), ())), preferred_ele...  7.9 us
    dot_general x4, matrix products, token_sum(): lax.dot_general(left, right, (((0,), (0,)), ((), ())), preferred_element_...  5.82 us
  transfers between devices with their start and end apart: 8, of which 4 were waited for; matrix products, arithmetic and copies ran while one was open for 16% of the time, Pallas kernels for 0%

profile of v1, /device:TPU:1, one launch (start us, length us, event | category | flops | bytes accessed | tf_op | source)
XLA Modules:
  0.0 178.2 jit_solution(540615475381520614)
XLA Ops:
  2.1 2.2 %fusion.11 = f32[512,768]{1,0:T(8,128)S(1)} fusion(bf16[512,768]{1,0:T(8,128)(2,1)S(1)} %multiply_convert_fusion.5, bf16[1,3,768,768]{3,2,1,0:T(8,128)(2,1)} %param.9), kind=kOutput, calls=%fused_computation.41 | convolution fusion | flops 603979776 | bytes 3538944 | tf_op jit(solution)/shard_map/dot_general | solution.py:58
  7.5 1.8 %fusion.10 = bf16[768,768]{1,0:T(8,128)(2,1)} fusion(bf16[512,768]{1,0:T(8,128)(2,1)S(1)} %copy-done, bf16[512,768]{1,0:T(8,128)(2,1)S(1)} %get-tuple-element.7, bf16[512,768]{1,0:T(8,128)(2,1)S(1)} %get-tuple-element.5, pred[]{:T(512)S(6)} %eq.8), kind=kOutput, calls=%fused_computation.34 | convolution fusion | flops 604962816 | bytes 3538945 | tf_op jit(solution)/shard_map/dot_general | solution.py:97
  9.4 3.2 %collective-permute-start = (bf16[768,768]{1,0:T(8,128)(2,1)}, bf16[768,768]{1,0:T(8,128)(2,1)S(1)}, u32[]{:S(2)}, u32[]{:S(2)}) collective-permute-start(bf16[768,768]{1,0:T(8,128)(2,1)} %fusion.10), channel_id=1, source_target_pairs={{0,4},{4,0},{8,12},{12,8},{16,20},{20,16},{24,28},{28,24},{32,36},... | collective-permute-start | bytes 3538952 | tf_op jit(solution)/shard_map/ppermute | solution.py:40
  14.0 2.2 %collective-permute-done.1 = bf16[768,384]{1,0:T(8,128)(2,1)S(1)} collective-permute-done((bf16[768,384]{1,0:T(8,128)(2,1)}, bf16[768,384]{1,0:T(8,128)(2,1)S(1)}, u32[]{:S(2)}, u32[]{:S(2)}) %collective-permute-start.1) | collective-permute-done | bytes 589856 | tf_op jit(solution)/shard_map/ppermute | solution.py:40
  19.0 24.7 %all_to_all.20 = bf16[4,192,1152]{2,1,0:T(8,128)(2,1)S(1)} all-to-all(bf16[4,192,1152]{2,1,0:T(8,128)(2,1)S(1)} %pad_maximum_fusion), channel_id=1, replica_groups={{0,64,128,192},{4,68,132,196},{8,72,136,200},{12,76,140,204},{16,80,144..., dimensions={0} | all-to-all | bytes 3538944 | tf_op jit(solution)/shard_map/all_to_all | solution.py:44
  44.2 21.5 %all_to_all.21 = bf16[8,24,1152]{2,1,0:T(8,128)(2,1)S(1)} all-to-all(bf16[8,24,1152]{2,1,0:T(8,128)(2,1)S(1)} %bitcast.84), channel_id=1, replica_groups={{0,8,16,24,32,40,48,56},{4,12,20,28,36,44,52,60},{64,72,80,88,96,104,11..., dimensions={0} | all-to-all | bytes 884736 | tf_op jit(solution)/shard_map/all_to_all | solution.py:44
  65.7 15.1 %all_to_all.22 = bf16[8,24,1152]{2,1,0:T(8,128)(2,1)S(1)} all-to-all(bf16[8,24,1152]{2,1,0:T(8,128)(2,1)S(1)} %broadcast_in_dim.6), channel_id=1, replica_groups={{0,8,16,24,32,40,48,56},{4,12,20,28,36,44,52,60},{64,72,80,88,96,104,11..., dimensions={0} | all-to-all | bytes 884736 | tf_op jit(solution)/shard_map/all_to_all | solution.py:44
  82.2 3.6 %all-to-all-start.3 = ((bf16[4,192,1152]{2,1,0:T(8,128)(2,1)}), bf16[4,192,1152]{2,1,0:T(8,128)(2,1)S(1)}, u32[]{:S(2)}, u32[]{:S(2)}) async-start(bf16[4,192,1152]{2,1,0:T(8,128)(2,1)} %broadcast_in_dim.15), calls=%async_computation.3 | async-start | bytes 3538944 | tf_op jit(solution)/shard_map/all_to_all | solution.py:44
  85.9 18.1 %all-to-all-done.3 = bf16[4,192,1152]{2,1,0:T(8,128)(2,1)S(1)} async-done(((bf16[4,192,1152]{2,1,0:T(8,128)(2,1)}), bf16[4,192,1152]{2,1,0:T(8,128)(2,1)S(1)}, u32[]{:S(2)}, u32[]{:S(2)}) %all-to-all-start.3) | async-done | bytes 1769504 | tf_op jit(solution)/shard_map/all_to_all | solution.py:44
  106.0 2.1 %multiply_convert_fusion.1 = bf16[768,768]{1,0:T(8,128)(2,1)} fusion(f32[]{:T(128)S(6)} %mul.144, bf16[768,1152]{1,0:T(8,128)(2,1)S(1)} %bitcast.81), kind=kOutput, calls=%fused_computation.23 | convolution fusion | flops 907149312 | bytes 2359300 | tf_op jit(solution)/shard_map/dot_general | solution.py:58
  108.1 5.5 %fusion.2 = bf16[768,768]{1,0:T(8,128)(2,1)} fusion(f32[]{:T(128)S(6)} %div.16, bf16[768,1152]{1,0:T(8,128)(2,1)S(1)} %bitcast.82, bf16[768,768]{1,0:T(8,128)(2,1)} %multiply_convert_fusion.1), kind=kOutput, calls=%fused_computation.6 | convolution fusion | flops 1817837568 | bytes 7077892 | tf_op jit(solution)/shard_map/dot_general | solution.py:73
  113.6 3.8 %convolution_convert_fusion.1 = bf16[768,768]{1,0:T(8,128)(2,1)} fusion(bf16[768,768]{1,0:T(8,128)(2,1)} %fusion.2), kind=kOutput, calls=%fused_computation.32 | convolution fusion | flops 906559488 | bytes 2359296 | tf_op jit(solution)/shard_map/dot_general | solution.py:58
  117.4 5.6 %collective-permute-start.3 = (bf16[768,384]{1,0:T(8,128)(2,1)S(1)}, bf16[768,384]{1,0:T(8,128)(2,1)}, u32[]{:S(2)}, u32[]{:S(2)}) collective-permute-start(bf16[768,384]{1,0:T(8,128)(2,1)S(1)} %slice.27), channel_id=1, source_target_pairs={{0,4},{4,0},{8,12},{12,8},{16,20},{20,16},{24,28},{28,24},{32,36},... | collective-permute-start | bytes 1769480 | tf_op jit(solution)/shard_map/ppermute | solution.py:40
  123.0 6.6 %subtract_convert_fusion.1 = bf16[768,768]{1,0:T(8,128)(2,1)} fusion(bf16[768,768]{1,0:T(8,128)(2,1)} %fusion.2, pred[]{:T(512)S(6)} %eq.8, bf16[1,3,768,768]{3,2,1,0:T(8,128)(2,1)} %param.9, bf16[768,768]{1,0:T(8,128)(2,1)} %convolution_convert_fusion.1), kind=kOutput, calls=%fused_computation.19 | convolution fusion | flops 1820196864 | bytes 9437185 | tf_op jit(solution)/shard_map/dot_general | solution.py:73
  129.6 2.7 %fusion.65 = f32[768,256]{1,0:T(8,128)} fusion(bf16[768,768]{1,0:T(8,128)(2,1)} %subtract_convert_fusion.1, bf16[256,768]{1,0:T(8,128)(2,1)S(1)} %copy-done.4), kind=kOutput, calls=%fused_computation.97 | convolution fusion | flops 301989888 | bytes 2359296 | tf_op jit(solution)/shard_map/dot_general | solution.py:127
  136.2 3.5 %multiply_convert_fusion = bf16[768,768]{1,0:T(8,128)(2,1)} fusion(f32[]{:T(128)S(6)} %mul.158, bf16[768,384]{1,0:T(8,128)(2,1)} %copy-done.1, bf16[768,384]{1,0:T(8,128)(2,1)S(1)} %get-tuple-element.8), kind=kOutput, calls=%fused_computation.18 | convolution fusion | flops 909508608 | bytes 2359300 | tf_op jit(solution)/shard_map/dot_general | solution.py:58
  139.7 4.2 %fusion.6 = bf16[768,768]{1,0:T(8,128)(2,1)S(1)} fusion(f32[]{:T(128)S(6)} %div.18, bf16[768,768]{1,0:T(8,128)(2,1)} %multiply_convert_fusion, bf16[768,384]{1,0:T(8,128)(2,1)S(1)} %copy-done.2, bf16[768,384]{1,0:T(8,128)(2,1)S(1)} %get-tuple-element.8), kind=kOutput, calls=%fused_computation.10 | convolution fusion | flops 1821966336 | bytes 3538948 | tf_op jit(solution)/shard_map/dot_general | solution.py:73
  146.1 2.1 %add_convert_fusion.1 = bf16[768,768]{1,0:T(8,128)(2,1)} fusion(bf16[768,768]{1,0:T(8,128)(2,1)S(1)} %convolution_convert_fusion), kind=kOutput, calls=%fused_computation.16 | convolution fusion | flops 908918784 | bytes 2359296 | tf_op jit(solution)/shard_map/dot_general | solution.py:69
  148.3 4.5 %convolution_convert_fusion.7 = bf16[256,768]{1,0:T(8,128)(2,1)S(1)} fusion(bf16[768,768]{1,0:T(8,128)(2,1)} %add_convert_fusion.1, bf16[768,768]{1,0:T(8,128)(2,1)} %copy-done.11, bf16[1,3,768,768]{3,2,1,0:T(8,128)(2,1)} %param.9, f32[768,256]{1,0:T(8,128)S(1)} %copy-done.3, pred[]{:T(512)S(6)} %eq.8, bf16[768,768]{1,0:T(8,128)(2,1)} %collective-permute-done.2, ...), kind=kOutput, calls=%fused_computation.39 | convolution fusion | flops 1516437504 | bytes 7471105 | tf_op jit(solution)/shard_map/dot_general | solution.py:132
  154.6 2.8 %collective-permute-start.4 = (bf16[768,256]{1,0:T(8,128)(2,1)S(1)}, bf16[768,256]{1,0:T(8,128)(2,1)S(1)}, u32[]{:S(2)}, u32[]{:S(2)}) collective-permute-start(bf16[768,256]{1,0:T(8,128)(2,1)S(1)} %convolution_convert_fusion.6), channel_id=1, source_target_pairs={{0,2},{1,3},{2,0},{3,1},{4,6},{5,7},{6,4},{7,5},{8,10},{9,11},{10,... | collective-permute-start | bytes 1179656 | tf_op jit(solution)/shard_map/ppermute | solution.py:144
  161.4 2.4 %collective-permute-start.6 = (bf16[768,256]{1,0:T(8,128)(2,1)S(1)}, bf16[768,256]{1,0:T(8,128)(2,1)S(1)}, u32[]{:S(2)}, u32[]{:S(2)}) collective-permute-start(bf16[768,256]{1,0:T(8,128)(2,1)S(1)} %convolution_convert_fusion.4), channel_id=1, source_target_pairs={{0,3},{1,0},{2,1},{3,2},{4,7},{5,4},{6,5},{7,6},{8,11},{9,8},{10,9... | collective-permute-start | bytes 1179656 | tf_op jit(solution)/shard_map/ppermute | solution.py:144
  163.8 2.6 %collective-permute-done.4 = bf16[768,256]{1,0:T(8,128)(2,1)S(1)} collective-permute-done((bf16[768,256]{1,0:T(8,128)(2,1)S(1)}, bf16[768,256]{1,0:T(8,128)(2,1)S(1)}, u32[]{:S(2)}, u32[]{:S(2)}) %collective-permute-start.4) | collective-permute-done | bytes 393248 | tf_op jit(solution)/shard_map/ppermute | solution.py:144
  166.4 9.2 %collective-permute-done.5 = bf16[768,256]{1,0:T(8,128)(2,1)S(1)} collective-permute-done((bf16[768,256]{1,0:T(8,128)(2,1)S(1)}, bf16[768,256]{1,0:T(8,128)(2,1)S(1)}, u32[]{:S(2)}, u32[]{:S(2)}) %collective-permute-start.5) | collective-permute-done | bytes 393248 | tf_op jit(solution)/shard_map/ppermute | solution.py:144
  175.7 2.5 %add_convert_fusion.7 = bf16[768,256]{1,0:T(8,128)(2,1)} fusion(bf16[768,256]{1,0:T(8,128)(2,1)S(1)} %collective-permute-done.6, bf16[768,256]{1,0:T(8,128)(2,1)S(1)} %collective-permute-done.5, bf16[768,256]{1,0:T(8,128)(2,1)S(1)} %collective-permute-done.4, bf16[256,768]{1,0:T(8,128)(2,1)S(1)} %convolution_convert_fusion.7, bf16[768,3072]{1,0:T(8,128)(2,1)} %param.11, ...), kind=kOutput, calls=%fused_computation.68 | convolution fusion | flops 303366144 | bytes 3145732 | tf_op jit(solution)/shard_map/dot_general | solution.py:138
  (51 shorter events, 23.7 us)
Async XLA Ops:
  0.0 4.3 %copy-start = (bf16[512,768]{1,0:T(8,128)(2,1)S(1)}, bf16[512,768]{1,0:T(8,128)(2,1)}, u32[]{:S(2)}) copy-start(bf16[512,768]{1,0:T(8,128)(2,1)} %param.6) | copy-start | bytes 2359300
  2.1 2.4 %copy-start.5 = (bf16[1,3,768,768]{3,2,1,0:T(8,128)(2,1)S(1)}, bf16[1,3,768,768]{3,2,1,0:T(8,128)(2,1)}, u32[]{:S(2)}) copy-start(bf16[1,3,768,768]{3,2,1,0:T(8,128)(2,1)} %param.9) | copy-start | bytes 10616836
  6.6 0.9 copy-start.7
  6.6 2.8 %copy-start.9 = (bf16[512,768]{1,0:T(8,128)(2,1)}, bf16[512,768]{1,0:T(8,128)(2,1)S(1)}, u32[]{:S(2)}) copy-start(bf16[512,768]{1,0:T(8,128)(2,1)S(1)} %get-tuple-element.7) | copy-start | bytes 2359300
  6.6 6.0 %copy-start.6 = (bf16[512,768]{1,0:T(8,128)(2,1)}, bf16[512,768]{1,0:T(8,128)(2,1)S(1)}, u32[]{:S(2)}) copy-start(bf16[512,768]{1,0:T(8,128)(2,1)S(1)} %get-tuple-element.6) | copy-start | bytes 2359300
  9.4 8.6 %collective-permute-start = (bf16[768,768]{1,0:T(8,128)(2,1)}, bf16[768,768]{1,0:T(8,128)(2,1)S(1)}, u32[]{:S(2)}, u32[]{:S(2)}) collective-permute-start(bf16[768,768]{1,0:T(8,128)(2,1)} %fusion.10), channel_id=1, source_target_pairs={{0,4},{4,0},{8,12},{12,8},{16,20},{20,16},{24,28},{28,24},{32,36},... | collective-permute-start | bytes 3538952 | tf_op jit(solution)/shard_map/ppermute | solution.py:40
  14.0 2.2 %collective-permute-start.1 = (bf16[768,384]{1,0:T(8,128)(2,1)}, bf16[768,384]{1,0:T(8,128)(2,1)S(1)}, u32[]{:S(2)}, u32[]{:S(2)}) collective-permute-start(bf16[768,384]{1,0:T(8,128)(2,1)} %convolution_convert_fusion.3), channel_id=1, source_target_pairs={{0,4},{4,0},{8,12},{12,8},{16,20},{20,16},{24,28},{28,24},{32,36},... | collective-permute-start | bytes 1769480 | tf_op jit(solution)/shard_map/ppermute | solution.py:40
  14.0 4.0 %copy-start.8 = (bf16[512,768]{1,0:T(8,128)(2,1)S(1)}, bf16[512,768]{1,0:T(8,128)(2,1)}, u32[]{:S(2)}) copy-start(bf16[512,768]{1,0:T(8,128)(2,1)} %copy-done.7) | copy-start | bytes 2359300
  14.0 4.0 %copy-start.10 = (bf16[512,768]{1,0:T(8,128)(2,1)S(1)}, bf16[512,768]{1,0:T(8,128)(2,1)}, u32[]{:S(2)}) copy-start(bf16[512,768]{1,0:T(8,128)(2,1)} %copy-done.9) | copy-start | bytes 2359300
  82.2 21.7 %all-to-all-start.3 = ((bf16[4,192,1152]{2,1,0:T(8,128)(2,1)}), bf16[4,192,1152]{2,1,0:T(8,128)(2,1)S(1)}, u32[]{:S(2)}, u32[]{:S(2)}) async-start(bf16[4,192,1152]{2,1,0:T(8,128)(2,1)} %broadcast_in_dim.15), calls=%async_computation.3 | async-start | bytes 3538944 | tf_op jit(solution)/shard_map/all_to_all | solution.py:44
  117.4 12.2 %copy-start.4 = (bf16[256,768]{1,0:T(8,128)(2,1)S(1)}, bf16[256,768]{1,0:T(8,128)(2,1)}, u32[]{:S(2)}) copy-start(bf16[256,768]{1,0:T(8,128)(2,1)} %param.10) | copy-start | bytes 1179652
  117.4 14.9 %collective-permute-start.3 = (bf16[768,384]{1,0:T(8,128)(2,1)S(1)}, bf16[768,384]{1,0:T(8,128)(2,1)}, u32[]{:S(2)}, u32[]{:S(2)}) collective-permute-start(bf16[768,384]{1,0:T(8,128)(2,1)S(1)} %slice.27), channel_id=1, source_target_pairs={{0,4},{4,0},{8,12},{12,8},{16,20},{20,16},{24,28},{28,24},{32,36},... | collective-permute-start | bytes 1769480 | tf_op jit(solution)/shard_map/ppermute | solution.py:40
  129.6 18.7 %collective-permute-start.2 = (bf16[768,768]{1,0:T(8,128)(2,1)}, bf16[768,768]{1,0:T(8,128)(2,1)}, u32[]{:S(2)}, u32[]{:S(2)}) collective-permute-start(bf16[768,768]{1,0:T(8,128)(2,1)} %subtract_convert_fusion.1), channel_id=1, source_target_pairs={{0,4},{4,0},{8,12},{12,8},{16,20},{20,16},{24,28},{28,24},{32,36},... | collective-permute-start | bytes 3538952 | tf_op jit(solution)/shard_map/ppermute | solution.py:40
  133.5 0.8 copy-start.1
  136.2 3.5 %copy-start.2 = (bf16[768,384]{1,0:T(8,128)(2,1)S(1)}, bf16[768,384]{1,0:T(8,128)(2,1)}, u32[]{:S(2)}) copy-start(bf16[768,384]{1,0:T(8,128)(2,1)} %copy-done.1) | copy-start | bytes 1769476
  143.9 1.0 copy-start.11
  146.1 2.2 %copy-start.3 = (f32[768,256]{1,0:T(8,128)S(1)}, f32[768,256]{1,0:T(8,128)}, u32[]{:S(2)}) copy-start(f32[768,256]{1,0:T(8,128)} %fusion.65) | copy-start | bytes 2359300
  154.6 11.8 %collective-permute-start.4 = (bf16[768,256]{1,0:T(8,128)(2,1)S(1)}, bf16[768,256]{1,0:T(8,128)(2,1)S(1)}, u32[]{:S(2)}, u32[]{:S(2)}) collective-permute-start(bf16[768,256]{1,0:T(8,128)(2,1)S(1)} %convolution_convert_fusion.6), channel_id=1, source_target_pairs={{0,2},{1,3},{2,0},{3,1},{4,6},{5,7},{6,4},{7,5},{8,10},{9,11},{10,... | collective-permute-start | bytes 1179656 | tf_op jit(solution)/shard_map/ppermute | solution.py:144
  159.2 16.4 %collective-permute-start.5 = (bf16[768,256]{1,0:T(8,128)(2,1)S(1)}, bf16[768,256]{1,0:T(8,128)(2,1)S(1)}, u32[]{:S(2)}, u32[]{:S(2)}) collective-permute-start(bf16[768,256]{1,0:T(8,128)(2,1)S(1)} %convolution_convert_fusion.5), channel_id=1, source_target_pairs={{0,1},{1,2},{2,3},{3,0},{4,5},{5,6},{6,7},{7,4},{8,9},{9,10},{10,1... | collective-permute-start | bytes 1179656 | tf_op jit(solution)/shard_map/ppermute | solution.py:144
  161.4 14.2 %collective-permute-start.6 = (bf16[768,256]{1,0:T(8,128)(2,1)S(1)}, bf16[768,256]{1,0:T(8,128)(2,1)S(1)}, u32[]{:S(2)}, u32[]{:S(2)}) collective-permute-start(bf16[768,256]{1,0:T(8,128)(2,1)S(1)} %convolution_convert_fusion.4), channel_id=1, source_target_pairs={{0,3},{1,0},{2,1},{3,2},{4,7},{5,4},{6,5},{7,6},{8,11},{9,8},{10,9... | collective-permute-start | bytes 1179656 | tf_op jit(solution)/shard_map/ppermute | solution.py:144

commit v2 on v1

v2 whole, which is shorter than its diff:
```python
import jax
import jax.numpy as jnp
from jax import lax
from jax.experimental import pallas as pl
from jax.experimental.pallas import tpu as pltpu
from jax.sharding import PartitionSpec as P

NS_ITERS = 2


ns_a = 3.4445
ns_b = -4.775
ns_c = 2.0315
step_scale = 1.0
eps = 1e-07

f32 = jnp.float32
bf16 = jnp.bfloat16

NY, NZ, NC = 4, 8, 2
ROWS = 256


def chip_index(y, z, core):
    return (y * NZ + z) * NC + core


Y_GROUPS = [
    [chip_index(y, z, core) for y in range(NY)] for z in range(NZ) for core in range(NC)
]
Z_GROUPS = [
    [chip_index(y, z, core) for z in range(NZ)] for y in range(NY) for core in range(NC)
]
CORE_SWAP = [(device, device ^ 1) for device in range(NY * NZ * NC)]

SMEM = pl.BlockSpec(memory_space=pltpu.SMEM)
VMEM = pl.BlockSpec(memory_space=pltpu.VMEM)
ANY = pl.BlockSpec(memory_space=pl.ANY)


def swap_cores(array):
    return lax.ppermute(array, "tok", CORE_SWAP)


def exchange(blocks, groups):
    return lax.all_to_all(blocks, "tok", 0, 0, axis_index_groups=groups)


def sum_shares(blocks, groups):
    return jnp.sum(exchange(blocks, groups).astype(f32), axis=0).astype(bf16)


def gather_rows(rows, groups):
    size = len(groups[0])
    gathered = exchange(jnp.broadcast_to(rows[None], (size,) + rows.shape), groups)
    return gathered.reshape(-1, rows.shape[1])


def dot(left, right):
    return jnp.dot(left, right, preferred_element_type=f32)


def dot_nt(left, right):
    return lax.dot_general(left, right, (((1,), (1,)), ((), ())), preferred_element_type=f32)


def dot_tn(left, right):
    return lax.dot_general(left, right, (((0,), (0,)), ((), ())), preferred_element_type=f32)


def call(body, outs, in_specs, scratch, mib, flops, moved, name):
    return pl.pallas_call(
        body,
        out_shape=outs,
        in_specs=in_specs,
        scratch_shapes=scratch,
        compiler_params=pltpu.CompilerParams(vmem_limit_bytes=mib << 20),
        cost_estimate=pl.CostEstimate(flops=flops, bytes_accessed=moved, transcendentals=0),
        name=name,
    )


def shape(*dims, dtype=bf16):
    return jax.ShapeDtypeStruct(dims, dtype)


def gradients(core, keys, values, rates, weights):
    tokens, width = keys.shape
    half = width // 2

    def body(core_ref, k_ref, v_ref, r_ref, w_ref, own_send, shared_send, own_keep, shared_keep,
             hidden, errors, g_keep, g_send):
        first = core_ref[0] == 0
        for row in range(0, tokens, ROWS):
            rows = slice(row, row + ROWS)
            k = k_ref[rows, :]
            h1 = dot(k, w_ref[0, 0])
            h3 = dot(k, w_ref[0, 1])
            sig = jax.nn.sigmoid(h1)
            act = h1 * sig
            hidden[rows, :] = (act * h3).astype(bf16)
            e = (-r_ref[rows, :] * v_ref[rows, :].astype(f32)).astype(bf16)
            errors[rows, :] = e
            dz = dot_nt(e, w_ref[0, 2])
            g1 = (dz * h3 * (sig * (1.0 + h1 * (1.0 - sig)))).astype(bf16)
            g3 = (dz * act).astype(bf16)
            g_keep[rows, :] = jnp.where(first, g1, g3)
            g_send[rows, :] = jnp.where(first, g3, g1)
        own_send[...] = dot_tn(k_ref[...], g_send[...]).astype(bf16)
        own_keep[...] = dot_tn(k_ref[...], g_keep[...])
        left = dot_tn(hidden[...], errors[:, :half])
        right = dot_tn(hidden[...], errors[:, half:])
        shared_keep[...] = jnp.where(first, left, right)
        shared_send[...] = jnp.where(first, right, left).astype(bf16)

    return call(
        body,
        [
            shape(width, width),
            shape(width, half),
            shape(width, width, dtype=f32),
            shape(width, half, dtype=f32),
        ],
        [SMEM] + [VMEM] * 4,
        [pltpu.VMEM((tokens, width), bf16)] * 4,
        32,
        12 * tokens * width * width,
        12 * width * width,
        "gradients",
    )(core, keys, values, rates, weights)


def newton_schulz(x_ref, w_ref, out_ref, gram, poly, other):
    width = x_ref.shape[0]
    blocks = [slice(row, row + ROWS) for row in range(0, width, ROWS)]
    square_sum = jnp.zeros((1, 1), f32)
    for rows in blocks:
        wide = x_ref[rows, :].astype(f32)
        square_sum = square_sum + jnp.sum(wide * wide).reshape(1, 1)
    scale = 1.0 / (jnp.sqrt(square_sum) + eps)
    now = x_ref
    for turn in range(NS_ITERS):
        for rows in blocks:
            product = dot_nt(now[rows, :], now[...])
            if turn == 0:
                product = product * (scale * scale)
            gram[rows, :] = product.astype(bf16)
        for rows in blocks:
            squared = dot(gram[rows, :], gram[...])
            poly[rows, :] = (ns_b * gram[rows, :].astype(f32) + ns_c * squared).astype(bf16)
        for rows in blocks:
            new = ns_a * now[rows, :].astype(f32) + dot(poly[rows, :], now[...])
            if turn == 0:
                new = new * scale
            new = new.astype(bf16)
            if turn < NS_ITERS - 1:
                other[rows, :] = new
            else:
                step = step_scale * new.astype(f32)
                out_ref[rows, :] = (w_ref[rows, :].astype(f32) - step).astype(bf16)
        now = other


def own_step(core, summed, weights):
    width = weights.shape[-1]

    def body(core_ref, x_ref, w_hbm, out_ref, gram, poly, other, w_ref, sem):
        copy = pltpu.make_async_copy(w_hbm.at[0, core_ref[0]], w_ref, sem)
        copy.start()
        copy.wait()
        newton_schulz(x_ref, w_ref, out_ref, gram, poly, other)

    return call(
        body,
        shape(width, width),
        [SMEM, VMEM, ANY],
        [pltpu.VMEM((width, width), bf16)] * 4 + [pltpu.SemaphoreType.DMA],
        20,
        12 * width**3,
        6 * width * width,
        "own_step",
    )(core, summed, weights)


def shared_step(core, mine, partners, weights):
    width = weights.shape[-1]
    half = width // 2

    def body(core_ref, a_ref, b_ref, w_hbm, out_ref, gram, poly, other, x_ref, w_ref, sem):
        copy = pltpu.make_async_copy(w_hbm.at[0, 2], w_ref, sem)
        copy.start()
        first = core_ref[0] == 0
        x_ref[:, :half] = jnp.where(first, a_ref[...], b_ref[...])
        x_ref[:, half:] = jnp.where(first, b_ref[...], a_ref[...])
        copy.wait()
        newton_schulz(x_ref, w_ref, out_ref, gram, poly, other)

    return call(
        body,
        shape(width, width),
        [SMEM, VMEM, VMEM, ANY],
        [pltpu.VMEM((width, width), bf16)] * 5 + [pltpu.SemaphoreType.DMA],
        20,
        12 * width**3,
        6 * width * width,
        "shared_step",
    )(core, mine, partners, weights)


def project(place, queries, own, other, shared, out_proj):
    tokens, width = queries.shape
    heads = out_proj.shape[1] // width

    def body(place_ref, q_ref, own_ref, other_ref, shared_ref, p_hbm, *rest):
        outs, p_ref, sems = rest[:heads], rest[heads], rest[heads + 1]
        copies = []
        for step in range(heads):
            head = lax.rem(place_ref[1] + step, heads)
            start = pl.multiple_of(head * width, width)
            copies.append(
                pltpu.make_async_copy(
                    p_hbm.at[:, pl.ds(start, width)], p_ref.at[step], sems.at[step]
                )
            )
        for copy in copies:
            copy.start()
        first = place_ref[0] == 0
        q_own = dot(q_ref[...], own_ref[...])
        q_other = dot(q_ref[...], other_ref[...])
        q1 = jnp.where(first, q_own, q_other)
        q3 = jnp.where(first, q_other, q_own)
        gated = (q1 * jax.nn.sigmoid(q1) * q3).astype(bf16)
        outputs = dot(gated, shared_ref[...]).astype(bf16)
        for step in range(heads):
            copies[step].wait()
            outs[step][...] = dot(outputs, p_ref[step]).astype(outs[step].dtype)

    return call(
        body,
        [shape(tokens, width, dtype=f32)] + [shape(tokens, width)] * (heads - 1),
        [SMEM] + [VMEM] * 4 + [ANY],
        [pltpu.VMEM((heads, width, width), bf16), pltpu.SemaphoreType.DMA((heads,))],
        24,
        2 * tokens * width * width * (3 + heads),
        16 * width * width,
        "project",
    )(place, queries, own, other, shared, out_proj)


def mix(own, *got):
    tokens, width = own.shape

    def body(*refs):
        total = refs[0][...]
        for ref in refs[1:-1]:
            total = total + ref[...].astype(f32)
        refs[-1][...] = total.T.astype(bf16)

    return call(
        body, shape(width, tokens), [VMEM] * (1 + len(got)), [], 16, 0, 12 * tokens * width, "mix"
    )(own, *got)


def on_device(keys, values, rates, fast_weights, queries, out_proj):
    width = fast_weights.shape[-1]
    core = lax.axis_index("tok") % NC
    head = lax.axis_index("head")
    heads = lax.axis_size("head")
    place = jnp.stack([core, head]).astype(jnp.int32)

    own_send, shared_send, own_keep, shared_keep = gradients(
        place, keys, values, rates, fast_weights
    )
    shared_got = swap_cores(shared_send)
    own_got = swap_cores(own_send)
    chip_sum = jnp.concatenate(
        [own_keep + own_got.astype(f32), shared_keep + shared_got.astype(f32)], axis=1
    ).astype(bf16)

    y_sum = sum_shares(chip_sum.reshape(NY, width // NY, -1), Y_GROUPS)
    z_sum = sum_shares(y_sum.reshape(NZ, width // NY // NZ, -1), Z_GROUPS)
    summed = gather_rows(gather_rows(z_sum, Z_GROUPS), Y_GROUPS)

    shared_part = summed[:, width:]
    shared_other = swap_cores(shared_part)
    own_fresh = own_step(place, summed[:, :width], fast_weights)
    other_fresh = swap_cores(own_fresh)
    shared_fresh = shared_step(place, shared_part, shared_other, fast_weights)

    mixed, *parts = project(place, queries, own_fresh, other_fresh, shared_fresh, out_proj)
    got = [
        lax.ppermute(part, "head", [(i, (i + step) % heads) for i in range(heads)])
        for step, part in enumerate(parts, 1)
    ]
    return mix(mixed, *got)


def solution(mesh):
    in_specs = (
        P("tok", "head"),
        P("tok", "head"),
        P("tok", "head"),
        P("head", None, None, None),
        P("tok", "head"),
        P("head", None),
    )
    out_specs = P("head", "tok")
    return jax.shard_map(
        on_device, mesh=mesh, in_specs=in_specs, out_specs=out_specs, check_vma=False
    )
```

time: 179 us -> 151 us (0.84)
  matrix products: 54.3 us -> 0 us
  Pallas kernels: 0 us -> 24.6 us
  blocking collectives: 61.3 us -> 82.1 us
  waiting for transfers between devices: 32.1 us -> 22.3 us
  other arithmetic: 6.35 us -> 1.23 us
  starting transfers between devices: 18.1 us -> 14.4 us
    dot_general x21 -> x0, matrix products: 54.3 us -> none  [the longest x3 16.3 us: orthogonal(): applied = jnp.dot(poly, part, preferred_element_type=f32)]
    pallas_call x0 -> x5, Pallas kernels: none -> 24.6 us  [the longest x1 6.97 us: shared_step(): call(body, shape(width, width), [SMEM, VMEM, VMEM, ANY], [pltpu.VMEM((wid...]
    all_to_all x3 -> x4, blocking collectives: 61.3 us -> 82.1 us  [exchange(): return lax.all_to_all(blocks, 'tok', 0, 0, axis_index_groups=groups)]
    all_to_all x1 -> x0, waiting for transfers between devices: 18.1 us -> none  [exchange(): return lax.all_to_all(blocks, 'tok', 0, 0, axis_index_groups=groups)]
    ppermute x3, waiting for transfers between devices: 11.8 us -> 16.1 us  [on_device(): lax.ppermute(part, 'head', [(i, (i + step) % heads) for i in range(heads)])]
    ppermute x4, waiting for transfers between devices: 2.2 us -> 6.11 us  [swap_cores(): return lax.ppermute(array, 'tok', CORE_SWAP)]
    all_to_all x1 -> x0, starting transfers between devices: 3.58 us -> none  [exchange(): return lax.all_to_all(blocks, 'tok', 0, 0, axis_index_groups=groups)]
    reduce_sum x2 -> x0, other arithmetic: 2.41 us -> none  [orthogonal(): jnp.sum(part.astype(f32) * part.astype(f32))]
  transfers between devices with their start and end apart: 8 -> 7, of which waited for: 4 -> 4; matrix products, arithmetic and copies ran while one was open for 16% -> 0% of each run, Pallas kernels for 0% -> 5%
where the time goes in v2:
time: 151 us; the launch traced here: 150 us
  blocking collectives  82.1 us (54%)
  Pallas kernels  24.6 us (16%)
  waiting for transfers between devices  22.3 us (15%)
  starting transfers between devices  14.4 us (10%)
  local copies, waits for them, and re-layouts  5.41 us (4%)
    all_to_all x4, blocking collectives, exchange(): return lax.all_to_all(blocks, 'tok', 0, 0, axis_index_groups=groups)  82.1 us
    ppermute x3, waiting for transfers between devices, on_device(): lax.ppermute(part, 'head', [(i, (i + step) % heads) for i in range(heads)])  16.1 us
    ppermute x4, starting transfers between devices, swap_cores(): return lax.ppermute(array, 'tok', CORE_SWAP)  9.46 us
    pallas_call x1, Pallas kernels, shared_step(): call(body, shape(width, width), [SMEM, VMEM, VMEM, ANY], [pltpu.VMEM((wid...  6.97 us
    pallas_call x1, Pallas kernels, own_step(): call(body, shape(width, width), [SMEM, VMEM, ANY], [pltpu.VMEM((width, wi...  6.88 us
    ppermute x4, waiting for transfers between devices, swap_cores(): return lax.ppermute(array, 'tok', CORE_SWAP)  6.11 us
    unnamed x15, local copies, waits for them, and re-layouts  5.11 us
    pallas_call x1, Pallas kernels, gradients(): call(body, [shape(width, width), shape(width, half), shape(width, width,...  5.04 us
  transfers between devices with their start and end apart: 7, of which 4 were waited for; matrix products, arithmetic and copies ran while one was open for 0% of the time, Pallas kernels for 5%

profile of v2, /device:TPU:1, one launch (start us, length us, event | category | flops | bytes accessed | tf_op | source)
XLA Modules:
  0.0 150.2 jit_solution(18085402689191566210)
XLA Ops:
  0.0 0.8 copy.8.r_ref
  0.9 2.0 %copy-done.1 = bf16[1,3,768,768]{3,2,1,0:T(8,128)(2,1)S(1)} copy-done((bf16[1,3,768,768]{3,2,1,0:T(8,128)(2,1)S(1)}, bf16[1,3,768,768]{3,2,1,0:T(8,128)(2,1)}, u32[]{:S(2)}) %copy-start.1) | copy-done | bytes 3538968
  2.9 1.1 copy-done.3
  4.0 1.1 copy-done.4
  5.2 5.0 %gradients.1 = (bf16[768,768]{1,0:T(8,128)(2,1)S(1)}, bf16[768,384]{1,0:T(8,128)(2,1)S(1)}, f32[768,768]{1,0:T(8,128)S(1)}, f32[768,384]{1,0:T(8,128)S(1)}) custom-call(s32[2]{0:T(128)S(1)} %pad_add_fusion.core_ref.place_ref, bf16[512,768]{1,0:T(8,128)(2,1)S(1)} %copy-done.3, bf16[512,768]{1,0:T(8,128)(2,1)S(1)} %copy-done.4, f32[512,1]{1,0:T(8,128)S(1)} %copy.8.r_ref, ...), custom_call_target="tpu_custom_call" | custom-call | flops 3623878656 | bytes 7077888 | tf_op jit(solution)/shard_map/gradients/pallas_call | solution.py:116
  10.2 3.3 %collective-permute-start = (bf16[768,768]{1,0:T(8,128)(2,1)S(1)}, bf16[768,768]{1,0:T(8,128)(2,1)S(1)}, u32[]{:S(2)}, u32[]{:S(2)}) collective-permute-start(bf16[768,768]{1,0:T(8,128)(2,1)S(1)} %get-tuple-element.14), channel_id=1, source_target_pairs={{0,4},{4,0},{8,12},{12,8},{16,20},{20,16},{24,28},{28,24},{32,36},... | collective-permute-start | bytes 3538952 | tf_op jit(solution)/shard_map/ppermute | solution.py:42
  13.7 3.2 %collective-permute-done.1 = bf16[768,384]{1,0:T(8,128)(2,1)S(1)} collective-permute-done((bf16[768,384]{1,0:T(8,128)(2,1)S(1)}, bf16[768,384]{1,0:T(8,128)(2,1)S(1)}, u32[]{:S(2)}, u32[]{:S(2)}) %collective-permute-start.1) | collective-permute-done | bytes 589856 | tf_op jit(solution)/shard_map/ppermute | solution.py:42
  17.5 24.6 %all_to_all.20 = bf16[4,192,1152]{2,1,0:T(8,128)(2,1)S(1)} all-to-all(bf16[4,192,1152]{2,1,0:T(8,128)(2,1)S(1)} %pad_maximum_fusion), channel_id=1, replica_groups={{0,64,128,192},{4,68,132,196},{8,72,136,200},{12,76,140,204},{16,80,144..., dimensions={0} | all-to-all | bytes 3538944 | tf_op jit(solution)/shard_map/all_to_all | solution.py:46
  42.1 0.5 reduce_sum.24
  42.6 21.4 %all_to_all.21 = bf16[8,24,1152]{2,1,0:T(8,128)(2,1)S(1)} all-to-all(bf16[8,24,1152]{2,1,0:T(8,128)(2,1)S(1)} %bitcast.13), channel_id=1, replica_groups={{0,8,16,24,32,40,48,56},{4,12,20,28,36,44,52,60},{64,72,80,88,96,104,11..., dimensions={0} | all-to-all | bytes 884736 | tf_op jit(solution)/shard_map/all_to_all | solution.py:46
  64.1 15.3 %all_to_all.22 = bf16[8,24,1152]{2,1,0:T(8,128)(2,1)S(1)} all-to-all(bf16[8,24,1152]{2,1,0:T(8,128)(2,1)S(1)} %broadcast_in_dim.6), channel_id=1, replica_groups={{0,8,16,24,32,40,48,56},{4,12,20,28,36,44,52,60},{64,72,80,88,96,104,11..., dimensions={0} | all-to-all | bytes 884736 | tf_op jit(solution)/shard_map/all_to_all | solution.py:46
  79.5 20.9 %all_to_all.23 = bf16[4,192,1152]{2,1,0:T(8,128)(2,1)S(1)} all-to-all(bf16[4,192,1152]{2,1,0:T(8,128)(2,1)S(1)} %broadcast_in_dim.15), channel_id=1, replica_groups={{0,64,128,192},{4,68,132,196},{8,72,136,200},{12,76,140,204},{16,80,144..., dimensions={0} | all-to-all | bytes 3538944 | tf_op jit(solution)/shard_map/all_to_all | solution.py:46
  100.5 6.9 %own_step.1.own_ref = bf16[768,768]{1,0:T(8,128)(2,1)S(1)} custom-call(s32[2]{0:T(128)S(1)} %pad_add_fusion.core_ref.place_ref, bf16[768,768]{1,0:T(8,128)(2,1)S(1)} %slice.8.x_ref, bf16[1,3,768,768]{3,2,1,0:T(8,128)(2,1)S(1)} %copy-done.2), custom_call_target="tpu_custom_call" | custom-call | flops 5435817984 | bytes 3538944 | tf_op jit(solution)/shard_map/own_step/pallas_call | solution.py:173
  107.4 5.7 %collective-permute-start.2 = (bf16[768,768]{1,0:T(8,128)(2,1)S(1)}, bf16[768,768]{1,0:T(8,128)(2,1)S(1)}, u32[]{:S(2)}, u32[]{:S(2)}) collective-permute-start(bf16[768,768]{1,0:T(8,128)(2,1)S(1)} %own_step.1.own_ref), channel_id=1, source_target_pairs={{0,4},{4,0},{8,12},{12,8},{16,20},{20,16},{24,28},{28,24},{32,36},... | collective-permute-start | bytes 3538952 | tf_op jit(solution)/shard_map/ppermute | solution.py:42
  113.2 0.3 collective-permute-start.3
  113.5 2.9 %collective-permute-done.3.b_ref = bf16[768,384]{1,0:T(8,128)(2,1)S(1)} collective-permute-done((bf16[768,384]{1,0:T(8,128)(2,1)S(1)}, bf16[768,384]{1,0:T(8,128)(2,1)S(1)}, u32[]{:S(2)}, u32[]{:S(2)}) %collective-permute-start.3) | collective-permute-done | bytes 589856 | tf_op jit(solution)/shard_map/ppermute | solution.py:42
  116.4 7.0 %shared_step.1.shared_ref = bf16[768,768]{1,0:T(8,128)(2,1)S(1)} custom-call(s32[2]{0:T(128)S(1)} %pad_add_fusion.core_ref.place_ref, bf16[768,384]{1,0:T(8,128)(2,1)S(1)} %slice.9.a_ref, bf16[768,384]{1,0:T(8,128)(2,1)S(1)} %collective-permute-done.3.b_ref, bf16[1,3,768,768]{3,2,1,0:T(8,128)(2,1)S(1)} %copy-done.2), custom_call_target="tpu_custom_call" | custom-call | flops 5435817984 | bytes 3538944 | tf_op jit(solution)/shard_map/shared_step/pallas_call | solution.py:198
  123.4 4.7 %project.1 = (f32[256,768]{1,0:T(8,128)S(1)}, bf16[256,768]{1,0:T(8,128)(2,1)S(1)}, bf16[256,768]{1,0:T(8,128)(2,1)S(1)}, bf16[256,768]{1,0:T(8,128)(2,1)S(1)}) custom-call(s32[2]{0:T(128)S(1)} %pad_add_fusion.core_ref.place_ref, bf16[256,768]{1,0:T(8,128)(2,1)S(1)} %copy-done, bf16[768,768]{1,0:T(8,128)(2,1)S(1)} %own_step.1.own_ref, ...), custom_call_target="tpu_custom_call" | custom-call | flops 2113929216 | bytes 9437184 | tf_op jit(solution)/shard_map/project/pallas_call | solution.py:238
  128.1 1.3 collective-permute-start.4
  129.4 2.5 %collective-permute-start.5 = (bf16[256,768]{1,0:T(8,128)(2,1)S(1)}, bf16[256,768]{1,0:T(8,128)(2,1)S(1)}, u32[]{:S(2)}, u32[]{:S(2)}) collective-permute-start(bf16[256,768]{1,0:T(8,128)(2,1)S(1)} %get-tuple-element.19), channel_id=1, source_target_pairs={{0,2},{1,3},{2,0},{3,1},{4,6},{5,7},{6,4},{7,5},{8,10},{9,11},{10,... | collective-permute-start | bytes 1179656 | tf_op jit(solution)/shard_map/ppermute | solution.py:292
  131.9 1.1 collective-permute-start.6
  133.0 6.7 %collective-permute-done.4.refs_1_ = bf16[256,768]{1,0:T(8,128)(2,1)S(1)} collective-permute-done((bf16[256,768]{1,0:T(8,128)(2,1)S(1)}, bf16[256,768]{1,0:T(8,128)(2,1)S(1)}, u32[]{:S(2)}, u32[]{:S(2)}) %collective-permute-start.4) | collective-permute-done | bytes 393248 | tf_op jit(solution)/shard_map/ppermute | solution.py:292
  139.8 9.4 %collective-permute-done.5.refs_2_ = bf16[256,768]{1,0:T(8,128)(2,1)S(1)} collective-permute-done((bf16[256,768]{1,0:T(8,128)(2,1)S(1)}, bf16[256,768]{1,0:T(8,128)(2,1)S(1)}, u32[]{:S(2)}, u32[]{:S(2)}) %collective-permute-start.5) | collective-permute-done | bytes 393248 | tf_op jit(solution)/shard_map/ppermute | solution.py:292
  149.2 1.0 mix.1
  (25 shorter events, 1.2 us)
Async XLA Ops:
  0.9 2.0 %copy-start.1 = (bf16[1,3,768,768]{3,2,1,0:T(8,128)(2,1)S(1)}, bf16[1,3,768,768]{3,2,1,0:T(8,128)(2,1)}, u32[]{:S(2)}) copy-start(bf16[1,3,768,768]{3,2,1,0:T(8,128)(2,1)} %w_hbm.3) | copy-start | bytes 10616836
  2.9 1.1 copy-start.3
  4.0 1.1 copy-start.4
  10.2 6.8 %collective-permute-start = (bf16[768,768]{1,0:T(8,128)(2,1)S(1)}, bf16[768,768]{1,0:T(8,128)(2,1)S(1)}, u32[]{:S(2)}, u32[]{:S(2)}) collective-permute-start(bf16[768,768]{1,0:T(8,128)(2,1)S(1)} %get-tuple-element.14), channel_id=1, source_target_pairs={{0,4},{4,0},{8,12},{12,8},{16,20},{20,16},{24,28},{28,24},{32,36},... | collective-permute-start | bytes 3538952 | tf_op jit(solution)/shard_map/ppermute | solution.py:42
  13.6 3.3 %collective-permute-start.1 = (bf16[768,384]{1,0:T(8,128)(2,1)S(1)}, bf16[768,384]{1,0:T(8,128)(2,1)S(1)}, u32[]{:S(2)}, u32[]{:S(2)}) collective-permute-start(bf16[768,384]{1,0:T(8,128)(2,1)S(1)} %get-tuple-element.16), channel_id=1, source_target_pairs={{0,4},{4,0},{8,12},{12,8},{16,20},{20,16},{24,28},{28,24},{32,36},... | collective-permute-start | bytes 1769480 | tf_op jit(solution)/shard_map/ppermute | solution.py:42
  79.5 21.0 %copy-start.2 = (bf16[1,3,768,768]{3,2,1,0:T(8,128)(2,1)S(1)}, bf16[1,3,768,768]{3,2,1,0:T(8,128)(2,1)}, u32[]{:S(2)}) copy-start(bf16[1,3,768,768]{3,2,1,0:T(8,128)(2,1)} %w_hbm.3) | copy-start | bytes 10616836
  107.4 16.0 %collective-permute-start.2 = (bf16[768,768]{1,0:T(8,128)(2,1)S(1)}, bf16[768,768]{1,0:T(8,128)(2,1)S(1)}, u32[]{:S(2)}, u32[]{:S(2)}) collective-permute-start(bf16[768,768]{1,0:T(8,128)(2,1)S(1)} %own_step.1.own_ref), channel_id=1, source_target_pairs={{0,4},{4,0},{8,12},{12,8},{16,20},{20,16},{24,28},{28,24},{32,36},... | collective-permute-start | bytes 3538952 | tf_op jit(solution)/shard_map/ppermute | solution.py:42
  113.1 10.3 %slice-start = ((s8[4718592]{0:T(1024)(128)(4,1)}), s8[4194304]{0:T(1024)(128)(4,1)S(1)}, s32[]{:S(2)}) async-start(s8[4718592]{0:T(1024)(128)(4,1)} %bitcast.7), calls=%async_computation.4 | async-start | bytes 8388608
  113.1 10.3 %slice-start.1 = ((s8[4718592]{0:T(1024)(128)(4,1)}), s8[524288]{0:T(1024)(128)(4,1)S(1)}, s32[]{:S(2)}) async-start(s8[4718592]{0:T(1024)(128)(4,1)} %bitcast.7), calls=%async_computation.5 | async-start | bytes 1048576
  113.1 10.2 %copy-start = (bf16[256,768]{1,0:T(8,128)(2,1)S(1)}, bf16[256,768]{1,0:T(8,128)(2,1)}, u32[]{:S(2)}) copy-start(bf16[256,768]{1,0:T(8,128)(2,1)} %q_ref.1) | copy-start | bytes 1179652
  113.2 3.2 %collective-permute-start.3 = (bf16[768,384]{1,0:T(8,128)(2,1)S(1)}, bf16[768,384]{1,0:T(8,128)(2,1)S(1)}, u32[]{:S(2)}, u32[]{:S(2)}) collective-permute-start(bf16[768,384]{1,0:T(8,128)(2,1)S(1)} %slice.9.a_ref), channel_id=1, source_target_pairs={{0,4},{4,0},{8,12},{12,8},{16,20},{20,16},{24,28},{28,24},{32,36},... | collective-permute-start | bytes 1769480 | tf_op jit(solution)/shard_map/ppermute | solution.py:42
  128.1 11.6 %collective-permute-start.4 = (bf16[256,768]{1,0:T(8,128)(2,1)S(1)}, bf16[256,768]{1,0:T(8,128)(2,1)S(1)}, u32[]{:S(2)}, u32[]{:S(2)}) collective-permute-start(bf16[256,768]{1,0:T(8,128)(2,1)S(1)} %get-tuple-element.18), channel_id=1, source_target_pairs={{0,1},{1,2},{2,3},{3,0},{4,5},{5,6},{6,7},{7,4},{8,9},{9,10},{10,1... | collective-permute-start | bytes 1179656 | tf_op jit(solution)/shard_map/ppermute | solution.py:292
  129.4 19.7 %collective-permute-start.5 = (bf16[256,768]{1,0:T(8,128)(2,1)S(1)}, bf16[256,768]{1,0:T(8,128)(2,1)S(1)}, u32[]{:S(2)}, u32[]{:S(2)}) collective-permute-start(bf16[256,768]{1,0:T(8,128)(2,1)S(1)} %get-tuple-element.19), channel_id=1, source_target_pairs={{0,2},{1,3},{2,0},{3,1},{4,6},{5,7},{6,4},{7,5},{8,10},{9,11},{10,... | collective-permute-start | bytes 1179656 | tf_op jit(solution)/shard_map/ppermute | solution.py:292
  131.9 17.3 %collective-permute-start.6 = (bf16[256,768]{1,0:T(8,128)(2,1)S(1)}, bf16[256,768]{1,0:T(8,128)(2,1)S(1)}, u32[]{:S(2)}, u32[]{:S(2)}) collective-permute-start(bf16[256,768]{1,0:T(8,128)(2,1)S(1)} %get-tuple-element.20), channel_id=1, source_target_pairs={{0,3},{1,0},{2,1},{3,2},{4,7},{5,4},{6,5},{7,6},{8,11},{9,8},{10,9... | collective-permute-start | bytes 1179656 | tf_op jit(solution)/shard_map/ppermute | solution.py:292

commit v3 on v2

--- a/solution.py
+++ b/solution.py
@@ -25,12 +25,11 @@
     return (y * NZ + z) * NC + core
 
 
-Y_GROUPS = [
-    [chip_index(y, z, core) for y in range(NY)] for z in range(NZ) for core in range(NC)
-]
 Z_GROUPS = [
     [chip_index(y, z, core) for z in range(NZ)] for y in range(NY) for core in range(NC)
 ]
+Y_UP = [(d, (d + NZ * NC) % (NY * NZ * NC)) for d in range(NY * NZ * NC)]
+Y_DOWN = [(there, here) for here, there in Y_UP]
 CORE_SWAP = [(device, device ^ 1) for device in range(NY * NZ * NC)]
 
 SMEM = pl.BlockSpec(memory_space=pltpu.SMEM)
@@ -84,24 +83,48 @@
     return jax.ShapeDtypeStruct(dims, dtype)
 
 
-def gradients(core, keys, values, rates, weights):
+def gradients(place, keys, values, rates, weights):
     tokens, width = keys.shape
     half = width // 2
-
-    def body(core_ref, k_ref, v_ref, r_ref, w_ref, own_send, shared_send, own_keep, shared_keep,
-             hidden, errors, g_keep, g_send):
-        first = core_ref[0] == 0
+    lanes = rates.shape[1]
+
+    def body(place_ref, r_ref, k_hbm, v_hbm, w_hbm, own_send, shared_send, own_keep, shared_keep,
+             k_ref, v_ref, w_ref, hidden, errors, g_keep, g_send, sems):
+        moves = [
+            (k_hbm, k_ref),
+            (w_hbm.at[0, 0], w_ref.at[0]),
+            (w_hbm.at[0, 1], w_ref.at[1]),
+            (v_hbm, v_ref),
+            (w_hbm.at[0, 2], w_ref.at[2]),
+        ]
+        copies = [
+            pltpu.make_async_copy(src, dst, sems.at[n]) for n, (src, dst) in enumerate(moves)
+        ]
+        for copy in copies:
+            copy.start()
+        first = place_ref[0] == 0
+        rate_columns = r_ref[...].T
+        copies[0].wait()
+        copies[1].wait()
         for row in range(0, tokens, ROWS):
             rows = slice(row, row + ROWS)
             k = k_ref[rows, :]
-            h1 = dot(k, w_ref[0, 0])
-            h3 = dot(k, w_ref[0, 1])
+            h1 = dot(k, w_ref[0])
+            if row == 0:
+                copies[2].wait()
+            h3 = dot(k, w_ref[1])
             sig = jax.nn.sigmoid(h1)
             act = h1 * sig
             hidden[rows, :] = (act * h3).astype(bf16)
-            e = (-r_ref[rows, :] * v_ref[rows, :].astype(f32)).astype(bf16)
-            errors[rows, :] = e
-            dz = dot_nt(e, w_ref[0, 2])
+            if row == 0:
+                copies[3].wait()
+            for part in range(row, row + ROWS, lanes):
+                rate = rate_columns[:, part // lanes : part // lanes + 1]
+                span = slice(part, part + lanes)
+                errors[span, :] = (-rate * v_ref[span, :].astype(f32)).astype(bf16)
+            if row == 0:
+                copies[4].wait()
+            dz = dot_nt(errors[rows, :], w_ref[2])
             g1 = (dz * h3 * (sig * (1.0 + h1 * (1.0 - sig)))).astype(bf16)
             g3 = (dz * act).astype(bf16)
             g_keep[rows, :] = jnp.where(first, g1, g3)
@@ -121,13 +144,79 @@
             shape(width, width, dtype=f32),
             shape(width, half, dtype=f32),
         ],
-        [SMEM] + [VMEM] * 4,
-        [pltpu.VMEM((tokens, width), bf16)] * 4,
-        32,
+        [SMEM, VMEM] + [ANY] * 3,
+        [pltpu.VMEM((tokens, width), bf16)] * 2
+        + [pltpu.VMEM((3, width, width), bf16)]
+        + [pltpu.VMEM((tokens, width), bf16)] * 4
+        + [pltpu.SemaphoreType.DMA((5,))],
+        40,
         12 * tokens * width * width,
         12 * width * width,
         "gradients",
-    )(core, keys, values, rates, weights)
+    )(place, rates, keys, values, weights)
+
+
+def chip_sum(place, own_keep, own_got, shared_keep, shared_got):
+    width, half = shared_keep.shape
+    rows = width // NY
+    wide = width + half
+
+    def body(place_ref, ok_ref, og_ref, sk_ref, sg_ref, mine, *outs):
+        for step in range(NY):
+            start = lax.rem(place_ref[2] + step, NY) * rows
+            for part in range(2):
+                cut = rows // 2
+                span = pl.ds(pl.multiple_of(start + part * cut, cut), cut)
+                own = ok_ref[span, :] + og_ref[span, :].astype(f32)
+                shared = sk_ref[span, :] + sg_ref[span, :].astype(f32)
+                if step == 0:
+                    mine[part * cut : (part + 1) * cut, :width] = own
+                    mine[part * cut : (part + 1) * cut, width:] = shared
+                else:
+                    out = outs[2 * (step - 1) + part]
+                    out[:, :width] = own.astype(bf16)
+                    out[:, width:] = shared.astype(bf16)
+
+    return call(
+        body,
+        [shape(rows, wide, dtype=f32)] + [shape(rows // 2, wide)] * (2 * NY - 2),
+        [SMEM] + [VMEM] * 4,
+        [],
+        16,
+        0,
+        10 * width * wide,
+        "chip_sum",
+    )(place, own_keep, own_got, shared_keep, shared_got)
+
+
+def assemble(place, own, previous, following, opposite):
+    rows, wide = own.shape
+    width = rows * NY
+    pieces = [own, *following, *opposite, *previous]
+
+    def body(place_ref, own_ref, *rest):
+        parts, (x_ref, s_ref) = rest[:-2], rest[-2:]
+        base = place_ref[2]
+        start = pl.multiple_of(base * rows, rows)
+        x_ref[pl.ds(start, rows), :] = own_ref[:, :width]
+        s_ref[pl.ds(start, rows), :] = own_ref[:, width:]
+        for n, part in enumerate(parts):
+            cut = rows // 2
+            start = lax.rem(base + 1 + n // 2, NY) * rows + (n % 2) * cut
+            span = pl.ds(pl.multiple_of(start, cut), cut)
+            x_ref[span, :] = part[:, :width]
+            s_ref[span, :] = part[:, width:]
+
+    return call(
+        body,
+        [shape(width, width), shape(width, wide - width)],
+        [SMEM] + [VMEM] * len(pieces),
+        [],
+        16,
+        0,
+        4 * width * wide,
+        "assemble",
+    )(place, *pieces)
 
 
 def newton_schulz(x_ref, w_ref, out_ref, gram, poly, other):
@@ -212,7 +301,7 @@
     heads = out_proj.shape[1] // width
 
     def body(place_ref, q_ref, own_ref, other_ref, shared_ref, p_hbm, *rest):
-        outs, p_ref, sems = rest[:heads], rest[heads], rest[heads + 1]
+        outs, p_ref, sems = rest[:-2], rest[-2], rest[-1]
         copies = []
         for step in range(heads):
             head = lax.rem(place_ref[1] + step, heads)
@@ -231,13 +320,19 @@
         q3 = jnp.where(first, q_other, q_own)
         gated = (q1 * jax.nn.sigmoid(q1) * q3).astype(bf16)
         outputs = dot(gated, shared_ref[...]).astype(bf16)
+        cut = tokens // 2
         for step in range(heads):
             copies[step].wait()
-            outs[step][...] = dot(outputs, p_ref[step]).astype(outs[step].dtype)
-
-    return call(
-        body,
-        [shape(tokens, width, dtype=f32)] + [shape(tokens, width)] * (heads - 1),
+            product = dot(outputs, p_ref[step])
+            if step == 0:
+                outs[0][...] = product
+            else:
+                outs[2 * step - 1][...] = product[:cut].astype(bf16)
+                outs[2 * step][...] = product[cut:].astype(bf16)
+
+    return call(
+        body,
+        [shape(tokens, width, dtype=f32)] + [shape(tokens // 2, width)] * (2 * heads - 2),
         [SMEM] + [VMEM] * 4 + [ANY],
         [pltpu.VMEM((heads, width, width), bf16), pltpu.SemaphoreType.DMA((heads,))],
         24,
@@ -247,52 +342,96 @@
     )(place, queries, own, other, shared, out_proj)
 
 
-def mix(own, *got):
+def mix(own, top, bottom):
     tokens, width = own.shape
-
-    def body(*refs):
-        total = refs[0][...]
-        for ref in refs[1:-1]:
-            total = total + ref[...].astype(f32)
-        refs[-1][...] = total.T.astype(bf16)
-
-    return call(
-        body, shape(width, tokens), [VMEM] * (1 + len(got)), [], 16, 0, 12 * tokens * width, "mix"
-    )(own, *got)
+    cut = tokens // 2
+    count = len(top)
+
+    def body(own_ref, *rest):
+        out = rest[-1]
+        for part in range(2):
+            total = own_ref[part * cut : (part + 1) * cut, :]
+            for ref in rest[part * count : (part + 1) * count]:
+                total = total + ref[...].astype(f32)
+            out[:, part * cut : (part + 1) * cut] = total.T.astype(bf16)
+
+    return call(
+        body,
+        shape(width, tokens),
+        [VMEM] * (1 + 2 * count),
+        [],
+        16,
+        0,
+        12 * tokens * width,
+        "mix",
+    )(own, *top, *bottom)
+
+
+def shift(array, axis, pairs):
+    return lax.ppermute(array, axis, pairs)
+
+
+def add(left, right):
+    return (left.astype(f32) + right.astype(f32)).astype(bf16)
+
+
+def ring_sum(pieces, axis, up, down):
+    next_a, next_b, far_a, far_b, previous_a, previous_b = pieces
+    relay_a = shift(far_a, axis, up)
+    relay_b = shift(far_b, axis, down)
+    from_down_b = shift(next_b, axis, up)
+    from_up_a = shift(previous_a, axis, down)
+    from_down_a = shift(add(next_a, relay_a), axis, up)
+    from_up_b = shift(add(previous_b, relay_b), axis, down)
+    return [from_down_a, from_up_a], [from_down_b, from_up_b]
+
+
+def ring_gather(block, axis, up, down):
+    cut = block.shape[0] // 2
+    block_a, block_b = block[:cut], block[cut:]
+    previous_a = shift(block_a, axis, up)
+    following_b = shift(block_b, axis, down)
+    previous_b = shift(block_b, axis, up)
+    following_a = shift(block_a, axis, down)
+    far_a = shift(previous_a, axis, up)
+    far_b = shift(following_b, axis, down)
+    return (previous_a, previous_b), (following_a, following_b), (far_a, far_b)
 
 
 def on_device(keys, values, rates, fast_weights, queries, out_proj):
     width = fast_weights.shape[-1]
-    core = lax.axis_index("tok") % NC
+    place_in_tok = lax.axis_index("tok")
+    core = place_in_tok % NC
     head = lax.axis_index("head")
     heads = lax.axis_size("head")
-    place = jnp.stack([core, head]).astype(jnp.int32)
+    place = jnp.stack([core, head, place_in_tok // (NC * NZ)]).astype(jnp.int32)
 
     own_send, shared_send, own_keep, shared_keep = gradients(
-        place, keys, values, rates, fast_weights
+        place, keys, values, rates.reshape(-1, 128), fast_weights
     )
+    own_got = swap_cores(own_send)
     shared_got = swap_cores(shared_send)
-    own_got = swap_cores(own_send)
-    chip_sum = jnp.concatenate(
-        [own_keep + own_got.astype(f32), shared_keep + shared_got.astype(f32)], axis=1
-    ).astype(bf16)
-
-    y_sum = sum_shares(chip_sum.reshape(NY, width // NY, -1), Y_GROUPS)
+    mine, *shares = chip_sum(place, own_keep, own_got, shared_keep, shared_got)
+
+    got_a, got_b = ring_sum(shares, "tok", Y_UP, Y_DOWN)
+    cut = mine.shape[0] // 2
+    first_half = mine[:cut] + got_a[0].astype(f32) + got_a[1].astype(f32)
+    second_half = mine[cut:] + got_b[0].astype(f32) + got_b[1].astype(f32)
+    y_sum = jnp.concatenate([first_half, second_half]).astype(bf16)
     z_sum = sum_shares(y_sum.reshape(NZ, width // NY // NZ, -1), Z_GROUPS)
-    summed = gather_rows(gather_rows(z_sum, Z_GROUPS), Y_GROUPS)
-
-    shared_part = summed[:, width:]
+    y_rows = gather_rows(z_sum, Z_GROUPS)
+    previous, following, far = ring_gather(y_rows, "tok", Y_UP, Y_DOWN)
+    own_sum, shared_part = assemble(place, y_rows, previous, following, far)
+
     shared_other = swap_cores(shared_part)
-    own_fresh = own_step(place, summed[:, :width], fast_weights)
+    own_fresh = own_step(place, own_sum, fast_weights)
     other_fresh = swap_cores(own_fresh)
     shared_fresh = shared_step(place, shared_part, shared_other, fast_weights)
 
-    mixed, *parts = project(place, queries, own_fresh, other_fresh, shared_fresh, out_proj)
-    got = [
-        lax.ppermute(part, "head", [(i, (i + step) % heads) for i in range(heads)])
-        for step, part in enumerate(parts, 1)
-    ]
-    return mix(mixed, *got)
+    mixed, *shares = project(place, queries, own_fresh, other_fresh, shared_fresh, out_proj)
+    up = [(i, (i + 1) % heads) for i in range(heads)]
+    down = [(i, (i - 1) % heads) for i in range(heads)]
+    return mix(mixed, *ring_sum(shares, "head", up, down))
 
 
 def solution(mesh):

time: 151 us -> 137 us (0.907)
  blocking collectives: 82.1 us -> 34.8 us
  starting transfers between devices: 14.4 us -> 34.1 us
  waiting for transfers between devices: 22.3 us -> 32.6 us
  Pallas kernels: 24.6 us -> 27.7 us
    all_to_all x4 -> x2, blocking collectives: 82.1 us -> 34.8 us  [exchange(): return lax.all_to_all(blocks, 'tok', 0, 0, axis_index_groups=groups)]
    ppermute x3 -> x18, starting transfers between devices: 4.89 us -> 25.4 us  [shift(): return lax.ppermute(array, axis, pairs)]
    ppermute x3 -> x18, waiting for transfers between devices: 16.1 us -> 26.4 us  [shift(): return lax.ppermute(array, axis, pairs)]
    pallas_call x2 -> x4, Pallas kernels: 5.74 us -> 7.32 us  [the longest x1 4.74 us: project(): call(body, [shape(tokens, width, dtype=f32)] + [shape(tokens // 2, width)...]
    unnamed x15 -> x16, local copies, waits for them, and re-layouts: 5.11 us -> 4.97 us
  transfers between devices with their start and end apart: 7 -> 22, of which waited for: 4 -> 13; matrix products, arithmetic and copies ran while one was open for 0% -> 0% of each run, Pallas kernels for 5% -> 5%
where the time goes in v3:
time: 137 us; the launch traced here: 135 us
  blocking collectives  34.8 us (25%)
  starting transfers between devices  34.1 us (25%)
  waiting for transfers between devices  32.6 us (24%)
  Pallas kernels  27.7 us (20%)
  local copies, waits for them, and re-layouts  5.03 us (4%)
    all_to_all x2, blocking collectives, exchange(): return lax.all_to_all(blocks, 'tok', 0, 0, axis_index_groups=groups)  34.8 us
    ppermute x18, waiting for transfers between devices, shift(): return lax.ppermute(array, axis, pairs)  26.4 us
    ppermute x18, starting transfers between devices, shift(): return lax.ppermute(array, axis, pairs)  25.4 us
    ppermute x4, starting transfers between devices, swap_cores(): return lax.ppermute(array, 'tok', CORE_SWAP)  8.7 us
    pallas_call x1, Pallas kernels, shared_step(): call(body, shape(width, width), [SMEM, VMEM, VMEM, ANY], [pltpu.VMEM((wid...  6.97 us
    pallas_call x1, Pallas kernels, own_step(): call(body, shape(width, width), [SMEM, VMEM, ANY], [pltpu.VMEM((width, wi...  6.88 us
    pallas_call x1, Pallas kernels, gradients(): call(body, [shape(width, width), shape(width, half), shape(width, width,...  6.5 us
    ppermute x4, waiting for transfers between devices, swap_cores(): return lax.ppermute(array, 'tok', CORE_SWAP)  6.18 us
  transfers between devices with their start and end apart: 22, of which 13 were waited for; matrix products, arithmetic and copies ran while one was open for 0% of the time, Pallas kernels for 5%

profile of v3, /device:TPU:1, one launch (start us, length us, event | category | flops | bytes accessed | tf_op | source)
XLA Modules:
  0.0 135.0 jit_solution(18128577526868038801)
XLA Ops:
  0.1 2.0 %copy-done.1 = bf16[1,3,768,768]{3,2,1,0:T(8,128)(2,1)S(1)} copy-done((bf16[1,3,768,768]{3,2,1,0:T(8,128)(2,1)S(1)}, bf16[1,3,768,768]{3,2,1,0:T(8,128)(2,1)}, u32[]{:S(2)}) %copy-start.1) | copy-done | bytes 3538968
  5.0 6.5 %gradients.1 = (bf16[768,768]{1,0:T(8,128)(2,1)S(1)}, bf16[768,384]{1,0:T(8,128)(2,1)S(1)}, f32[768,768]{1,0:T(8,128)S(1)}, f32[768,384]{1,0:T(8,128)S(1)}) custom-call(s32[3]{0:T(128)S(1)} %pad_add_fusion.place_ref.core_ref, f32[4,128]{1,0:T(4,128)S(1)} %bitcast.11, bf16[512,768]{1,0:T(8,128)(2,1)S(1)} %copy-done.3, bf16[512,768]{1,0:T(8,128)(2,1)S(1)} %copy-done.4, ...), custom_call_target="tpu_custom_call" | custom-call | flops 3623878656 | bytes 7077888 | tf_op jit(solution)/shard_map/gradients/pallas_call | solution.py:139
  11.5 3.3 %collective-permute-start = (bf16[768,768]{1,0:T(8,128)(2,1)S(1)}, bf16[768,768]{1,0:T(8,128)(2,1)S(1)}, u32[]{:S(2)}, u32[]{:S(2)}) collective-permute-start(bf16[768,768]{1,0:T(8,128)(2,1)S(1)} %get-tuple-element.26), channel_id=1, source_target_pairs={{0,4},{4,0},{8,12},{12,8},{16,20},{20,16},{24,28},{28,24},{32,36},... | collective-permute-start | bytes 3538952 | tf_op jit(solution)/shard_map/ppermute | solution.py:41
  15.0 3.2 %collective-permute-done.1.sg_ref = bf16[768,384]{1,0:T(8,128)(2,1)S(1)} collective-permute-done((bf16[768,384]{1,0:T(8,128)(2,1)S(1)}, bf16[768,384]{1,0:T(8,128)(2,1)S(1)}, u32[]{:S(2)}, u32[]{:S(2)}) %collective-permute-start.1) | collective-permute-done | bytes 589856 | tf_op jit(solution)/shard_map/ppermute | solution.py:41
  19.2 2.7 %collective-permute-start.4 = (bf16[96,1152]{1,0:T(8,128)(2,1)S(1)}, bf16[96,1152]{1,0:T(8,128)(2,1)S(1)}, u32[]{:S(2)}, u32[]{:S(2)}) collective-permute-start(bf16[96,1152]{1,0:T(8,128)(2,1)S(1)} %get-tuple-element.32), channel_id=1, source_target_pairs={{64,0},{68,4},{72,8},{76,12},{80,16},{84,20},{88,24},{92,28},{96,3... | collective-permute-start | bytes 663560 | tf_op jit(solution)/shard_map/ppermute | solution.py:371
  21.9 2.7 %collective-permute-start.6 = (bf16[96,1152]{1,0:T(8,128)(2,1)S(1)}, bf16[96,1152]{1,0:T(8,128)(2,1)S(1)}, u32[]{:S(2)}, u32[]{:S(2)}) collective-permute-start(bf16[96,1152]{1,0:T(8,128)(2,1)S(1)} %get-tuple-element.35), channel_id=1, source_target_pairs={{64,0},{68,4},{72,8},{76,12},{80,16},{84,20},{88,24},{92,28},{96,3... | collective-permute-start | bytes 663560 | tf_op jit(solution)/shard_map/ppermute | solution.py:371
  24.6 2.5 %collective-permute-done.2 = bf16[96,1152]{1,0:T(8,128)(2,1)S(1)} collective-permute-done((bf16[96,1152]{1,0:T(8,128)(2,1)S(1)}, bf16[96,1152]{1,0:T(8,128)(2,1)S(1)}, u32[]{:S(2)}, u32[]{:S(2)}) %collective-permute-start.2) | collective-permute-done | bytes 221216 | tf_op jit(solution)/shard_map/ppermute | solution.py:371
  27.2 3.5 %collective-permute-done.6 = bf16[96,1152]{1,0:T(8,128)(2,1)S(1)} collective-permute-done((bf16[96,1152]{1,0:T(8,128)(2,1)S(1)}, bf16[96,1152]{1,0:T(8,128)(2,1)S(1)}, u32[]{:S(2)}, u32[]{:S(2)}) %collective-permute-start.6) | collective-permute-done | bytes 221216 | tf_op jit(solution)/shard_map/ppermute | solution.py:371
  30.8 3.5 %collective-permute-start.7 = (bf16[96,1152]{1,0:T(8,128)(2,1)S(1)}, bf16[96,1152]{1,0:T(8,128)(2,1)S(1)}, u32[]{:S(2)}, u32[]{:S(2)}) collective-permute-start(bf16[96,1152]{1,0:T(8,128)(2,1)S(1)} %add_convert_fusion.1), channel_id=1, source_target_pairs={{64,0},{68,4},{72,8},{76,12},{80,16},{84,20},{88,24},{92,28},{96,3... | collective-permute-start | bytes 663560 | tf_op jit(solution)/shard_map/ppermute | solution.py:371
  34.3 2.0 %collective-permute-done.3 = bf16[96,1152]{1,0:T(8,128)(2,1)S(1)} collective-permute-done((bf16[96,1152]{1,0:T(8,128)(2,1)S(1)}, bf16[96,1152]{1,0:T(8,128)(2,1)S(1)}, u32[]{:S(2)}, u32[]{:S(2)}) %collective-permute-start.3) | collective-permute-done | bytes 221216 | tf_op jit(solution)/shard_map/ppermute | solution.py:371
  37.7 19.1 %all_to_all.10 = bf16[8,24,1152]{2,1,0:T(8,128)(2,1)S(1)} all-to-all(bf16[8,24,1152]{2,1,0:T(8,128)(2,1)S(1)} %bitcast.12), channel_id=1, replica_groups={{0,8,16,24,32,40,48,56},{4,12,20,28,36,44,52,60},{64,72,80,88,96,104,11..., dimensions={0} | all-to-all | bytes 884736 | tf_op jit(solution)/shard_map/all_to_all | solution.py:45
  56.9 15.8 %all_to_all.11 = bf16[8,24,1152]{2,1,0:T(8,128)(2,1)S(1)} all-to-all(bf16[8,24,1152]{2,1,0:T(8,128)(2,1)S(1)} %broadcast_in_dim.2), channel_id=1, replica_groups={{0,8,16,24,32,40,48,56},{4,12,20,28,36,44,52,60},{64,72,80,88,96,104,11..., dimensions={0} | all-to-all | bytes 884736 | tf_op jit(solution)/shard_map/all_to_all | solution.py:45
  72.8 3.7 %collective-permute-start.9 = (bf16[96,1152]{1,0:T(8,128)(2,1)S(1)}, bf16[96,1152]{1,0:T(8,128)(2,1)S(1)}, u32[]{:S(2)}, u32[]{:S(2)}) collective-permute-start(bf16[96,1152]{1,0:T(8,128)(2,1)S(1)} %bitcast.13), channel_id=1, source_target_pairs={{64,0},{68,4},{72,8},{76,12},{80,16},{84,20},{88,24},{92,28},{96,3... | collective-permute-start | bytes 663560 | tf_op jit(solution)/shard_map/ppermute | solution.py:371
  79.5 2.9 %collective-permute-start.12 = (bf16[96,1152]{1,0:T(8,128)(2,1)S(1)}, bf16[96,1152]{1,0:T(8,128)(2,1)S(1)}, u32[]{:S(2)}, u32[]{:S(2)}) collective-permute-start(bf16[96,1152]{1,0:T(8,128)(2,1)S(1)} %collective-permute-done.9.rest_1_), channel_id=1, source_target_pairs={{64,0},{68,4},{72,8},{76,12},{80,16},{84,20},{88,24},{92,28},{96,3... | collective-permute-start | bytes 663560 | tf_op jit(solution)/shard_map/ppermute | solution.py:371
  82.4 3.1 %collective-permute-done.13.rest_5_ = bf16[96,1152]{1,0:T(8,128)(2,1)S(1)} collective-permute-done((bf16[96,1152]{1,0:T(8,128)(2,1)S(1)}, bf16[96,1152]{1,0:T(8,128)(2,1)S(1)}, u32[]{:S(2)}, u32[]{:S(2)}) %collective-permute-start.13) | collective-permute-done | bytes 221216 | tf_op jit(solution)/shard_map/ppermute | solution.py:371
  85.6 4.1 %collective-permute-done.11.rest_2_ = bf16[96,1152]{1,0:T(8,128)(2,1)S(1)} collective-permute-done((bf16[96,1152]{1,0:T(8,128)(2,1)S(1)}, bf16[96,1152]{1,0:T(8,128)(2,1)S(1)}, u32[]{:S(2)}, u32[]{:S(2)}) %collective-permute-start.11) | collective-permute-done | bytes 221216 | tf_op jit(solution)/shard_map/ppermute | solution.py:371
  90.4 6.9 %own_step.1.own_ref = bf16[768,768]{1,0:T(8,128)(2,1)S(1)} custom-call(s32[3]{0:T(128)S(1)} %pad_add_fusion.place_ref.core_ref, bf16[768,768]{1,0:T(8,128)(2,1)S(1)} %get-tuple-element.36.x_ref, bf16[1,3,768,768]{3,2,1,0:T(8,128)(2,1)S(1)} %copy-done.2), custom_call_target="tpu_custom_call" | custom-call | flops 5435817984 | bytes 3538944 | tf_op jit(solution)/shard_map/own_step/pallas_call | solution.py:262
  97.3 4.9 %collective-permute-start.14 = (bf16[768,768]{1,0:T(8,128)(2,1)S(1)}, bf16[768,768]{1,0:T(8,128)(2,1)S(1)}, u32[]{:S(2)}, u32[]{:S(2)}) collective-permute-start(bf16[768,768]{1,0:T(8,128)(2,1)S(1)} %own_step.1.own_ref), channel_id=1, source_target_pairs={{0,4},{4,0},{8,12},{12,8},{16,20},{20,16},{24,28},{28,24},{32,36},... | collective-permute-start | bytes 3538952 | tf_op jit(solution)/shard_map/ppermute | solution.py:41
  102.6 3.0 %collective-permute-done.15.b_ref = bf16[768,384]{1,0:T(8,128)(2,1)S(1)} collective-permute-done((bf16[768,384]{1,0:T(8,128)(2,1)S(1)}, bf16[768,384]{1,0:T(8,128)(2,1)S(1)}, u32[]{:S(2)}, u32[]{:S(2)}) %collective-permute-start.15) | collective-permute-done | bytes 589856 | tf_op jit(solution)/shard_map/ppermute | solution.py:41
  105.5 7.0 %shared_step.1.shared_ref = bf16[768,768]{1,0:T(8,128)(2,1)S(1)} custom-call(s32[3]{0:T(128)S(1)} %pad_add_fusion.place_ref.core_ref, bf16[768,384]{1,0:T(8,128)(2,1)S(1)} %get-tuple-element.37.a_ref, bf16[768,384]{1,0:T(8,128)(2,1)S(1)} %collective-permute-done.15.b_ref, bf16[1,3,768,768]{3,2,1,0:T(8,128)(2,1)S(1)} %copy-done.2), custom_call_target="tpu_custom_call" | custom-call | flops 5435817984 | bytes 3538944 | tf_op jit(solution)/shard_map/shared_step/pallas_call | solution.py:287
  112.6 4.7 %project.1 = (f32[256,768]{1,0:T(8,128)S(1)}, bf16[128,768]{1,0:T(8,128)(2,1)S(1)}, bf16[128,768]{1,0:T(8,128)(2,1)S(1)}, bf16[128,768]{1,0:T(8,128)(2,1)S(1)}, ...) custom-call(s32[3]{0:T(128)S(1)} %pad_add_fusion.place_ref.core_ref, ...), custom_call_target="tpu_custom_call" | custom-call | flops 2113929216 | bytes 9437184 | tf_op jit(solution)/shard_map/project/pallas_call | solution.py:333
  120.1 2.7 %collective-permute-start.20 = (bf16[128,768]{1,0:T(8,128)(2,1)S(1)}, bf16[128,768]{1,0:T(8,128)(2,1)S(1)}, u32[]{:S(2)}, u32[]{:S(2)}) collective-permute-start(bf16[128,768]{1,0:T(8,128)(2,1)S(1)} %get-tuple-element.44), channel_id=1, source_target_pairs={{0,3},{1,0},{2,1},{3,2},{4,7},{5,4},{6,5},{7,6},{8,11},{9,8},{10,9... | collective-permute-start | bytes 589832 | tf_op jit(solution)/shard_map/ppermute | solution.py:371
  124.9 3.7 %collective-permute-done.20 = bf16[128,768]{1,0:T(8,128)(2,1)S(1)} collective-permute-done((bf16[128,768]{1,0:T(8,128)(2,1)S(1)}, bf16[128,768]{1,0:T(8,128)(2,1)S(1)}, u32[]{:S(2)}, u32[]{:S(2)}) %collective-permute-start.20) | collective-permute-done | bytes 196640 | tf_op jit(solution)/shard_map/ppermute | solution.py:371
  128.7 2.7 %collective-permute-start.21 = (bf16[128,768]{1,0:T(8,128)(2,1)S(1)}, bf16[128,768]{1,0:T(8,128)(2,1)S(1)}, u32[]{:S(2)}, u32[]{:S(2)}) collective-permute-start(bf16[128,768]{1,0:T(8,128)(2,1)S(1)} %add_convert_fusion.4), channel_id=1, source_target_pairs={{0,3},{1,0},{2,1},{3,2},{4,7},{5,4},{6,5},{7,6},{8,11},{9,8},{10,9... | collective-permute-start | bytes 589832 | tf_op jit(solution)/shard_map/ppermute | solution.py:371
  (56 shorter events, 18.6 us)
Async XLA Ops:
  11.5 6.7 %collective-permute-start = (bf16[768,768]{1,0:T(8,128)(2,1)S(1)}, bf16[768,768]{1,0:T(8,128)(2,1)S(1)}, u32[]{:S(2)}, u32[]{:S(2)}) collective-permute-start(bf16[768,768]{1,0:T(8,128)(2,1)S(1)} %get-tuple-element.26), channel_id=1, source_target_pairs={{0,4},{4,0},{8,12},{12,8},{16,20},{20,16},{24,28},{28,24},{32,36},... | collective-permute-start | bytes 3538952 | tf_op jit(solution)/shard_map/ppermute | solution.py:41
  14.9 3.3 %collective-permute-start.1 = (bf16[768,384]{1,0:T(8,128)(2,1)S(1)}, bf16[768,384]{1,0:T(8,128)(2,1)S(1)}, u32[]{:S(2)}, u32[]{:S(2)}) collective-permute-start(bf16[768,384]{1,0:T(8,128)(2,1)S(1)} %get-tuple-element.28), channel_id=1, source_target_pairs={{0,4},{4,0},{8,12},{12,8},{16,20},{20,16},{24,28},{28,24},{32,36},... | collective-permute-start | bytes 1769480 | tf_op jit(solution)/shard_map/ppermute | solution.py:41
  19.1 7.9 %collective-permute-start.2 = (bf16[96,1152]{1,0:T(8,128)(2,1)S(1)}, bf16[96,1152]{1,0:T(8,128)(2,1)S(1)}, u32[]{:S(2)}, u32[]{:S(2)}) collective-permute-start(bf16[96,1152]{1,0:T(8,128)(2,1)S(1)} %get-tuple-element.31), channel_id=1, source_target_pairs={{0,64},{4,68},{8,72},{12,76},{16,80},{20,84},{24,88},{28,92},{32,9... | collective-permute-start | bytes 663560 | tf_op jit(solution)/shard_map/ppermute | solution.py:371
  19.2 15.1 %collective-permute-start.4 = (bf16[96,1152]{1,0:T(8,128)(2,1)S(1)}, bf16[96,1152]{1,0:T(8,128)(2,1)S(1)}, u32[]{:S(2)}, u32[]{:S(2)}) collective-permute-start(bf16[96,1152]{1,0:T(8,128)(2,1)S(1)} %get-tuple-element.32), channel_id=1, source_target_pairs={{64,0},{68,4},{72,8},{76,12},{80,16},{84,20},{88,24},{92,28},{96,3... | collective-permute-start | bytes 663560 | tf_op jit(solution)/shard_map/ppermute | solution.py:371
  21.9 12.4 %collective-permute-start.5 = (bf16[96,1152]{1,0:T(8,128)(2,1)S(1)}, bf16[96,1152]{1,0:T(8,128)(2,1)S(1)}, u32[]{:S(2)}, u32[]{:S(2)}) collective-permute-start(bf16[96,1152]{1,0:T(8,128)(2,1)S(1)} %get-tuple-element.33), channel_id=1, source_target_pairs={{0,64},{4,68},{8,72},{12,76},{16,80},{20,84},{24,88},{28,92},{32,9... | collective-permute-start | bytes 663560 | tf_op jit(solution)/shard_map/ppermute | solution.py:371
  21.9 8.9 %collective-permute-start.6 = (bf16[96,1152]{1,0:T(8,128)(2,1)S(1)}, bf16[96,1152]{1,0:T(8,128)(2,1)S(1)}, u32[]{:S(2)}, u32[]{:S(2)}) collective-permute-start(bf16[96,1152]{1,0:T(8,128)(2,1)S(1)} %get-tuple-element.35), channel_id=1, source_target_pairs={{64,0},{68,4},{72,8},{76,12},{80,16},{84,20},{88,24},{92,28},{96,3... | collective-permute-start | bytes 663560 | tf_op jit(solution)/shard_map/ppermute | solution.py:371
  27.1 9.2 %collective-permute-start.3 = (bf16[96,1152]{1,0:T(8,128)(2,1)S(1)}, bf16[96,1152]{1,0:T(8,128)(2,1)S(1)}, u32[]{:S(2)}, u32[]{:S(2)}) collective-permute-start(bf16[96,1152]{1,0:T(8,128)(2,1)S(1)} %add_convert_fusion.3), channel_id=1, source_target_pairs={{0,64},{4,68},{8,72},{12,76},{16,80},{20,84},{24,88},{28,92},{32,9... | collective-permute-start | bytes 663560 | tf_op jit(solution)/shard_map/ppermute | solution.py:371
  30.8 6.7 %collective-permute-start.7 = (bf16[96,1152]{1,0:T(8,128)(2,1)S(1)}, bf16[96,1152]{1,0:T(8,128)(2,1)S(1)}, u32[]{:S(2)}, u32[]{:S(2)}) collective-permute-start(bf16[96,1152]{1,0:T(8,128)(2,1)S(1)} %add_convert_fusion.1), channel_id=1, source_target_pairs={{64,0},{68,4},{72,8},{76,12},{80,16},{84,20},{88,24},{92,28},{96,3... | collective-permute-start | bytes 663560 | tf_op jit(solution)/shard_map/ppermute | solution.py:371
  56.9 33.5 %copy-start.2 = (bf16[1,3,768,768]{3,2,1,0:T(8,128)(2,1)S(1)}, bf16[1,3,768,768]{3,2,1,0:T(8,128)(2,1)}, u32[]{:S(2)}) copy-start(bf16[1,3,768,768]{3,2,1,0:T(8,128)(2,1)} %w_hbm.5) | copy-start | bytes 10616836
  72.7 6.8 %collective-permute-start.10 = (bf16[96,1152]{1,0:T(8,128)(2,1)S(1)}, bf16[96,1152]{1,0:T(8,128)(2,1)S(1)}, u32[]{:S(2)}, u32[]{:S(2)}) collective-permute-start(bf16[96,1152]{1,0:T(8,128)(2,1)S(1)} %bitcast.15), channel_id=1, source_target_pairs={{0,64},{4,68},{8,72},{12,76},{16,80},{20,84},{24,88},{28,92},{32,9... | collective-permute-start | bytes 663560 | tf_op jit(solution)/shard_map/ppermute | solution.py:371
  72.8 6.7 %collective-permute-start.9 = (bf16[96,1152]{1,0:T(8,128)(2,1)S(1)}, bf16[96,1152]{1,0:T(8,128)(2,1)S(1)}, u32[]{:S(2)}, u32[]{:S(2)}) collective-permute-start(bf16[96,1152]{1,0:T(8,128)(2,1)S(1)} %bitcast.13), channel_id=1, source_target_pairs={{64,0},{68,4},{72,8},{76,12},{80,16},{84,20},{88,24},{92,28},{96,3... | collective-permute-start | bytes 663560 | tf_op jit(solution)/shard_map/ppermute | solution.py:371
  76.4 6.0 %collective-permute-start.8 = (bf16[96,1152]{1,0:T(8,128)(2,1)S(1)}, bf16[96,1152]{1,0:T(8,128)(2,1)S(1)}, u32[]{:S(2)}, u32[]{:S(2)}) collective-permute-start(bf16[96,1152]{1,0:T(8,128)(2,1)S(1)} %bitcast.16), channel_id=1, source_target_pairs={{64,0},{68,4},{72,8},{76,12},{80,16},{84,20},{88,24},{92,28},{96,3... | collective-permute-start | bytes 663560 | tf_op jit(solution)/shard_map/ppermute | solution.py:371
  77.6 8.0 %collective-permute-start.13 = (bf16[96,1152]{1,0:T(8,128)(2,1)S(1)}, bf16[96,1152]{1,0:T(8,128)(2,1)S(1)}, u32[]{:S(2)}, u32[]{:S(2)}) collective-permute-start(bf16[96,1152]{1,0:T(8,128)(2,1)S(1)} %bitcast.14), channel_id=1, source_target_pairs={{0,64},{4,68},{8,72},{12,76},{16,80},{20,84},{24,88},{28,92},{32,9... | collective-permute-start | bytes 663560 | tf_op jit(solution)/shard_map/ppermute | solution.py:371
  79.5 10.2 %collective-permute-start.11 = (bf16[96,1152]{1,0:T(8,128)(2,1)S(1)}, bf16[96,1152]{1,0:T(8,128)(2,1)S(1)}, u32[]{:S(2)}, u32[]{:S(2)}) collective-permute-start(bf16[96,1152]{1,0:T(8,128)(2,1)S(1)} %collective-permute-done.10.rest_4_), channel_id=1, source_target_pairs={{0,64},{4,68},{8,72},{12,76},{16,80},{20,84},{24,88},{28,92},{32,9... | collective-permute-start | bytes 663560 | tf_op jit(solution)/shard_map/ppermute | solution.py:371
  79.5 10.2 %collective-permute-start.12 = (bf16[96,1152]{1,0:T(8,128)(2,1)S(1)}, bf16[96,1152]{1,0:T(8,128)(2,1)S(1)}, u32[]{:S(2)}, u32[]{:S(2)}) collective-permute-start(bf16[96,1152]{1,0:T(8,128)(2,1)S(1)} %collective-permute-done.9.rest_1_), channel_id=1, source_target_pairs={{64,0},{68,4},{72,8},{76,12},{80,16},{84,20},{88,24},{92,28},{96,3... | collective-permute-start | bytes 663560 | tf_op jit(solution)/shard_map/ppermute | solution.py:371
  97.3 15.2 %collective-permute-start.14 = (bf16[768,768]{1,0:T(8,128)(2,1)S(1)}, bf16[768,768]{1,0:T(8,128)(2,1)S(1)}, u32[]{:S(2)}, u32[]{:S(2)}) collective-permute-start(bf16[768,768]{1,0:T(8,128)(2,1)S(1)} %own_step.1.own_ref), channel_id=1, source_target_pairs={{0,4},{4,0},{8,12},{12,8},{16,20},{20,16},{24,28},{28,24},{32,36},... | collective-permute-start | bytes 3538952 | tf_op jit(solution)/shard_map/ppermute | solution.py:41
  102.2 10.3 %copy-start = (bf16[256,768]{1,0:T(8,128)(2,1)S(1)}, bf16[256,768]{1,0:T(8,128)(2,1)}, u32[]{:S(2)}) copy-start(bf16[256,768]{1,0:T(8,128)(2,1)} %q_ref.1) | copy-start | bytes 1179652
  102.2 3.3 %collective-permute-start.15 = (bf16[768,384]{1,0:T(8,128)(2,1)S(1)}, bf16[768,384]{1,0:T(8,128)(2,1)S(1)}, u32[]{:S(2)}, u32[]{:S(2)}) collective-permute-start(bf16[768,384]{1,0:T(8,128)(2,1)S(1)} %get-tuple-element.37.a_ref), channel_id=1, source_target_pairs={{0,4},{4,0},{8,12},{12,8},{16,20},{20,16},{24,28},{28,24},{32,36},... | collective-permute-start | bytes 1769480 | tf_op jit(solution)/shard_map/ppermute | solution.py:41
  117.3 7.4 %collective-permute-start.16 = (bf16[128,768]{1,0:T(8,128)(2,1)S(1)}, bf16[128,768]{1,0:T(8,128)(2,1)S(1)}, u32[]{:S(2)}, u32[]{:S(2)}) collective-permute-start(bf16[128,768]{1,0:T(8,128)(2,1)S(1)} %get-tuple-element.40), channel_id=1, source_target_pairs={{0,1},{1,2},{2,3},{3,0},{4,5},{5,6},{6,7},{7,4},{8,9},{9,10},{10,1... | collective-permute-start | bytes 589832 | tf_op jit(solution)/shard_map/ppermute | solution.py:371
  118.6 12.8 %collective-permute-start.18 = (bf16[128,768]{1,0:T(8,128)(2,1)S(1)}, bf16[128,768]{1,0:T(8,128)(2,1)S(1)}, u32[]{:S(2)}, u32[]{:S(2)}) collective-permute-start(bf16[128,768]{1,0:T(8,128)(2,1)S(1)} %get-tuple-element.41), channel_id=1, source_target_pairs={{0,3},{1,0},{2,1},{3,2},{4,7},{5,4},{6,5},{7,6},{8,11},{9,8},{10,9... | collective-permute-start | bytes 589832 | tf_op jit(solution)/shard_map/ppermute | solution.py:371
  120.1 11.4 %collective-permute-start.19 = (bf16[128,768]{1,0:T(8,128)(2,1)S(1)}, bf16[128,768]{1,0:T(8,128)(2,1)S(1)}, u32[]{:S(2)}, u32[]{:S(2)}) collective-permute-start(bf16[128,768]{1,0:T(8,128)(2,1)S(1)} %get-tuple-element.42), channel_id=1, source_target_pairs={{0,1},{1,2},{2,3},{3,0},{4,5},{5,6},{6,7},{7,4},{8,9},{9,10},{10,1... | collective-permute-start | bytes 589832 | tf_op jit(solution)/shard_map/ppermute | solution.py:371
  120.1 8.5 %collective-permute-start.20 = (bf16[128,768]{1,0:T(8,128)(2,1)S(1)}, bf16[128,768]{1,0:T(8,128)(2,1)S(1)}, u32[]{:S(2)}, u32[]{:S(2)}) collective-permute-start(bf16[128,768]{1,0:T(8,128)(2,1)S(1)} %get-tuple-element.44), channel_id=1, source_target_pairs={{0,3},{1,0},{2,1},{3,2},{4,7},{5,4},{6,5},{7,6},{8,11},{9,8},{10,9... | collective-permute-start | bytes 589832 | tf_op jit(solution)/shard_map/ppermute | solution.py:371
  124.8 7.6 %collective-permute-start.17 = (bf16[128,768]{1,0:T(8,128)(2,1)S(1)}, bf16[128,768]{1,0:T(8,128)(2,1)S(1)}, u32[]{:S(2)}, u32[]{:S(2)}) collective-permute-start(bf16[128,768]{1,0:T(8,128)(2,1)S(1)} %add_convert_fusion.5), channel_id=1, source_target_pairs={{0,1},{1,2},{2,3},{3,0},{4,5},{5,6},{6,7},{7,4},{8,9},{9,10},{10,1... | collective-permute-start | bytes 589832 | tf_op jit(solution)/shard_map/ppermute | solution.py:371
  128.7 5.4 %collective-permute-start.21 = (bf16[128,768]{1,0:T(8,128)(2,1)S(1)}, bf16[128,768]{1,0:T(8,128)(2,1)S(1)}, u32[]{:S(2)}, u32[]{:S(2)}) collective-permute-start(bf16[128,768]{1,0:T(8,128)(2,1)S(1)} %add_convert_fusion.4), channel_id=1, source_target_pairs={{0,3},{1,0},{2,1},{3,2},{4,7},{5,4},{6,5},{7,6},{8,11},{9,8},{10,9... | collective-permute-start | bytes 589832 | tf_op jit(solution)/shard_map/ppermute | solution.py:371
  (6 other events, 25.6 us)

commit v4 on v3

--- a/solution.py
+++ b/solution.py
@@ -34,7 +34,7 @@
 
 SMEM = pl.BlockSpec(memory_space=pltpu.SMEM)
 VMEM = pl.BlockSpec(memory_space=pltpu.VMEM)
-ANY = pl.BlockSpec(memory_space=pl.ANY)
+HBM = pl.BlockSpec(memory_space=pltpu.HBM)
 
 
 def swap_cores(array):
@@ -67,11 +67,14 @@
     return lax.dot_general(left, right, (((0,), (0,)), ((), ())), preferred_element_type=f32)
 
 
-def call(body, outs, in_specs, scratch, mib, flops, moved, name):
+def call(body, outs, in_specs, scratch, mib, flops, moved, name, out_specs=None):
+    if out_specs is None:
+        out_specs = [VMEM] * len(outs) if isinstance(outs, list) else VMEM
     return pl.pallas_call(
         body,
         out_shape=outs,
         in_specs=in_specs,
+        out_specs=out_specs,
         scratch_shapes=scratch,
         compiler_params=pltpu.CompilerParams(vmem_limit_bytes=mib << 20),
         cost_estimate=pl.CostEstimate(flops=flops, bytes_accessed=moved, transcendentals=0),
@@ -88,8 +91,14 @@
     half = width // 2
     lanes = rates.shape[1]
 
-    def body(place_ref, r_ref, k_hbm, v_hbm, w_hbm, own_send, shared_send, own_keep, shared_keep,
-             k_ref, v_ref, w_ref, hidden, errors, g_keep, g_send, sems):
+    def body(place_ref, r_ref, k_hbm, v_hbm, w_hbm, *rest):
+        outs, refs = rest[:5], rest[5:10]
+        k_ref, v_ref, w_ref, errors, g_send, sems, out_sems = rest[10:]
+        own_send, shared_send, g_keep, hidden, e_keep = refs
+        stores = [
+            pltpu.make_async_copy(ref, out, out_sems.at[n])
+            for n, (ref, out) in enumerate(zip(refs, outs))
+        ]
         moves = [
             (k_hbm, k_ref),
             (w_hbm.at[0, 0], w_ref.at[0]),
@@ -129,31 +138,53 @@
             g3 = (dz * act).astype(bf16)
             g_keep[rows, :] = jnp.where(first, g1, g3)
             g_send[rows, :] = jnp.where(first, g3, g1)
+        left = errors[:, :half]
+        right = errors[:, half:]
+        e_keep[...] = jnp.where(first, left, right)
+        for store in stores[2:]:
+            store.start()
         own_send[...] = dot_tn(k_ref[...], g_send[...]).astype(bf16)
-        own_keep[...] = dot_tn(k_ref[...], g_keep[...])
-        left = dot_tn(hidden[...], errors[:, :half])
-        right = dot_tn(hidden[...], errors[:, half:])
-        shared_keep[...] = jnp.where(first, left, right)
-        shared_send[...] = jnp.where(first, right, left).astype(bf16)
-
-    return call(
-        body,
-        [
-            shape(width, width),
-            shape(width, half),
-            shape(width, width, dtype=f32),
-            shape(width, half, dtype=f32),
-        ],
-        [SMEM, VMEM] + [ANY] * 3,
-        [pltpu.VMEM((tokens, width), bf16)] * 2
+        stores[0].start()
+        shared_send[...] = dot_tn(hidden[...], jnp.where(first, right, left)).astype(bf16)
+        stores[1].start()
+        for store in stores:
+            store.wait()
+
+    results = [(width, width), (width, half), (tokens, width), (tokens, width), (tokens, half)]
+    return call(
+        body,
+        [shape(*dims) for dims in results],
+        [SMEM, VMEM] + [HBM] * 3,
+        [pltpu.VMEM(dims, bf16) for dims in results]
+        + [pltpu.VMEM((tokens, width), bf16)] * 2
         + [pltpu.VMEM((3, width, width), bf16)]
-        + [pltpu.VMEM((tokens, width), bf16)] * 4
-        + [pltpu.SemaphoreType.DMA((5,))],
-        40,
-        12 * tokens * width * width,
+        + [pltpu.VMEM((tokens, width), bf16)] * 2
+        + [pltpu.SemaphoreType.DMA((5,))] * 2,
+        60,
+        9 * tokens * width * width,
         12 * width * width,
         "gradients",
+        [HBM] * len(results),
     )(place, rates, keys, values, weights)
+
+
+def keep(keys, g_keep, hidden, e_keep):
+    width, half = hidden.shape[1], e_keep.shape[1]
+
+    def body(k_ref, g_ref, h_ref, e_ref, own, shared):
+        own[...] = dot_tn(k_ref[...], g_ref[...])
+        shared[...] = dot_tn(h_ref[...], e_ref[...])
+
+    return call(
+        body,
+        [shape(width, width, dtype=f32), shape(width, half, dtype=f32)],
+        [VMEM] * 4,
+        [],
+        16,
+        3 * keys.shape[0] * width * width,
+        9 * width * width,
+        "keep",
+    )(keys, g_keep, hidden, e_keep)
 
 
 def chip_sum(place, own_keep, own_got, shared_keep, shared_got):
@@ -219,9 +250,16 @@
     )(place, *pieces)
 
 
-def newton_schulz(x_ref, w_ref, out_ref, gram, poly, other):
+def newton_schulz(x_ref, w_ref, w_copy, outs, gram, poly, other):
     width = x_ref.shape[0]
     blocks = [slice(row, row + ROWS) for row in range(0, width, ROWS)]
+
+    def store(ref, n, below):
+        rows = blocks[n]
+        ref[rows, : rows.stop] = below
+        for column in blocks[:n]:
+            ref[column, rows] = below[:, column].T
+
     square_sum = jnp.zeros((1, 1), f32)
     for rows in blocks:
         wide = x_ref[rows, :].astype(f32)
@@ -229,14 +267,17 @@
     scale = 1.0 / (jnp.sqrt(square_sum) + eps)
     now = x_ref
     for turn in range(NS_ITERS):
-        for rows in blocks:
-            product = dot_nt(now[rows, :], now[...])
+        for n, rows in enumerate(blocks):
+            product = dot_nt(now[rows, :], now[: rows.stop, :])
             if turn == 0:
                 product = product * (scale * scale)
-            gram[rows, :] = product.astype(bf16)
-        for rows in blocks:
-            squared = dot(gram[rows, :], gram[...])
-            poly[rows, :] = (ns_b * gram[rows, :].astype(f32) + ns_c * squared).astype(bf16)
+            store(gram, n, product.astype(bf16))
+        for n, rows in enumerate(blocks):
+            squared = dot(gram[rows, :], gram[:, : rows.stop])
+            linear = gram[rows, : rows.stop].astype(f32)
+            store(poly, n, (ns_b * linear + ns_c * squared).astype(bf16))
+        if turn == NS_ITERS - 1:
+            w_copy.wait()
         for rows in blocks:
             new = ns_a * now[rows, :].astype(f32) + dot(poly[rows, :], now[...])
             if turn == 0:
@@ -246,26 +287,31 @@
                 other[rows, :] = new
             else:
                 step = step_scale * new.astype(f32)
-                out_ref[rows, :] = (w_ref[rows, :].astype(f32) - step).astype(bf16)
+                fresh = (w_ref[rows, :].astype(f32) - step).astype(bf16)
+                for n, out in enumerate(outs):
+                    height = out.shape[0]
+                    start, stop = max(rows.start, n * height), min(rows.stop, (n + 1) * height)
+                    if start < stop:
+                        inside = slice(start - n * height, stop - n * height)
+                        out[inside, :] = fresh[start - rows.start : stop - rows.start]
         now = other
 
 
 def own_step(core, summed, weights):
     width = weights.shape[-1]
 
-    def body(core_ref, x_ref, w_hbm, out_ref, gram, poly, other, w_ref, sem):
+    def body(core_ref, x_ref, w_hbm, top, bottom, gram, poly, other, w_ref, sem):
         copy = pltpu.make_async_copy(w_hbm.at[0, core_ref[0]], w_ref, sem)
         copy.start()
-        copy.wait()
-        newton_schulz(x_ref, w_ref, out_ref, gram, poly, other)
-
-    return call(
-        body,
-        shape(width, width),
-        [SMEM, VMEM, ANY],
+        newton_schulz(x_ref, w_ref, copy, (top, bottom), gram, poly, other)
+
+    return call(
+        body,
+        [shape(width // 2, width)] * 2,
+        [SMEM, VMEM, HBM],
         [pltpu.VMEM((width, width), bf16)] * 4 + [pltpu.SemaphoreType.DMA],
         20,
-        12 * width**3,
+        10 * width**3,
         6 * width * width,
         "own_step",
     )(core, summed, weights)
@@ -281,16 +327,15 @@
         first = core_ref[0] == 0
         x_ref[:, :half] = jnp.where(first, a_ref[...], b_ref[...])
         x_ref[:, half:] = jnp.where(first, b_ref[...], a_ref[...])
-        copy.wait()
-        newton_schulz(x_ref, w_ref, out_ref, gram, poly, other)
+        newton_schulz(x_ref, w_ref, copy, (out_ref,), gram, poly, other)
 
     return call(
         body,
         shape(width, width),
-        [SMEM, VMEM, VMEM, ANY],
+        [SMEM, VMEM, VMEM, HBM],
         [pltpu.VMEM((width, width), bf16)] * 5 + [pltpu.SemaphoreType.DMA],
         20,
-        12 * width**3,
+        10 * width**3,
         6 * width * width,
         "shared_step",
     )(core, mine, partners, weights)
@@ -300,30 +345,22 @@
     tokens, width = queries.shape
     heads = out_proj.shape[1] // width
 
-    def body(place_ref, q_ref, own_ref, other_ref, shared_ref, p_hbm, *rest):
-        outs, p_ref, sems = rest[:-2], rest[-2], rest[-1]
-        copies = []
-        for step in range(heads):
-            head = lax.rem(place_ref[1] + step, heads)
-            start = pl.multiple_of(head * width, width)
-            copies.append(
-                pltpu.make_async_copy(
-                    p_hbm.at[:, pl.ds(start, width)], p_ref.at[step], sems.at[step]
-                )
-            )
-        for copy in copies:
-            copy.start()
+    half = width // 2
+
+    def body(place_ref, q_ref, own_a, own_b, other_a, other_b, shared_ref, p_ref, *outs):
         first = place_ref[0] == 0
-        q_own = dot(q_ref[...], own_ref[...])
-        q_other = dot(q_ref[...], other_ref[...])
+        left, right = q_ref[:, :half], q_ref[:, half:]
+        q_own = dot(left, own_a[...]) + dot(right, own_b[...])
+        q_other = dot(left, other_a[...]) + dot(right, other_b[...])
         q1 = jnp.where(first, q_own, q_other)
         q3 = jnp.where(first, q_other, q_own)
         gated = (q1 * jax.nn.sigmoid(q1) * q3).astype(bf16)
         outputs = dot(gated, shared_ref[...]).astype(bf16)
         cut = tokens // 2
         for step in range(heads):
-            copies[step].wait()
-            product = dot(outputs, p_ref[step])
+            head = lax.rem(place_ref[1] + step, heads)
+            start = pl.multiple_of(head * width, width)
+            product = dot(outputs, p_ref[:, pl.ds(start, width)])
             if step == 0:
                 outs[0][...] = product
             else:
@@ -333,13 +370,13 @@
     return call(
         body,
         [shape(tokens, width, dtype=f32)] + [shape(tokens // 2, width)] * (2 * heads - 2),
-        [SMEM] + [VMEM] * 4 + [ANY],
-        [pltpu.VMEM((heads, width, width), bf16), pltpu.SemaphoreType.DMA((heads,))],
-        24,
+        [SMEM] + [VMEM] * 7,
+        [],
+        20,
         2 * tokens * width * width * (3 + heads),
         16 * width * width,
         "project",
-    )(place, queries, own, other, shared, out_proj)
+    )(place, queries, *own, *other, shared, out_proj)
 
 
 def mix(own, top, bottom):
@@ -406,11 +443,12 @@
     heads = lax.axis_size("head")
     place = jnp.stack([core, head, place_in_tok // (NC * NZ)]).astype(jnp.int32)
 
-    own_send, shared_send, own_keep, shared_keep = gradients(
+    own_send, shared_send, g_keep, hidden, e_keep = gradients(
         place, keys, values, rates.reshape(-1, 128), fast_weights
     )
     own_got = swap_cores(own_send)
     shared_got = swap_cores(shared_send)
+    own_keep, shared_keep = keep(keys, g_keep, hidden, e_keep)
     mine, *shares = chip_sum(place, own_keep, own_got, shared_keep, shared_got)
 
     got_a, got_b = ring_sum(shares, "tok", Y_UP, Y_DOWN)
@@ -425,7 +463,7 @@
 
     shared_other = swap_cores(shared_part)
     own_fresh = own_step(place, own_sum, fast_weights)
-    other_fresh = swap_cores(own_fresh)
+    other_fresh = [swap_cores(rows) for rows in own_fresh]
     shared_fresh = shared_step(place, shared_part, shared_other, fast_weights)
 
     mixed, *shares = project(place, queries, own_fresh, other_fresh, shared_fresh, out_proj)

time: 137 us -> 128 us (0.934)
  waiting for transfers between devices: 32.6 us -> 26.2 us
  Pallas kernels: 27.7 us -> 26 us
  local copies, waits for them, and re-layouts: 5.03 us -> 3.36 us
    ppermute x4 -> x5, waiting for transfers between devices: 6.18 us -> 0.01 us  [swap_cores(): return lax.ppermute(array, 'tok', CORE_SWAP)]
    unnamed x16 -> x18, local copies, waits for them, and re-layouts: 4.97 us -> 3.29 us
    pallas_call x1, Pallas kernels: 4.74 us -> 3.24 us  [project(): call(body, [shape(tokens, width, dtype=f32)] + [shape(tokens // 2, width)...]
    ppermute x4 -> x5, starting transfers between devices: 8.7 us -> 9.45 us  [swap_cores(): return lax.ppermute(array, 'tok', CORE_SWAP)]
    pallas_call x3 -> x4, Pallas kernels: 20.3 us -> 20.3 us  [the longest x1 7.3 us: gradients(): call(body, [shape(*dims) for dims in results], [SMEM, VMEM] + [HBM] * 3,...]
  transfers between devices with their start and end apart: 22 -> 23, of which waited for: 13 -> 11; matrix products, arithmetic and copies ran while one was open for 0% -> 0% of each run, Pallas kernels for 5% -> 10%
where the time goes in v4:
time: 128 us; the launch traced here: 126 us
  starting transfers between devices  34.9 us (27%)
  blocking collectives  34.2 us (27%)
  waiting for transfers between devices  26.2 us (20%)
  Pallas kernels  26 us (20%)
  local copies, waits for them, and re-layouts  3.36 us (3%)
    all_to_all x2, blocking collectives, exchange(): return lax.all_to_all(blocks, 'tok', 0, 0, axis_index_groups=groups)  34.2 us
    ppermute x18, waiting for transfers between devices, shift(): return lax.ppermute(array, axis, pairs)  26.1 us
    ppermute x18, starting transfers between devices, shift(): return lax.ppermute(array, axis, pairs)  25.4 us
    ppermute x5, starting transfers between devices, swap_cores(): return lax.ppermute(array, 'tok', CORE_SWAP)  9.45 us
    pallas_call x1, Pallas kernels, gradients(): call(body, [shape(*dims) for dims in results], [SMEM, VMEM] + [HBM] * 3,...  7.3 us
    pallas_call x1, Pallas kernels, shared_step(): call(body, shape(width, width), [SMEM, VMEM, VMEM, HBM], [pltpu.VMEM((wid...  5.94 us
    pallas_call x1, Pallas kernels, own_step(): call(body, [shape(width // 2, width)] * 2, [SMEM, VMEM, HBM], [pltpu.VMEM...  5.83 us
    unnamed x18, local copies, waits for them, and re-layouts  3.29 us
  transfers between devices with their start and end apart: 23, of which 11 were waited for; matrix products, arithmetic and copies ran while one was open for 0% of the time, Pallas kernels for 10%

profile of v4, /device:TPU:1, one launch (start us, length us, event | category | flops | bytes accessed | tf_op | source)
XLA Modules:
  0.0 125.9 jit_solution(4300170446315726841)
XLA Ops:
  0.6 7.3 %gradients.1 = (bf16[768,768]{1,0:T(8,128)(2,1)}, bf16[768,384]{1,0:T(8,128)(2,1)}, bf16[512,768]{1,0:T(8,128)(2,1)}, bf16[512,768]{1,0:T(8,128)(2,1)}, bf16[512,384]{1,0:T(8,128)(2,1)}) custom-call(s32[3]{0:T(128)} %pad_add_fusion.place_ref.core_ref, f32[4,128]{1,0:T(4,128)} %bitcast.16, bf16[512,768]{1,0:T(8,128)(2,1)} %k_ref.1, bf16[512,768]{1,0:T(8,128)(2,1)} %v_hbm.1, ...), custom_call_target="tpu_custom_call" | custom-call | flops 2717908992 | bytes 7077888 | tf_op jit(solution)/shard_map/gradients/pallas_call | solution.py:154
  7.9 3.3 %collective-permute-start = (bf16[768,768]{1,0:T(8,128)(2,1)}, bf16[768,768]{1,0:T(8,128)(2,1)S(1)}, u32[]{:S(2)}, u32[]{:S(2)}) collective-permute-start(bf16[768,768]{1,0:T(8,128)(2,1)} %get-tuple-element.34), channel_id=1, source_target_pairs={{0,4},{4,0},{8,12},{12,8},{16,20},{20,16},{24,28},{28,24},{32,36},... | collective-permute-start | bytes 3538952 | tf_op jit(solution)/shard_map/ppermute | solution.py:41
  16.8 2.7 %collective-permute-start.4 = (bf16[96,1152]{1,0:T(8,128)(2,1)S(1)}, bf16[96,1152]{1,0:T(8,128)(2,1)S(1)}, u32[]{:S(2)}, u32[]{:S(2)}) collective-permute-start(bf16[96,1152]{1,0:T(8,128)(2,1)S(1)} %get-tuple-element.40), channel_id=1, source_target_pairs={{64,0},{68,4},{72,8},{76,12},{80,16},{84,20},{88,24},{92,28},{96,3... | collective-permute-start | bytes 663560 | tf_op jit(solution)/shard_map/ppermute | solution.py:408
  19.5 2.7 %collective-permute-start.6 = (bf16[96,1152]{1,0:T(8,128)(2,1)S(1)}, bf16[96,1152]{1,0:T(8,128)(2,1)S(1)}, u32[]{:S(2)}, u32[]{:S(2)}) collective-permute-start(bf16[96,1152]{1,0:T(8,128)(2,1)S(1)} %get-tuple-element.43), channel_id=1, source_target_pairs={{64,0},{68,4},{72,8},{76,12},{80,16},{84,20},{88,24},{92,28},{96,3... | collective-permute-start | bytes 663560 | tf_op jit(solution)/shard_map/ppermute | solution.py:408
  22.1 2.5 %collective-permute-done.2 = bf16[96,1152]{1,0:T(8,128)(2,1)S(1)} collective-permute-done((bf16[96,1152]{1,0:T(8,128)(2,1)S(1)}, bf16[96,1152]{1,0:T(8,128)(2,1)S(1)}, u32[]{:S(2)}, u32[]{:S(2)}) %collective-permute-start.2) | collective-permute-done | bytes 221216 | tf_op jit(solution)/shard_map/ppermute | solution.py:408
  24.8 3.5 %collective-permute-done.6 = bf16[96,1152]{1,0:T(8,128)(2,1)S(1)} collective-permute-done((bf16[96,1152]{1,0:T(8,128)(2,1)S(1)}, bf16[96,1152]{1,0:T(8,128)(2,1)S(1)}, u32[]{:S(2)}, u32[]{:S(2)}) %collective-permute-start.6) | collective-permute-done | bytes 221216 | tf_op jit(solution)/shard_map/ppermute | solution.py:408
  28.3 3.5 %collective-permute-start.7 = (bf16[96,1152]{1,0:T(8,128)(2,1)S(1)}, bf16[96,1152]{1,0:T(8,128)(2,1)S(1)}, u32[]{:S(2)}, u32[]{:S(2)}) collective-permute-start(bf16[96,1152]{1,0:T(8,128)(2,1)S(1)} %add_convert_fusion.1), channel_id=1, source_target_pairs={{64,0},{68,4},{72,8},{76,12},{80,16},{84,20},{88,24},{92,28},{96,3... | collective-permute-start | bytes 663560 | tf_op jit(solution)/shard_map/ppermute | solution.py:408
  31.8 2.0 %collective-permute-done.3 = bf16[96,1152]{1,0:T(8,128)(2,1)S(1)} collective-permute-done((bf16[96,1152]{1,0:T(8,128)(2,1)S(1)}, bf16[96,1152]{1,0:T(8,128)(2,1)S(1)}, u32[]{:S(2)}, u32[]{:S(2)}) %collective-permute-start.3) | collective-permute-done | bytes 221216 | tf_op jit(solution)/shard_map/ppermute | solution.py:408
  35.2 19.0 %all_to_all.10 = bf16[8,24,1152]{2,1,0:T(8,128)(2,1)S(1)} all-to-all(bf16[8,24,1152]{2,1,0:T(8,128)(2,1)S(1)} %bitcast.11), channel_id=1, replica_groups={{0,8,16,24,32,40,48,56},{4,12,20,28,36,44,52,60},{64,72,80,88,96,104,11..., dimensions={0} | all-to-all | bytes 884736 | tf_op jit(solution)/shard_map/all_to_all | solution.py:45
  54.3 15.1 %all_to_all.11 = bf16[8,24,1152]{2,1,0:T(8,128)(2,1)S(1)} all-to-all(bf16[8,24,1152]{2,1,0:T(8,128)(2,1)S(1)} %broadcast_in_dim.2), channel_id=1, replica_groups={{0,8,16,24,32,40,48,56},{4,12,20,28,36,44,52,60},{64,72,80,88,96,104,11..., dimensions={0} | all-to-all | bytes 884736 | tf_op jit(solution)/shard_map/all_to_all | solution.py:45
  69.6 3.7 %collective-permute-start.9 = (bf16[96,1152]{1,0:T(8,128)(2,1)S(1)}, bf16[96,1152]{1,0:T(8,128)(2,1)S(1)}, u32[]{:S(2)}, u32[]{:S(2)}) collective-permute-start(bf16[96,1152]{1,0:T(8,128)(2,1)S(1)} %bitcast.12), channel_id=1, source_target_pairs={{64,0},{68,4},{72,8},{76,12},{80,16},{84,20},{88,24},{92,28},{96,3... | collective-permute-start | bytes 663560 | tf_op jit(solution)/shard_map/ppermute | solution.py:408
  74.8 1.6 %collective-permute-done.10.rest_4_ = bf16[96,1152]{1,0:T(8,128)(2,1)S(1)} collective-permute-done((bf16[96,1152]{1,0:T(8,128)(2,1)S(1)}, bf16[96,1152]{1,0:T(8,128)(2,1)S(1)}, u32[]{:S(2)}, u32[]{:S(2)}) %collective-permute-start.10) | collective-permute-done | bytes 221216 | tf_op jit(solution)/shard_map/ppermute | solution.py:408
  76.4 2.9 %collective-permute-start.12 = (bf16[96,1152]{1,0:T(8,128)(2,1)S(1)}, bf16[96,1152]{1,0:T(8,128)(2,1)S(1)}, u32[]{:S(2)}, u32[]{:S(2)}) collective-permute-start(bf16[96,1152]{1,0:T(8,128)(2,1)S(1)} %collective-permute-done.9.rest_1_), channel_id=1, source_target_pairs={{64,0},{68,4},{72,8},{76,12},{80,16},{84,20},{88,24},{92,28},{96,3... | collective-permute-start | bytes 663560 | tf_op jit(solution)/shard_map/ppermute | solution.py:408
  79.3 2.9 %collective-permute-done.13.rest_5_ = bf16[96,1152]{1,0:T(8,128)(2,1)S(1)} collective-permute-done((bf16[96,1152]{1,0:T(8,128)(2,1)S(1)}, bf16[96,1152]{1,0:T(8,128)(2,1)S(1)}, u32[]{:S(2)}, u32[]{:S(2)}) %collective-permute-start.13) | collective-permute-done | bytes 221216 | tf_op jit(solution)/shard_map/ppermute | solution.py:408
  82.2 4.1 %collective-permute-done.11.rest_2_ = bf16[96,1152]{1,0:T(8,128)(2,1)S(1)} collective-permute-done((bf16[96,1152]{1,0:T(8,128)(2,1)S(1)}, bf16[96,1152]{1,0:T(8,128)(2,1)S(1)}, u32[]{:S(2)}, u32[]{:S(2)}) %collective-permute-start.11) | collective-permute-done | bytes 221216 | tf_op jit(solution)/shard_map/ppermute | solution.py:408
  87.0 5.4 %collective-permute-start.16 = (bf16[768,384]{1,0:T(8,128)(2,1)S(1)}, bf16[768,384]{1,0:T(8,128)(2,1)S(1)}, u32[]{:S(2)}, u32[]{:S(2)}) collective-permute-start(bf16[768,384]{1,0:T(8,128)(2,1)S(1)} %get-tuple-element.47.a_ref), channel_id=1, source_target_pairs={{0,4},{4,0},{8,12},{12,8},{16,20},{20,16},{24,28},{28,24},{32,36},... | collective-permute-start | bytes 1769480 | tf_op jit(solution)/shard_map/ppermute | solution.py:41
  92.5 5.8 %own_step.1 = (bf16[384,768]{1,0:T(8,128)(2,1)S(1)}, bf16[384,768]{1,0:T(8,128)(2,1)S(1)}) custom-call(s32[3]{0:T(128)S(1)} %copy-done.1, bf16[768,768]{1,0:T(8,128)(2,1)S(1)} %get-tuple-element.44.x_ref, bf16[1,3,768,768]{3,2,1,0:T(8,128)(2,1)S(1)} %copy-done.2), custom_call_target="tpu_custom_call" | custom-call | flops 4529848320 | bytes 3538944 | tf_op jit(solution)/shard_map/own_step/pallas_call | solution.py:308
  98.9 5.9 %shared_step.1.shared_ref = bf16[768,768]{1,0:T(8,128)(2,1)S(1)} custom-call(s32[3]{0:T(128)S(1)} %copy-done.1, bf16[768,384]{1,0:T(8,128)(2,1)S(1)} %get-tuple-element.47.a_ref, bf16[768,384]{1,0:T(8,128)(2,1)S(1)} %collective-permute-done.16.b_ref, bf16[1,3,768,768]{3,2,1,0:T(8,128)(2,1)S(1)} %copy-done.2), custom_call_target="tpu_custom_call" | custom-call | flops 4529848320 | bytes 3538944 | tf_op jit(solution)/shard_map/shared_step/pallas_call | solution.py:332
  104.9 3.2 %project.1 = (f32[256,768]{1,0:T(8,128)S(1)}, bf16[128,768]{1,0:T(8,128)(2,1)S(1)}, bf16[128,768]{1,0:T(8,128)(2,1)S(1)}, bf16[128,768]{1,0:T(8,128)(2,1)S(1)}, ...) custom-call(s32[3]{0:T(128)S(1)} %copy-done.1, ...), custom_call_target="tpu_custom_call" | custom-call | flops 2113929216 | bytes 9437184 | tf_op jit(solution)/shard_map/project/pallas_call | solution.py:370
  110.9 2.7 %collective-permute-start.21 = (bf16[128,768]{1,0:T(8,128)(2,1)S(1)}, bf16[128,768]{1,0:T(8,128)(2,1)S(1)}, u32[]{:S(2)}, u32[]{:S(2)}) collective-permute-start(bf16[128,768]{1,0:T(8,128)(2,1)S(1)} %get-tuple-element.54), channel_id=1, source_target_pairs={{0,3},{1,0},{2,1},{3,2},{4,7},{5,4},{6,5},{7,6},{8,11},{9,8},{10,9... | collective-permute-start | bytes 589832 | tf_op jit(solution)/shard_map/ppermute | solution.py:408
  113.6 2.0 %collective-permute-done.17 = bf16[128,768]{1,0:T(8,128)(2,1)S(1)} collective-permute-done((bf16[128,768]{1,0:T(8,128)(2,1)S(1)}, bf16[128,768]{1,0:T(8,128)(2,1)S(1)}, u32[]{:S(2)}, u32[]{:S(2)}) %collective-permute-start.17) | collective-permute-done | bytes 196640 | tf_op jit(solution)/shard_map/ppermute | solution.py:408
  115.7 3.7 %collective-permute-done.21 = bf16[128,768]{1,0:T(8,128)(2,1)S(1)} collective-permute-done((bf16[128,768]{1,0:T(8,128)(2,1)S(1)}, bf16[128,768]{1,0:T(8,128)(2,1)S(1)}, u32[]{:S(2)}, u32[]{:S(2)}) %collective-permute-start.21) | collective-permute-done | bytes 196640 | tf_op jit(solution)/shard_map/ppermute | solution.py:408
  119.5 2.7 %collective-permute-start.22 = (bf16[128,768]{1,0:T(8,128)(2,1)S(1)}, bf16[128,768]{1,0:T(8,128)(2,1)S(1)}, u32[]{:S(2)}, u32[]{:S(2)}) collective-permute-start(bf16[128,768]{1,0:T(8,128)(2,1)S(1)} %add_convert_fusion.4), channel_id=1, source_target_pairs={{0,3},{1,0},{2,1},{3,2},{4,7},{5,4},{6,5},{7,6},{8,11},{9,8},{10,9... | collective-permute-start | bytes 589832 | tf_op jit(solution)/shard_map/ppermute | solution.py:408
  123.2 1.7 %collective-permute-done.22.rest_3_ = bf16[128,768]{1,0:T(8,128)(2,1)S(1)} collective-permute-done((bf16[128,768]{1,0:T(8,128)(2,1)S(1)}, bf16[128,768]{1,0:T(8,128)(2,1)S(1)}, u32[]{:S(2)}, u32[]{:S(2)}) %collective-permute-start.22) | collective-permute-done | bytes 196640 | tf_op jit(solution)/shard_map/ppermute | solution.py:408
  (61 shorter events, 15.5 us)
Async XLA Ops:
  7.9 7.9 %collective-permute-start = (bf16[768,768]{1,0:T(8,128)(2,1)}, bf16[768,768]{1,0:T(8,128)(2,1)S(1)}, u32[]{:S(2)}, u32[]{:S(2)}) collective-permute-start(bf16[768,768]{1,0:T(8,128)(2,1)} %get-tuple-element.34), channel_id=1, source_target_pairs={{0,4},{4,0},{8,12},{12,8},{16,20},{20,16},{24,28},{28,24},{32,36},... | collective-permute-start | bytes 3538952 | tf_op jit(solution)/shard_map/ppermute | solution.py:41
  11.2 4.6 %collective-permute-start.1 = (bf16[768,384]{1,0:T(8,128)(2,1)}, bf16[768,384]{1,0:T(8,128)(2,1)S(1)}, u32[]{:S(2)}, u32[]{:S(2)}) collective-permute-start(bf16[768,384]{1,0:T(8,128)(2,1)} %get-tuple-element.36), channel_id=1, source_target_pairs={{0,4},{4,0},{8,12},{12,8},{16,20},{20,16},{24,28},{28,24},{32,36},... | collective-permute-start | bytes 1769480 | tf_op jit(solution)/shard_map/ppermute | solution.py:41
  16.7 7.9 %collective-permute-start.2 = (bf16[96,1152]{1,0:T(8,128)(2,1)S(1)}, bf16[96,1152]{1,0:T(8,128)(2,1)S(1)}, u32[]{:S(2)}, u32[]{:S(2)}) collective-permute-start(bf16[96,1152]{1,0:T(8,128)(2,1)S(1)} %get-tuple-element.39), channel_id=1, source_target_pairs={{0,64},{4,68},{8,72},{12,76},{16,80},{20,84},{24,88},{28,92},{32,9... | collective-permute-start | bytes 663560 | tf_op jit(solution)/shard_map/ppermute | solution.py:408
  16.8 15.0 %collective-permute-start.4 = (bf16[96,1152]{1,0:T(8,128)(2,1)S(1)}, bf16[96,1152]{1,0:T(8,128)(2,1)S(1)}, u32[]{:S(2)}, u32[]{:S(2)}) collective-permute-start(bf16[96,1152]{1,0:T(8,128)(2,1)S(1)} %get-tuple-element.40), channel_id=1, source_target_pairs={{64,0},{68,4},{72,8},{76,12},{80,16},{84,20},{88,24},{92,28},{96,3... | collective-permute-start | bytes 663560 | tf_op jit(solution)/shard_map/ppermute | solution.py:408
  19.5 12.4 %collective-permute-start.5 = (bf16[96,1152]{1,0:T(8,128)(2,1)S(1)}, bf16[96,1152]{1,0:T(8,128)(2,1)S(1)}, u32[]{:S(2)}, u32[]{:S(2)}) collective-permute-start(bf16[96,1152]{1,0:T(8,128)(2,1)S(1)} %get-tuple-element.41), channel_id=1, source_target_pairs={{0,64},{4,68},{8,72},{12,76},{16,80},{20,84},{24,88},{28,92},{32,9... | collective-permute-start | bytes 663560 | tf_op jit(solution)/shard_map/ppermute | solution.py:408
  19.5 8.8 %collective-permute-start.6 = (bf16[96,1152]{1,0:T(8,128)(2,1)S(1)}, bf16[96,1152]{1,0:T(8,128)(2,1)S(1)}, u32[]{:S(2)}, u32[]{:S(2)}) collective-permute-start(bf16[96,1152]{1,0:T(8,128)(2,1)S(1)} %get-tuple-element.43), channel_id=1, source_target_pairs={{64,0},{68,4},{72,8},{76,12},{80,16},{84,20},{88,24},{92,28},{96,3... | collective-permute-start | bytes 663560 | tf_op jit(solution)/shard_map/ppermute | solution.py:408
  24.7 9.2 %collective-permute-start.3 = (bf16[96,1152]{1,0:T(8,128)(2,1)S(1)}, bf16[96,1152]{1,0:T(8,128)(2,1)S(1)}, u32[]{:S(2)}, u32[]{:S(2)}) collective-permute-start(bf16[96,1152]{1,0:T(8,128)(2,1)S(1)} %add_convert_fusion.3), channel_id=1, source_target_pairs={{0,64},{4,68},{8,72},{12,76},{16,80},{20,84},{24,88},{28,92},{32,9... | collective-permute-start | bytes 663560 | tf_op jit(solution)/shard_map/ppermute | solution.py:408
  28.3 6.6 %collective-permute-start.7 = (bf16[96,1152]{1,0:T(8,128)(2,1)S(1)}, bf16[96,1152]{1,0:T(8,128)(2,1)S(1)}, u32[]{:S(2)}, u32[]{:S(2)}) collective-permute-start(bf16[96,1152]{1,0:T(8,128)(2,1)S(1)} %add_convert_fusion.1), channel_id=1, source_target_pairs={{64,0},{68,4},{72,8},{76,12},{80,16},{84,20},{88,24},{92,28},{96,3... | collective-permute-start | bytes 663560 | tf_op jit(solution)/shard_map/ppermute | solution.py:408
  54.3 38.1 %copy-start.2 = (bf16[1,3,768,768]{3,2,1,0:T(8,128)(2,1)S(1)}, bf16[1,3,768,768]{3,2,1,0:T(8,128)(2,1)}, u32[]{:S(2)}) copy-start(bf16[1,3,768,768]{3,2,1,0:T(8,128)(2,1)} %w_hbm.5) | copy-start | bytes 10616836
  69.5 6.8 %collective-permute-start.10 = (bf16[96,1152]{1,0:T(8,128)(2,1)S(1)}, bf16[96,1152]{1,0:T(8,128)(2,1)S(1)}, u32[]{:S(2)}, u32[]{:S(2)}) collective-permute-start(bf16[96,1152]{1,0:T(8,128)(2,1)S(1)} %bitcast.14), channel_id=1, source_target_pairs={{0,64},{4,68},{8,72},{12,76},{16,80},{20,84},{24,88},{28,92},{32,9... | collective-permute-start | bytes 663560 | tf_op jit(solution)/shard_map/ppermute | solution.py:408
  69.6 6.7 %collective-permute-start.9 = (bf16[96,1152]{1,0:T(8,128)(2,1)S(1)}, bf16[96,1152]{1,0:T(8,128)(2,1)S(1)}, u32[]{:S(2)}, u32[]{:S(2)}) collective-permute-start(bf16[96,1152]{1,0:T(8,128)(2,1)S(1)} %bitcast.12), channel_id=1, source_target_pairs={{64,0},{68,4},{72,8},{76,12},{80,16},{84,20},{88,24},{92,28},{96,3... | collective-permute-start | bytes 663560 | tf_op jit(solution)/shard_map/ppermute | solution.py:408
  73.3 6.0 %collective-permute-start.8 = (bf16[96,1152]{1,0:T(8,128)(2,1)S(1)}, bf16[96,1152]{1,0:T(8,128)(2,1)S(1)}, u32[]{:S(2)}, u32[]{:S(2)}) collective-permute-start(bf16[96,1152]{1,0:T(8,128)(2,1)S(1)} %bitcast.15), channel_id=1, source_target_pairs={{64,0},{68,4},{72,8},{76,12},{80,16},{84,20},{88,24},{92,28},{96,3... | collective-permute-start | bytes 663560 | tf_op jit(solution)/shard_map/ppermute | solution.py:408
  74.5 7.7 %collective-permute-start.13 = (bf16[96,1152]{1,0:T(8,128)(2,1)S(1)}, bf16[96,1152]{1,0:T(8,128)(2,1)S(1)}, u32[]{:S(2)}, u32[]{:S(2)}) collective-permute-start(bf16[96,1152]{1,0:T(8,128)(2,1)S(1)} %bitcast.13), channel_id=1, source_target_pairs={{0,64},{4,68},{8,72},{12,76},{16,80},{20,84},{24,88},{28,92},{32,9... | collective-permute-start | bytes 663560 | tf_op jit(solution)/shard_map/ppermute | solution.py:408
  76.3 10.0 %collective-permute-start.11 = (bf16[96,1152]{1,0:T(8,128)(2,1)S(1)}, bf16[96,1152]{1,0:T(8,128)(2,1)S(1)}, u32[]{:S(2)}, u32[]{:S(2)}) collective-permute-start(bf16[96,1152]{1,0:T(8,128)(2,1)S(1)} %collective-permute-done.10.rest_4_), channel_id=1, source_target_pairs={{0,64},{4,68},{8,72},{12,76},{16,80},{20,84},{24,88},{28,92},{32,9... | collective-permute-start | bytes 663560 | tf_op jit(solution)/shard_map/ppermute | solution.py:408
  76.4 10.0 %collective-permute-start.12 = (bf16[96,1152]{1,0:T(8,128)(2,1)S(1)}, bf16[96,1152]{1,0:T(8,128)(2,1)S(1)}, u32[]{:S(2)}, u32[]{:S(2)}) collective-permute-start(bf16[96,1152]{1,0:T(8,128)(2,1)S(1)} %collective-permute-done.9.rest_1_), channel_id=1, source_target_pairs={{64,0},{68,4},{72,8},{76,12},{80,16},{84,20},{88,24},{92,28},{96,3... | collective-permute-start | bytes 663560 | tf_op jit(solution)/shard_map/ppermute | solution.py:408
  87.0 11.9 %collective-permute-start.16 = (bf16[768,384]{1,0:T(8,128)(2,1)S(1)}, bf16[768,384]{1,0:T(8,128)(2,1)S(1)}, u32[]{:S(2)}, u32[]{:S(2)}) collective-permute-start(bf16[768,384]{1,0:T(8,128)(2,1)S(1)} %get-tuple-element.47.a_ref), channel_id=1, source_target_pairs={{0,4},{4,0},{8,12},{12,8},{16,20},{20,16},{24,28},{28,24},{32,36},... | collective-permute-start | bytes 1769480 | tf_op jit(solution)/shard_map/ppermute | solution.py:41
  98.3 6.6 %collective-permute-start.14 = (bf16[384,768]{1,0:T(8,128)(2,1)S(1)}, bf16[384,768]{1,0:T(8,128)(2,1)S(1)}, u32[]{:S(2)}, u32[]{:S(2)}) collective-permute-start(bf16[384,768]{1,0:T(8,128)(2,1)S(1)} %get-tuple-element.45.own_a), channel_id=1, source_target_pairs={{0,4},{4,0},{8,12},{12,8},{16,20},{20,16},{24,28},{28,24},{32,36},... | collective-permute-start | bytes 1769480 | tf_op jit(solution)/shard_map/ppermute | solution.py:41
  98.4 6.4 %collective-permute-start.15 = (bf16[384,768]{1,0:T(8,128)(2,1)S(1)}, bf16[384,768]{1,0:T(8,128)(2,1)S(1)}, u32[]{:S(2)}, u32[]{:S(2)}) collective-permute-start(bf16[384,768]{1,0:T(8,128)(2,1)S(1)} %get-tuple-element.46.own_b), channel_id=1, source_target_pairs={{0,4},{4,0},{8,12},{12,8},{16,20},{20,16},{24,28},{28,24},{32,36},... | collective-permute-start | bytes 1769480 | tf_op jit(solution)/shard_map/ppermute | solution.py:41
  108.1 7.4 %collective-permute-start.17 = (bf16[128,768]{1,0:T(8,128)(2,1)S(1)}, bf16[128,768]{1,0:T(8,128)(2,1)S(1)}, u32[]{:S(2)}, u32[]{:S(2)}) collective-permute-start(bf16[128,768]{1,0:T(8,128)(2,1)S(1)} %get-tuple-element.50), channel_id=1, source_target_pairs={{0,1},{1,2},{2,3},{3,0},{4,5},{5,6},{6,7},{7,4},{8,9},{9,10},{10,1... | collective-permute-start | bytes 589832 | tf_op jit(solution)/shard_map/ppermute | solution.py:408
  109.4 12.8 %collective-permute-start.19 = (bf16[128,768]{1,0:T(8,128)(2,1)S(1)}, bf16[128,768]{1,0:T(8,128)(2,1)S(1)}, u32[]{:S(2)}, u32[]{:S(2)}) collective-permute-start(bf16[128,768]{1,0:T(8,128)(2,1)S(1)} %get-tuple-element.51), channel_id=1, source_target_pairs={{0,3},{1,0},{2,1},{3,2},{4,7},{5,4},{6,5},{7,6},{8,11},{9,8},{10,9... | collective-permute-start | bytes 589832 | tf_op jit(solution)/shard_map/ppermute | solution.py:408
  110.9 11.4 %collective-permute-start.20 = (bf16[128,768]{1,0:T(8,128)(2,1)S(1)}, bf16[128,768]{1,0:T(8,128)(2,1)S(1)}, u32[]{:S(2)}, u32[]{:S(2)}) collective-permute-start(bf16[128,768]{1,0:T(8,128)(2,1)S(1)} %get-tuple-element.52), channel_id=1, source_target_pairs={{0,1},{1,2},{2,3},{3,0},{4,5},{5,6},{6,7},{7,4},{8,9},{9,10},{10,1... | collective-permute-start | bytes 589832 | tf_op jit(solution)/shard_map/ppermute | solution.py:408
  110.9 8.6 %collective-permute-start.21 = (bf16[128,768]{1,0:T(8,128)(2,1)S(1)}, bf16[128,768]{1,0:T(8,128)(2,1)S(1)}, u32[]{:S(2)}, u32[]{:S(2)}) collective-permute-start(bf16[128,768]{1,0:T(8,128)(2,1)S(1)} %get-tuple-element.54), channel_id=1, source_target_pairs={{0,3},{1,0},{2,1},{3,2},{4,7},{5,4},{6,5},{7,6},{8,11},{9,8},{10,9... | collective-permute-start | bytes 589832 | tf_op jit(solution)/shard_map/ppermute | solution.py:408
  115.6 7.6 %collective-permute-start.18 = (bf16[128,768]{1,0:T(8,128)(2,1)S(1)}, bf16[128,768]{1,0:T(8,128)(2,1)S(1)}, u32[]{:S(2)}, u32[]{:S(2)}) collective-permute-start(bf16[128,768]{1,0:T(8,128)(2,1)S(1)} %add_convert_fusion.5), channel_id=1, source_target_pairs={{0,1},{1,2},{2,3},{3,0},{4,5},{5,6},{6,7},{7,4},{8,9},{9,10},{10,1... | collective-permute-start | bytes 589832 | tf_op jit(solution)/shard_map/ppermute | solution.py:408
  119.5 5.4 %collective-permute-start.22 = (bf16[128,768]{1,0:T(8,128)(2,1)S(1)}, bf16[128,768]{1,0:T(8,128)(2,1)S(1)}, u32[]{:S(2)}, u32[]{:S(2)}) collective-permute-start(bf16[128,768]{1,0:T(8,128)(2,1)S(1)} %add_convert_fusion.4), channel_id=1, source_target_pairs={{0,3},{1,0},{2,1},{3,2},{4,7},{5,4},{6,5},{7,6},{8,11},{9,8},{10,9... | collective-permute-start | bytes 589832 | tf_op jit(solution)/shard_map/ppermute | solution.py:408
  (8 other events, 34.7 us)

commit v5 on v4

--- a/solution.py
+++ b/solution.py
@@ -32,7 +32,6 @@
 Y_DOWN = [(there, here) for here, there in Y_UP]
 CORE_SWAP = [(device, device ^ 1) for device in range(NY * NZ * NC)]
 
-SMEM = pl.BlockSpec(memory_space=pltpu.SMEM)
 VMEM = pl.BlockSpec(memory_space=pltpu.VMEM)
 HBM = pl.BlockSpec(memory_space=pltpu.HBM)
 
@@ -82,19 +81,28 @@
     )
 
 
+def own_core():
+    return lax.rem(lax.axis_index("tok"), NC)
+
+
+def own_y():
+    return lax.div(lax.axis_index("tok"), NZ * NC)
+
+
 def shape(*dims, dtype=bf16):
     return jax.ShapeDtypeStruct(dims, dtype)
 
 
-def gradients(place, keys, values, rates, weights):
+def gradients(keys, values, rates, weights):
     tokens, width = keys.shape
     half = width // 2
     lanes = rates.shape[1]
 
-    def body(place_ref, r_ref, k_hbm, v_hbm, w_hbm, *rest):
-        outs, refs = rest[:5], rest[5:10]
-        k_ref, v_ref, w_ref, errors, g_send, sems, out_sems = rest[10:]
-        own_send, shared_send, g_keep, hidden, e_keep = refs
+    def body(r_ref, k_hbm, v_hbm, w_hbm, *rest):
+        outs, refs = rest[:3], rest[3:6]
+        k_ref, v_ref, w_ref, errors, g_send, sems, out_sems = rest[6:]
+        own_send, shared_send, factors = refs
+        g_keep, hidden = factors.at[:, :width], factors.at[:, width : 2 * width]
         stores = [
             pltpu.make_async_copy(ref, out, out_sems.at[n])
             for n, (ref, out) in enumerate(zip(refs, outs))
@@ -111,7 +119,7 @@
         ]
         for copy in copies:
             copy.start()
-        first = place_ref[0] == 0
+        first = own_core() == 0
         rate_columns = r_ref[...].T
         copies[0].wait()
         copies[1].wait()
@@ -140,9 +148,8 @@
             g_send[rows, :] = jnp.where(first, g3, g1)
         left = errors[:, :half]
         right = errors[:, half:]
-        e_keep[...] = jnp.where(first, left, right)
-        for store in stores[2:]:
-            store.start()
+        factors[:, 2 * width :] = jnp.where(first, left, right)
+        stores[2].start()
         own_send[...] = dot_tn(k_ref[...], g_send[...]).astype(bf16)
         stores[0].start()
         shared_send[...] = dot_tn(hidden[...], jnp.where(first, right, left)).astype(bf16)
@@ -150,51 +157,52 @@
         for store in stores:
             store.wait()
 
-    results = [(width, width), (width, half), (tokens, width), (tokens, width), (tokens, half)]
+    results = [(width, width), (width, half), (tokens, 2 * width + half)]
     return call(
         body,
         [shape(*dims) for dims in results],
-        [SMEM, VMEM] + [HBM] * 3,
+        [VMEM] + [HBM] * 3,
         [pltpu.VMEM(dims, bf16) for dims in results]
         + [pltpu.VMEM((tokens, width), bf16)] * 2
         + [pltpu.VMEM((3, width, width), bf16)]
         + [pltpu.VMEM((tokens, width), bf16)] * 2
-        + [pltpu.SemaphoreType.DMA((5,))] * 2,
+        + [pltpu.SemaphoreType.DMA((5,)), pltpu.SemaphoreType.DMA((3,))],
         60,
         9 * tokens * width * width,
         12 * width * width,
         "gradients",
         [HBM] * len(results),
-    )(place, rates, keys, values, weights)
-
-
-def keep(keys, g_keep, hidden, e_keep):
-    width, half = hidden.shape[1], e_keep.shape[1]
-
-    def body(k_ref, g_ref, h_ref, e_ref, own, shared):
-        own[...] = dot_tn(k_ref[...], g_ref[...])
-        shared[...] = dot_tn(h_ref[...], e_ref[...])
+    )(rates, keys, values, weights)
+
+
+def keep(keys, factors):
+    width = keys.shape[1]
+    half = width // 2
+
+    def body(k_ref, f_ref, own, shared):
+        own[...] = dot_tn(k_ref[...], f_ref[:, :width])
+        shared[...] = dot_tn(f_ref[:, width : 2 * width], f_ref[:, 2 * width :])
 
     return call(
         body,
         [shape(width, width, dtype=f32), shape(width, half, dtype=f32)],
-        [VMEM] * 4,
+        [VMEM] * 2,
         [],
         16,
         3 * keys.shape[0] * width * width,
         9 * width * width,
         "keep",
-    )(keys, g_keep, hidden, e_keep)
-
-
-def chip_sum(place, own_keep, own_got, shared_keep, shared_got):
+    )(keys, factors)
+
+
+def chip_sum(own_keep, own_got, shared_keep, shared_got):
     width, half = shared_keep.shape
     rows = width // NY
     wide = width + half
 
-    def body(place_ref, ok_ref, og_ref, sk_ref, sg_ref, mine, *outs):
+    def body(ok_ref, og_ref, sk_ref, sg_ref, mine, *outs):
         for step in range(NY):
-            start = lax.rem(place_ref[2] + step, NY) * rows
+            start = lax.rem(own_y() + step, NY) * rows
             for part in range(2):
                 cut = rows // 2
                 span = pl.ds(pl.multiple_of(start + part * cut, cut), cut)
@@ -211,23 +219,23 @@
     return call(
         body,
         [shape(rows, wide, dtype=f32)] + [shape(rows // 2, wide)] * (2 * NY - 2),
-        [SMEM] + [VMEM] * 4,
+        [VMEM] * 4,
         [],
         16,
         0,
         10 * width * wide,
         "chip_sum",
-    )(place, own_keep, own_got, shared_keep, shared_got)
-
-
-def assemble(place, own, previous, following, opposite):
+    )(own_keep, own_got, shared_keep, shared_got)
+
+
+def assemble(own, previous, following, opposite):
     rows, wide = own.shape
     width = rows * NY
     pieces = [own, *following, *opposite, *previous]
 
-    def body(place_ref, own_ref, *rest):
+    def body(own_ref, *rest):
         parts, (x_ref, s_ref) = rest[:-2], rest[-2:]
-        base = place_ref[2]
+        base = own_y()
         start = pl.multiple_of(base * rows, rows)
         x_ref[pl.ds(start, rows), :] = own_ref[:, :width]
         s_ref[pl.ds(start, rows), :] = own_ref[:, width:]
@@ -241,13 +249,13 @@
     return call(
         body,
         [shape(width, width), shape(width, wide - width)],
-        [SMEM] + [VMEM] * len(pieces),
+        [VMEM] * len(pieces),
         [],
         16,
         0,
         4 * width * wide,
         "assemble",
-    )(place, *pieces)
+    )(*pieces)
 
 
 def newton_schulz(x_ref, w_ref, w_copy, outs, gram, poly, other):
@@ -297,34 +305,34 @@
         now = other
 
 
-def own_step(core, summed, weights):
+def own_step(summed, weights):
     width = weights.shape[-1]
 
-    def body(core_ref, x_ref, w_hbm, top, bottom, gram, poly, other, w_ref, sem):
-        copy = pltpu.make_async_copy(w_hbm.at[0, core_ref[0]], w_ref, sem)
+    def body(x_ref, w_hbm, top, bottom, gram, poly, other, w_ref, sem):
+        copy = pltpu.make_async_copy(w_hbm.at[0, own_core()], w_ref, sem)
         copy.start()
         newton_schulz(x_ref, w_ref, copy, (top, bottom), gram, poly, other)
 
     return call(
         body,
         [shape(width // 2, width)] * 2,
-        [SMEM, VMEM, HBM],
+        [VMEM, HBM],
         [pltpu.VMEM((width, width), bf16)] * 4 + [pltpu.SemaphoreType.DMA],
         20,
         10 * width**3,
         6 * width * width,
         "own_step",
-    )(core, summed, weights)
-
-
-def shared_step(core, mine, partners, weights):
+    )(summed, weights)
+
+
+def shared_step(mine, partners, weights):
     width = weights.shape[-1]
     half = width // 2
 
-    def body(core_ref, a_ref, b_ref, w_hbm, out_ref, gram, poly, other, x_ref, w_ref, sem):
+    def body(a_ref, b_ref, w_hbm, out_ref, gram, poly, other, x_ref, w_ref, sem):
         copy = pltpu.make_async_copy(w_hbm.at[0, 2], w_ref, sem)
         copy.start()
-        first = core_ref[0] == 0
+        first = own_core() == 0
         x_ref[:, :half] = jnp.where(first, a_ref[...], b_ref[...])
         x_ref[:, half:] = jnp.where(first, b_ref[...], a_ref[...])
         newton_schulz(x_ref, w_ref, copy, (out_ref,), gram, poly, other)
@@ -332,23 +340,23 @@
     return call(
         body,
         shape(width, width),
-        [SMEM, VMEM, VMEM, HBM],
+        [VMEM, VMEM, HBM],
         [pltpu.VMEM((width, width), bf16)] * 5 + [pltpu.SemaphoreType.DMA],
         20,
         10 * width**3,
         6 * width * width,
         "shared_step",
-    )(core, mine, partners, weights)
-
-
-def project(place, queries, own, other, shared, out_proj):
+    )(mine, partners, weights)
+
+
+def project(queries, own, other, shared, out_proj):
     tokens, width = queries.shape
     heads = out_proj.shape[1] // width
 
     half = width // 2
 
-    def body(place_ref, q_ref, own_a, own_b, other_a, other_b, shared_ref, p_ref, *outs):
-        first = place_ref[0] == 0
+    def body(q_ref, own_a, own_b, other_a, other_b, shared_ref, p_ref, *outs):
+        first = own_core() == 0
         left, right = q_ref[:, :half], q_ref[:, half:]
         q_own = dot(left, own_a[...]) + dot(right, own_b[...])
         q_other = dot(left, other_a[...]) + dot(right, other_b[...])
@@ -358,7 +366,7 @@
         outputs = dot(gated, shared_ref[...]).astype(bf16)
         cut = tokens // 2
         for step in range(heads):
-            head = lax.rem(place_ref[1] + step, heads)
+            head = lax.rem(lax.axis_index("head") + step, heads)
             start = pl.multiple_of(head * width, width)
             product = dot(outputs, p_ref[:, pl.ds(start, width)])
             if step == 0:
@@ -370,38 +378,29 @@
     return call(
         body,
         [shape(tokens, width, dtype=f32)] + [shape(tokens // 2, width)] * (2 * heads - 2),
-        [SMEM] + [VMEM] * 7,
+        [VMEM] * 7,
         [],
         20,
         2 * tokens * width * width * (3 + heads),
         16 * width * width,
         "project",
-    )(place, queries, *own, *other, shared, out_proj)
-
-
-def mix(own, top, bottom):
+    )(queries, *own, *other, shared, out_proj)
+
+
+def mix(own, sum_a, sum_b, direct_a, direct_b):
     tokens, width = own.shape
     cut = tokens // 2
-    count = len(top)
-
-    def body(own_ref, *rest):
-        out = rest[-1]
-        for part in range(2):
-            total = own_ref[part * cut : (part + 1) * cut, :]
-            for ref in rest[part * count : (part + 1) * count]:
-                total = total + ref[...].astype(f32)
-            out[:, part * cut : (part + 1) * cut] = total.T.astype(bf16)
-
-    return call(
-        body,
-        shape(width, tokens),
-        [VMEM] * (1 + 2 * count),
-        [],
-        16,
-        0,
-        12 * tokens * width,
-        "mix",
-    )(own, *top, *bottom)
+
+    def body(sum_a_ref, sum_b_ref, direct_a_ref, direct_b_ref, own_ref, out):
+        halves = [(sum_a_ref, direct_a_ref), (sum_b_ref, direct_b_ref)]
+        for part, (relayed, direct) in enumerate(halves):
+            span = slice(part * cut, (part + 1) * cut)
+            total = own_ref[span, :] + relayed[...].astype(f32) + direct[...].astype(f32)
+            out[:, span] = total.T.astype(bf16)
+
+    return call(
+        body, shape(width, tokens), [VMEM] * 5, [], 16, 0, 12 * tokens * width, "mix"
+    )(sum_a, sum_b, direct_a, direct_b, own)
 
 
 def shift(array, axis, pairs):
@@ -420,7 +419,7 @@
     from_up_a = shift(previous_a, axis, down)
     from_down_a = shift(add(next_a, relay_a), axis, up)
     from_up_b = shift(add(previous_b, relay_b), axis, down)
-    return [from_down_a, from_up_a], [from_down_b, from_up_b]
+    return from_down_a, from_up_b, from_up_a, from_down_b
 
 
 def ring_gather(block, axis, up, down):
@@ -437,36 +436,31 @@
 
 def on_device(keys, values, rates, fast_weights, queries, out_proj):
     width = fast_weights.shape[-1]
-    place_in_tok = lax.axis_index("tok")
-    core = place_in_tok % NC
-    head = lax.axis_index("head")
     heads = lax.axis_size("head")
-    place = jnp.stack([core, head, place_in_tok // (NC * NZ)]).astype(jnp.int32)
-
-    own_send, shared_send, g_keep, hidden, e_keep = gradients(
-        place, keys, values, rates.reshape(-1, 128), fast_weights
+
+    own_send, shared_send, factors = gradients(
+        keys, values, rates.reshape(-1, 128), fast_weights
     )
     own_got = swap_cores(own_send)
     shared_got = swap_cores(shared_send)
-    own_keep, shared_keep = keep(keys, g_keep, hidden, e_keep)
-    mine, *shares = chip_sum(place, own_keep, own_got, shared_keep, shared_got)
-
-    got_a, got_b = ring_sum(shares, "tok", Y_UP, Y_DOWN)
-    cut = mine.shape[0] // 2
-    first_half = mine[:cut] + got_a[0].astype(f32) + got_a[1].astype(f32)
-    second_half = mine[cut:] + got_b[0].astype(f32) + got_b[1].astype(f32)
-    y_sum = jnp.concatenate([first_half, second_half]).astype(bf16)
+    own_keep, shared_keep = keep(keys, factors)
+    mine, *shares = chip_sum(own_keep, own_got, shared_keep, shared_got)
+
+    sum_a, sum_b, direct_a, direct_b = ring_sum(shares, "tok", Y_UP, Y_DOWN)
+    relayed = jnp.concatenate([sum_a, sum_b]).astype(f32)
+    direct = jnp.concatenate([direct_a, direct_b]).astype(f32)
+    y_sum = (relayed + direct + mine).astype(bf16)
     z_sum = sum_shares(y_sum.reshape(NZ, width // NY // NZ, -1), Z_GROUPS)
     y_rows = gather_rows(z_sum, Z_GROUPS)
     previous, following, far = ring_gather(y_rows, "tok", Y_UP, Y_DOWN)
-    own_sum, shared_part = assemble(place, y_rows, previous, following, far)
+    own_sum, shared_part = assemble(y_rows, previous, following, far)
 
     shared_other = swap_cores(shared_part)
-    own_fresh = own_step(place, own_sum, fast_weights)
+    own_fresh = own_step(own_sum, fast_weights)
     other_fresh = [swap_cores(rows) for rows in own_fresh]
-    shared_fresh = shared_step(place, shared_part, shared_other, fast_weights)
-
-    mixed, *shares = project(place, queries, own_fresh, other_fresh, shared_fresh, out_proj)
+    shared_fresh = shared_step(shared_part, shared_other, fast_weights)
+
+    mixed, *shares = project(queries, own_fresh, other_fresh, shared_fresh, out_proj)
     up = [(i, (i + 1) % heads) for i in range(heads)]
     down = [(i, (i - 1) % heads) for i in range(heads)]
     return mix(mixed, *ring_sum(shares, "head", up, down))

time: 128 us -> 120 us (0.938); the launches traced: 126 us -> 119 us
  starting transfers between devices: 34.9 us -> 30 us
  Pallas kernels: 26 us -> 23.5 us
  waiting for transfers between devices: 26.2 us -> 28.4 us
  local copies, waits for them, and re-layouts: 3.36 us -> 1.63 us
    ppermute x18, starting transfers between devices: 25.4 us -> 21.3 us  [shift(): return lax.ppermute(array, axis, pairs)]
    unnamed x18 -> x12, local copies, waits for them, and re-layouts: 3.29 us -> 1.57 us
    ppermute x18, waiting for transfers between devices: 26.1 us -> 27.7 us  [shift(): return lax.ppermute(array, axis, pairs)]
    pallas_call x5, Pallas kernels: 20.7 us -> 19.2 us  [the longest x1 7.48 us: gradients(): call(body, [shape(*dims) for dims in results], [VMEM] + [HBM] * 3, [pltpu...]
where the time goes in v5:
time: 120 us; the launch traced here: 119 us
  blocking collectives  35.3 us (29%)
  starting transfers between devices  30 us (25%)
  waiting for transfers between devices  28.4 us (24%)
  Pallas kernels  23.5 us (20%)
  local copies, waits for them, and re-layouts  1.63 us (1%)
    all_to_all x2, blocking collectives, exchange(): return lax.all_to_all(blocks, 'tok', 0, 0, axis_index_groups=groups)  35.3 us
    ppermute x18, waiting for transfers between devices, shift(): return lax.ppermute(array, axis, pairs)  27.7 us
    ppermute x18, starting transfers between devices, shift(): return lax.ppermute(array, axis, pairs)  21.3 us
    ppermute x5, starting transfers between devices, swap_cores(): return lax.ppermute(array, 'tok', CORE_SWAP)  8.71 us
    pallas_call x1, Pallas kernels, gradients(): call(body, [shape(*dims) for dims in results], [VMEM] + [HBM] * 3, [pltpu...  7.48 us
    pallas_call x1, Pallas kernels, shared_step(): call(body, shape(width, width), [VMEM, VMEM, HBM], [pltpu.VMEM((width, wi...  5.4 us
    pallas_call x1, Pallas kernels, own_step(): call(body, [shape(width // 2, width)] * 2, [VMEM, HBM], [pltpu.VMEM((widt...  5.28 us
    pallas_call x1, Pallas kernels, project(): call(body, [shape(tokens, width, dtype=f32)] + [shape(tokens // 2, width)...  2.69 us
  transfers between devices with their start and end apart: 23, of which 11 were waited for; matrix products, arithmetic and copies ran while one was open for 0% of the time, Pallas kernels for 10%

profile of v5, /device:TPU:1, one launch (start us, length us, event | category | flops | bytes accessed | tf_op | source)
XLA Modules:
  0.0 119.4 jit_solution(3426872130615033811)
XLA Ops:
  0.0 7.5 %gradients.1 = (bf16[768,768]{1,0:T(8,128)(2,1)}, bf16[768,384]{1,0:T(8,128)(2,1)}, bf16[512,1920]{1,0:T(8,128)(2,1)}) custom-call(f32[4,128]{1,0:T(4,128)} %bitcast.13, bf16[512,768]{1,0:T(8,128)(2,1)} %k_ref.1, bf16[512,768]{1,0:T(8,128)(2,1)} %v_hbm.1, bf16[1,3,768,768]{3,2,1,0:T(8,128)(2,1)} %w_hbm.5), custom_call_target="tpu_custom_call" | custom-call | flops 2717908992 | bytes 7077888 | tf_op jit(solution)/shard_map/gradients/pallas_call | solution.py:161
  7.5 3.3 %collective-permute-start = (bf16[768,768]{1,0:T(8,128)(2,1)}, bf16[768,768]{1,0:T(8,128)(2,1)S(1)}, u32[]{:S(2)}, u32[]{:S(2)}) collective-permute-start(bf16[768,768]{1,0:T(8,128)(2,1)} %get-tuple-element.30), channel_id=1, source_target_pairs={{0,4},{4,0},{8,12},{12,8},{16,20},{20,16},{24,28},{28,24},{32,36},... | collective-permute-start | bytes 3538952 | tf_op jit(solution)/shard_map/ppermute | solution.py:40
  10.9 1.5 %copy-done.3 = bf16[512,1920]{1,0:T(8,128)(2,1)S(1)} copy-done((bf16[512,1920]{1,0:T(8,128)(2,1)S(1)}, bf16[512,1920]{1,0:T(8,128)(2,1)}, u32[]{:S(2)}) %copy-start.3) | copy-done | bytes 1966104
  14.7 2.7 %collective-permute-start.4 = (bf16[96,1152]{1,0:T(8,128)(2,1)S(1)}, bf16[96,1152]{1,0:T(8,128)(2,1)S(1)}, u32[]{:S(2)}, u32[]{:S(2)}) collective-permute-start(bf16[96,1152]{1,0:T(8,128)(2,1)S(1)} %get-tuple-element.36), channel_id=1, source_target_pairs={{64,0},{68,4},{72,8},{76,12},{80,16},{84,20},{88,24},{92,28},{96,3... | collective-permute-start | bytes 663560 | tf_op jit(solution)/shard_map/ppermute | solution.py:407
  17.4 1.4 %collective-permute-start.7 = (bf16[96,1152]{1,0:T(8,128)(2,1)S(1)}, bf16[96,1152]{1,0:T(8,128)(2,1)S(1)}, u32[]{:S(2)}, u32[]{:S(2)}) collective-permute-start(bf16[96,1152]{1,0:T(8,128)(2,1)S(1)} %get-tuple-element.38), channel_id=1, source_target_pairs={{0,64},{4,68},{8,72},{12,76},{16,80},{20,84},{24,88},{28,92},{32,9... | collective-permute-start | bytes 663560 | tf_op jit(solution)/shard_map/ppermute | solution.py:407
  18.9 3.7 %collective-permute-done.2 = bf16[96,1152]{1,0:T(8,128)(2,1)S(1)} collective-permute-done((bf16[96,1152]{1,0:T(8,128)(2,1)S(1)}, bf16[96,1152]{1,0:T(8,128)(2,1)S(1)}, u32[]{:S(2)}, u32[]{:S(2)}) %collective-permute-start.2) | collective-permute-done | bytes 221216 | tf_op jit(solution)/shard_map/ppermute | solution.py:407
  22.8 2.7 %collective-permute-start.5 = (bf16[96,1152]{1,0:T(8,128)(2,1)S(1)}, bf16[96,1152]{1,0:T(8,128)(2,1)S(1)}, u32[]{:S(2)}, u32[]{:S(2)}) collective-permute-start(bf16[96,1152]{1,0:T(8,128)(2,1)S(1)} %add_convert_fusion.1), channel_id=1, source_target_pairs={{64,0},{68,4},{72,8},{76,12},{80,16},{84,20},{88,24},{92,28},{96,3... | collective-permute-start | bytes 663560 | tf_op jit(solution)/shard_map/ppermute | solution.py:407
  27.3 4.5 %collective-permute-done.3 = bf16[96,1152]{1,0:T(8,128)(2,1)S(1)} collective-permute-done((bf16[96,1152]{1,0:T(8,128)(2,1)S(1)}, bf16[96,1152]{1,0:T(8,128)(2,1)S(1)}, u32[]{:S(2)}, u32[]{:S(2)}) %collective-permute-start.3) | collective-permute-done | bytes 221216 | tf_op jit(solution)/shard_map/ppermute | solution.py:407
  32.0 19.8 %all_to_all.10 = bf16[8,24,1152]{2,1,0:T(8,128)(2,1)S(1)} all-to-all(bf16[8,24,1152]{2,1,0:T(8,128)(2,1)S(1)} %bitcast.8), channel_id=1, replica_groups={{0,8,16,24,32,40,48,56},{4,12,20,28,36,44,52,60},{64,72,80,88,96,104,11..., dimensions={0} | all-to-all | bytes 884736 | tf_op jit(solution)/shard_map/all_to_all | solution.py:44
  51.9 15.5 %all_to_all.11 = bf16[8,24,1152]{2,1,0:T(8,128)(2,1)S(1)} all-to-all(bf16[8,24,1152]{2,1,0:T(8,128)(2,1)S(1)} %broadcast_in_dim.2), channel_id=1, replica_groups={{0,8,16,24,32,40,48,56},{4,12,20,28,36,44,52,60},{64,72,80,88,96,104,11..., dimensions={0} | all-to-all | bytes 884736 | tf_op jit(solution)/shard_map/all_to_all | solution.py:44
  67.4 1.4 %collective-permute-start.10 = (bf16[96,1152]{1,0:T(8,128)(2,1)S(1)}, bf16[96,1152]{1,0:T(8,128)(2,1)S(1)}, u32[]{:S(2)}, u32[]{:S(2)}) collective-permute-start(bf16[96,1152]{1,0:T(8,128)(2,1)S(1)} %bitcast.11), channel_id=1, source_target_pairs={{0,64},{4,68},{8,72},{12,76},{16,80},{20,84},{24,88},{28,92},{32,9... | collective-permute-start | bytes 663560 | tf_op jit(solution)/shard_map/ppermute | solution.py:407
  68.8 1.6 %collective-permute-start.9 = (bf16[96,1152]{1,0:T(8,128)(2,1)S(1)}, bf16[96,1152]{1,0:T(8,128)(2,1)S(1)}, u32[]{:S(2)}, u32[]{:S(2)}) collective-permute-start(bf16[96,1152]{1,0:T(8,128)(2,1)S(1)} %bitcast.9), channel_id=1, source_target_pairs={{64,0},{68,4},{72,8},{76,12},{80,16},{84,20},{88,24},{92,28},{96,3... | collective-permute-start | bytes 663560 | tf_op jit(solution)/shard_map/ppermute | solution.py:407
  71.9 1.7 %collective-permute-done.10.rest_4_ = bf16[96,1152]{1,0:T(8,128)(2,1)S(1)} collective-permute-done((bf16[96,1152]{1,0:T(8,128)(2,1)S(1)}, bf16[96,1152]{1,0:T(8,128)(2,1)S(1)}, u32[]{:S(2)}, u32[]{:S(2)}) %collective-permute-start.10) | collective-permute-done | bytes 221216 | tf_op jit(solution)/shard_map/ppermute | solution.py:407
  73.6 2.8 %collective-permute-start.12 = (bf16[96,1152]{1,0:T(8,128)(2,1)S(1)}, bf16[96,1152]{1,0:T(8,128)(2,1)S(1)}, u32[]{:S(2)}, u32[]{:S(2)}) collective-permute-start(bf16[96,1152]{1,0:T(8,128)(2,1)S(1)} %collective-permute-done.9.rest_1_), channel_id=1, source_target_pairs={{64,0},{68,4},{72,8},{76,12},{80,16},{84,20},{88,24},{92,28},{96,3... | collective-permute-start | bytes 663560 | tf_op jit(solution)/shard_map/ppermute | solution.py:407
  76.4 3.1 %collective-permute-done.13.rest_5_ = bf16[96,1152]{1,0:T(8,128)(2,1)S(1)} collective-permute-done((bf16[96,1152]{1,0:T(8,128)(2,1)S(1)}, bf16[96,1152]{1,0:T(8,128)(2,1)S(1)}, u32[]{:S(2)}, u32[]{:S(2)}) %collective-permute-start.13) | collective-permute-done | bytes 221216 | tf_op jit(solution)/shard_map/ppermute | solution.py:407
  79.5 4.4 %collective-permute-done.11.rest_2_ = bf16[96,1152]{1,0:T(8,128)(2,1)S(1)} collective-permute-done((bf16[96,1152]{1,0:T(8,128)(2,1)S(1)}, bf16[96,1152]{1,0:T(8,128)(2,1)S(1)}, u32[]{:S(2)}, u32[]{:S(2)}) %collective-permute-start.11) | collective-permute-done | bytes 221216 | tf_op jit(solution)/shard_map/ppermute | solution.py:407
  84.1 4.7 %collective-permute-start.16 = (bf16[768,384]{1,0:T(8,128)(2,1)S(1)}, bf16[768,384]{1,0:T(8,128)(2,1)S(1)}, u32[]{:S(2)}, u32[]{:S(2)}) collective-permute-start(bf16[768,384]{1,0:T(8,128)(2,1)S(1)} %get-tuple-element.43.a_ref), channel_id=1, source_target_pairs={{0,4},{4,0},{8,12},{12,8},{16,20},{20,16},{24,28},{28,24},{32,36},... | collective-permute-start | bytes 1769480 | tf_op jit(solution)/shard_map/ppermute | solution.py:40
  88.8 5.3 %own_step.1 = (bf16[384,768]{1,0:T(8,128)(2,1)S(1)}, bf16[384,768]{1,0:T(8,128)(2,1)S(1)}) custom-call(bf16[768,768]{1,0:T(8,128)(2,1)S(1)} %get-tuple-element.40.x_ref, bf16[1,3,768,768]{3,2,1,0:T(8,128)(2,1)S(1)} %copy-done.1), custom_call_target="tpu_custom_call" | custom-call | flops 4529848320 | bytes 3538944 | tf_op jit(solution)/shard_map/own_step/pallas_call | solution.py:316
  94.7 5.4 %shared_step.1.shared_ref = bf16[768,768]{1,0:T(8,128)(2,1)S(1)} custom-call(bf16[768,384]{1,0:T(8,128)(2,1)S(1)} %get-tuple-element.43.a_ref, bf16[768,384]{1,0:T(8,128)(2,1)S(1)} %collective-permute-done.16.b_ref, bf16[1,3,768,768]{3,2,1,0:T(8,128)(2,1)S(1)} %copy-done.1), custom_call_target="tpu_custom_call" | custom-call | flops 4529848320 | bytes 3538944 | tf_op jit(solution)/shard_map/shared_step/pallas_call | solution.py:340
  100.1 2.7 %project.1 = (f32[256,768]{1,0:T(8,128)S(1)}, bf16[128,768]{1,0:T(8,128)(2,1)S(1)}, bf16[128,768]{1,0:T(8,128)(2,1)S(1)}, bf16[128,768]{1,0:T(8,128)(2,1)S(1)}, ...) custom-call(bf16[256,768]{1,0:T(8,128)(2,1)S(1)} %copy-done, ...), custom_call_target="tpu_custom_call" | custom-call | flops 2113929216 | bytes 9437184 | tf_op jit(solution)/shard_map/project/pallas_call | solution.py:378
  104.1 1.5 %collective-permute-start.19 = (bf16[128,768]{1,0:T(8,128)(2,1)S(1)}, bf16[128,768]{1,0:T(8,128)(2,1)S(1)}, u32[]{:S(2)}, u32[]{:S(2)}) collective-permute-start(bf16[128,768]{1,0:T(8,128)(2,1)S(1)} %get-tuple-element.47), channel_id=1, source_target_pairs={{0,3},{1,0},{2,1},{3,2},{4,7},{5,4},{6,5},{7,6},{8,11},{9,8},{10,9... | collective-permute-start | bytes 589832 | tf_op jit(solution)/shard_map/ppermute | solution.py:407
  107.1 3.2 %collective-permute-done.17 = bf16[128,768]{1,0:T(8,128)(2,1)S(1)} collective-permute-done((bf16[128,768]{1,0:T(8,128)(2,1)S(1)}, bf16[128,768]{1,0:T(8,128)(2,1)S(1)}, u32[]{:S(2)}, u32[]{:S(2)}) %collective-permute-start.17) | collective-permute-done | bytes 196640 | tf_op jit(solution)/shard_map/ppermute | solution.py:407
  110.5 2.7 %collective-permute-start.20 = (bf16[128,768]{1,0:T(8,128)(2,1)S(1)}, bf16[128,768]{1,0:T(8,128)(2,1)S(1)}, u32[]{:S(2)}, u32[]{:S(2)}) collective-permute-start(bf16[128,768]{1,0:T(8,128)(2,1)S(1)} %add_convert_fusion.3), channel_id=1, source_target_pairs={{0,3},{1,0},{2,1},{3,2},{4,7},{5,4},{6,5},{7,6},{8,11},{9,8},{10,9... | collective-permute-start | bytes 589832 | tf_op jit(solution)/shard_map/ppermute | solution.py:407
  114.1 4.3 %collective-permute-done.18.sum_a_ref = bf16[128,768]{1,0:T(8,128)(2,1)S(1)} collective-permute-done((bf16[128,768]{1,0:T(8,128)(2,1)S(1)}, bf16[128,768]{1,0:T(8,128)(2,1)S(1)}, u32[]{:S(2)}, u32[]{:S(2)}) %collective-permute-start.18) | collective-permute-done | bytes 196640 | tf_op jit(solution)/shard_map/ppermute | solution.py:407
  (53 shorter events, 11.8 us)
Async XLA Ops:
  7.5 6.9 %collective-permute-start = (bf16[768,768]{1,0:T(8,128)(2,1)}, bf16[768,768]{1,0:T(8,128)(2,1)S(1)}, u32[]{:S(2)}, u32[]{:S(2)}) collective-permute-start(bf16[768,768]{1,0:T(8,128)(2,1)} %get-tuple-element.30), channel_id=1, source_target_pairs={{0,4},{4,0},{8,12},{12,8},{16,20},{20,16},{24,28},{28,24},{32,36},... | collective-permute-start | bytes 3538952 | tf_op jit(solution)/shard_map/ppermute | solution.py:40
  10.8 3.5 %collective-permute-start.1 = (bf16[768,384]{1,0:T(8,128)(2,1)}, bf16[768,384]{1,0:T(8,128)(2,1)S(1)}, u32[]{:S(2)}, u32[]{:S(2)}) collective-permute-start(bf16[768,384]{1,0:T(8,128)(2,1)} %get-tuple-element.32), channel_id=1, source_target_pairs={{0,4},{4,0},{8,12},{12,8},{16,20},{20,16},{24,28},{28,24},{32,36},... | collective-permute-start | bytes 1769480 | tf_op jit(solution)/shard_map/ppermute | solution.py:40
  14.7 7.9 %collective-permute-start.2 = (bf16[96,1152]{1,0:T(8,128)(2,1)S(1)}, bf16[96,1152]{1,0:T(8,128)(2,1)S(1)}, u32[]{:S(2)}, u32[]{:S(2)}) collective-permute-start(bf16[96,1152]{1,0:T(8,128)(2,1)S(1)} %get-tuple-element.34), channel_id=1, source_target_pairs={{0,64},{4,68},{8,72},{12,76},{16,80},{20,84},{24,88},{28,92},{32,9... | collective-permute-start | bytes 663560 | tf_op jit(solution)/shard_map/ppermute | solution.py:407
  14.7 8.0 %collective-permute-start.4 = (bf16[96,1152]{1,0:T(8,128)(2,1)S(1)}, bf16[96,1152]{1,0:T(8,128)(2,1)S(1)}, u32[]{:S(2)}, u32[]{:S(2)}) collective-permute-start(bf16[96,1152]{1,0:T(8,128)(2,1)S(1)} %get-tuple-element.36), channel_id=1, source_target_pairs={{64,0},{68,4},{72,8},{76,12},{80,16},{84,20},{88,24},{92,28},{96,3... | collective-permute-start | bytes 663560 | tf_op jit(solution)/shard_map/ppermute | solution.py:407
  17.4 8.9 %collective-permute-start.6 = (bf16[96,1152]{1,0:T(8,128)(2,1)S(1)}, bf16[96,1152]{1,0:T(8,128)(2,1)S(1)}, u32[]{:S(2)}, u32[]{:S(2)}) collective-permute-start(bf16[96,1152]{1,0:T(8,128)(2,1)S(1)} %get-tuple-element.37), channel_id=1, source_target_pairs={{64,0},{68,4},{72,8},{76,12},{80,16},{84,20},{88,24},{92,28},{96,3... | collective-permute-start | bytes 663560 | tf_op jit(solution)/shard_map/ppermute | solution.py:407
  17.4 9.9 %collective-permute-start.7 = (bf16[96,1152]{1,0:T(8,128)(2,1)S(1)}, bf16[96,1152]{1,0:T(8,128)(2,1)S(1)}, u32[]{:S(2)}, u32[]{:S(2)}) collective-permute-start(bf16[96,1152]{1,0:T(8,128)(2,1)S(1)} %get-tuple-element.38), channel_id=1, source_target_pairs={{0,64},{4,68},{8,72},{12,76},{16,80},{20,84},{24,88},{28,92},{32,9... | collective-permute-start | bytes 663560 | tf_op jit(solution)/shard_map/ppermute | solution.py:407
  22.6 9.2 %collective-permute-start.3 = (bf16[96,1152]{1,0:T(8,128)(2,1)S(1)}, bf16[96,1152]{1,0:T(8,128)(2,1)S(1)}, u32[]{:S(2)}, u32[]{:S(2)}) collective-permute-start(bf16[96,1152]{1,0:T(8,128)(2,1)S(1)} %add_convert_fusion.2), channel_id=1, source_target_pairs={{0,64},{4,68},{8,72},{12,76},{16,80},{20,84},{24,88},{28,92},{32,9... | collective-permute-start | bytes 663560 | tf_op jit(solution)/shard_map/ppermute | solution.py:407
  22.8 9.0 %collective-permute-start.5 = (bf16[96,1152]{1,0:T(8,128)(2,1)S(1)}, bf16[96,1152]{1,0:T(8,128)(2,1)S(1)}, u32[]{:S(2)}, u32[]{:S(2)}) collective-permute-start(bf16[96,1152]{1,0:T(8,128)(2,1)S(1)} %add_convert_fusion.1), channel_id=1, source_target_pairs={{64,0},{68,4},{72,8},{76,12},{80,16},{84,20},{88,24},{92,28},{96,3... | collective-permute-start | bytes 663560 | tf_op jit(solution)/shard_map/ppermute | solution.py:407
  51.9 36.9 %copy-start.1 = (bf16[1,3,768,768]{3,2,1,0:T(8,128)(2,1)S(1)}, bf16[1,3,768,768]{3,2,1,0:T(8,128)(2,1)}, u32[]{:S(2)}) copy-start(bf16[1,3,768,768]{3,2,1,0:T(8,128)(2,1)} %w_hbm.5) | copy-start | bytes 10616836
  67.4 6.1 %collective-permute-start.10 = (bf16[96,1152]{1,0:T(8,128)(2,1)S(1)}, bf16[96,1152]{1,0:T(8,128)(2,1)S(1)}, u32[]{:S(2)}, u32[]{:S(2)}) collective-permute-start(bf16[96,1152]{1,0:T(8,128)(2,1)S(1)} %bitcast.11), channel_id=1, source_target_pairs={{0,64},{4,68},{8,72},{12,76},{16,80},{20,84},{24,88},{28,92},{32,9... | collective-permute-start | bytes 663560 | tf_op jit(solution)/shard_map/ppermute | solution.py:407
  68.8 4.8 %collective-permute-start.9 = (bf16[96,1152]{1,0:T(8,128)(2,1)S(1)}, bf16[96,1152]{1,0:T(8,128)(2,1)S(1)}, u32[]{:S(2)}, u32[]{:S(2)}) collective-permute-start(bf16[96,1152]{1,0:T(8,128)(2,1)S(1)} %bitcast.9), channel_id=1, source_target_pairs={{64,0},{68,4},{72,8},{76,12},{80,16},{84,20},{88,24},{92,28},{96,3... | collective-permute-start | bytes 663560 | tf_op jit(solution)/shard_map/ppermute | solution.py:407
  70.4 6.0 %collective-permute-start.8 = (bf16[96,1152]{1,0:T(8,128)(2,1)S(1)}, bf16[96,1152]{1,0:T(8,128)(2,1)S(1)}, u32[]{:S(2)}, u32[]{:S(2)}) collective-permute-start(bf16[96,1152]{1,0:T(8,128)(2,1)S(1)} %bitcast.12), channel_id=1, source_target_pairs={{64,0},{68,4},{72,8},{76,12},{80,16},{84,20},{88,24},{92,28},{96,3... | collective-permute-start | bytes 663560 | tf_op jit(solution)/shard_map/ppermute | solution.py:407
  71.6 7.9 %collective-permute-start.13 = (bf16[96,1152]{1,0:T(8,128)(2,1)S(1)}, bf16[96,1152]{1,0:T(8,128)(2,1)S(1)}, u32[]{:S(2)}, u32[]{:S(2)}) collective-permute-start(bf16[96,1152]{1,0:T(8,128)(2,1)S(1)} %bitcast.10), channel_id=1, source_target_pairs={{0,64},{4,68},{8,72},{12,76},{16,80},{20,84},{24,88},{28,92},{32,9... | collective-permute-start | bytes 663560 | tf_op jit(solution)/shard_map/ppermute | solution.py:407
  73.5 10.4 %collective-permute-start.11 = (bf16[96,1152]{1,0:T(8,128)(2,1)S(1)}, bf16[96,1152]{1,0:T(8,128)(2,1)S(1)}, u32[]{:S(2)}, u32[]{:S(2)}) collective-permute-start(bf16[96,1152]{1,0:T(8,128)(2,1)S(1)} %collective-permute-done.10.rest_4_), channel_id=1, source_target_pairs={{0,64},{4,68},{8,72},{12,76},{16,80},{20,84},{24,88},{28,92},{32,9... | collective-permute-start | bytes 663560 | tf_op jit(solution)/shard_map/ppermute | solution.py:407
  73.6 10.3 %collective-permute-start.12 = (bf16[96,1152]{1,0:T(8,128)(2,1)S(1)}, bf16[96,1152]{1,0:T(8,128)(2,1)S(1)}, u32[]{:S(2)}, u32[]{:S(2)}) collective-permute-start(bf16[96,1152]{1,0:T(8,128)(2,1)S(1)} %collective-permute-done.9.rest_1_), channel_id=1, source_target_pairs={{64,0},{68,4},{72,8},{76,12},{80,16},{84,20},{88,24},{92,28},{96,3... | collective-permute-start | bytes 663560 | tf_op jit(solution)/shard_map/ppermute | solution.py:407
  84.1 10.6 %collective-permute-start.16 = (bf16[768,384]{1,0:T(8,128)(2,1)S(1)}, bf16[768,384]{1,0:T(8,128)(2,1)S(1)}, u32[]{:S(2)}, u32[]{:S(2)}) collective-permute-start(bf16[768,384]{1,0:T(8,128)(2,1)S(1)} %get-tuple-element.43.a_ref), channel_id=1, source_target_pairs={{0,4},{4,0},{8,12},{12,8},{16,20},{20,16},{24,28},{28,24},{32,36},... | collective-permute-start | bytes 1769480 | tf_op jit(solution)/shard_map/ppermute | solution.py:40
  94.1 6.0 %collective-permute-start.14 = (bf16[384,768]{1,0:T(8,128)(2,1)S(1)}, bf16[384,768]{1,0:T(8,128)(2,1)S(1)}, u32[]{:S(2)}, u32[]{:S(2)}) collective-permute-start(bf16[384,768]{1,0:T(8,128)(2,1)S(1)} %get-tuple-element.41.own_a), channel_id=1, source_target_pairs={{0,4},{4,0},{8,12},{12,8},{16,20},{20,16},{24,28},{28,24},{32,36},... | collective-permute-start | bytes 1769480 | tf_op jit(solution)/shard_map/ppermute | solution.py:40
  94.2 5.9 %collective-permute-start.15 = (bf16[384,768]{1,0:T(8,128)(2,1)S(1)}, bf16[384,768]{1,0:T(8,128)(2,1)S(1)}, u32[]{:S(2)}, u32[]{:S(2)}) collective-permute-start(bf16[384,768]{1,0:T(8,128)(2,1)S(1)} %get-tuple-element.42.own_b), channel_id=1, source_target_pairs={{0,4},{4,0},{8,12},{12,8},{16,20},{20,16},{24,28},{28,24},{32,36},... | collective-permute-start | bytes 1769480 | tf_op jit(solution)/shard_map/ppermute | solution.py:40
  102.8 7.4 %collective-permute-start.17 = (bf16[128,768]{1,0:T(8,128)(2,1)S(1)}, bf16[128,768]{1,0:T(8,128)(2,1)S(1)}, u32[]{:S(2)}, u32[]{:S(2)}) collective-permute-start(bf16[128,768]{1,0:T(8,128)(2,1)S(1)} %get-tuple-element.45), channel_id=1, source_target_pairs={{0,1},{1,2},{2,3},{3,0},{4,5},{5,6},{6,7},{7,4},{8,9},{9,10},{10,1... | collective-permute-start | bytes 589832 | tf_op jit(solution)/shard_map/ppermute | solution.py:407
  104.1 6.3 %collective-permute-start.19 = (bf16[128,768]{1,0:T(8,128)(2,1)S(1)}, bf16[128,768]{1,0:T(8,128)(2,1)S(1)}, u32[]{:S(2)}, u32[]{:S(2)}) collective-permute-start(bf16[128,768]{1,0:T(8,128)(2,1)S(1)} %get-tuple-element.47), channel_id=1, source_target_pairs={{0,3},{1,0},{2,1},{3,2},{4,7},{5,4},{6,5},{7,6},{8,11},{9,8},{10,9... | collective-permute-start | bytes 589832 | tf_op jit(solution)/shard_map/ppermute | solution.py:407
  105.6 8.6 %collective-permute-start.21 = (bf16[128,768]{1,0:T(8,128)(2,1)S(1)}, bf16[128,768]{1,0:T(8,128)(2,1)S(1)}, u32[]{:S(2)}, u32[]{:S(2)}) collective-permute-start(bf16[128,768]{1,0:T(8,128)(2,1)S(1)} %get-tuple-element.48), channel_id=1, source_target_pairs={{0,3},{1,0},{2,1},{3,2},{4,7},{5,4},{6,5},{7,6},{8,11},{9,8},{10,9... | collective-permute-start | bytes 589832 | tf_op jit(solution)/shard_map/ppermute | solution.py:407
  106.8 7.3 %collective-permute-start.22 = (bf16[128,768]{1,0:T(8,128)(2,1)S(1)}, bf16[128,768]{1,0:T(8,128)(2,1)S(1)}, u32[]{:S(2)}, u32[]{:S(2)}) collective-permute-start(bf16[128,768]{1,0:T(8,128)(2,1)S(1)} %get-tuple-element.49), channel_id=1, source_target_pairs={{0,1},{1,2},{2,3},{3,0},{4,5},{5,6},{6,7},{7,4},{8,9},{9,10},{10,1... | collective-permute-start | bytes 589832 | tf_op jit(solution)/shard_map/ppermute | solution.py:407
  110.3 8.2 %collective-permute-start.18 = (bf16[128,768]{1,0:T(8,128)(2,1)S(1)}, bf16[128,768]{1,0:T(8,128)(2,1)S(1)}, u32[]{:S(2)}, u32[]{:S(2)}) collective-permute-start(bf16[128,768]{1,0:T(8,128)(2,1)S(1)} %add_convert_fusion.4), channel_id=1, source_target_pairs={{0,1},{1,2},{2,3},{3,0},{4,5},{5,6},{6,7},{7,4},{8,9},{9,10},{10,1... | collective-permute-start | bytes 589832 | tf_op jit(solution)/shard_map/ppermute | solution.py:407
  110.5 8.0 %collective-permute-start.20 = (bf16[128,768]{1,0:T(8,128)(2,1)S(1)}, bf16[128,768]{1,0:T(8,128)(2,1)S(1)}, u32[]{:S(2)}, u32[]{:S(2)}) collective-permute-start(bf16[128,768]{1,0:T(8,128)(2,1)S(1)} %add_convert_fusion.3), channel_id=1, source_target_pairs={{0,3},{1,0},{2,1},{3,2},{4,7},{5,4},{6,5},{7,6},{8,11},{9,8},{10,9... | collective-permute-start | bytes 589832 | tf_op jit(solution)/shard_map/ppermute | solution.py:407
  (5 other events, 30.2 us)

commit v6 on v5

--- a/solution.py
+++ b/solution.py
@@ -64,6 +64,10 @@
 
 def dot_tn(left, right):
     return lax.dot_general(left, right, (((0,), (0,)), ((), ())), preferred_element_type=f32)
+
+
+def sigmoid(x):
+    return 0.5 + 0.5 * jnp.tanh(0.5 * x)
 
 
 def call(body, outs, in_specs, scratch, mib, flops, moved, name, out_specs=None):
@@ -97,16 +101,10 @@
     tokens, width = keys.shape
     half = width // 2
     lanes = rates.shape[1]
-
-    def body(r_ref, k_hbm, v_hbm, w_hbm, *rest):
-        outs, refs = rest[:3], rest[3:6]
-        k_ref, v_ref, w_ref, errors, g_send, sems, out_sems = rest[6:]
-        own_send, shared_send, factors = refs
-        g_keep, hidden = factors.at[:, :width], factors.at[:, width : 2 * width]
-        stores = [
-            pltpu.make_async_copy(ref, out, out_sems.at[n])
-            for n, (ref, out) in enumerate(zip(refs, outs))
-        ]
+    parts = tokens // ROWS
+
+    def body(r_ref, k_hbm, v_hbm, w_hbm, own_out, shared_out, factors_out,
+             k_ref, v_ref, w_ref, errors, hidden, grads, own_send, shared_send, sems, out_sems):
         moves = [
             (k_hbm, k_ref),
             (w_hbm.at[0, 0], w_ref.at[0]),
@@ -119,7 +117,16 @@
         ]
         for copy in copies:
             copy.start()
-        first = own_core() == 0
+        stores = []
+
+        def store(src, dst):
+            copy = pltpu.make_async_copy(src, dst, out_sems.at[len(stores)])
+            copy.start()
+            stores.append(copy)
+
+        core = own_core()
+        kept = pl.ds(pl.multiple_of(core * half, half), half)
+        sent = pl.ds(pl.multiple_of((1 - core) * half, half), half)
         rate_columns = r_ref[...].T
         copies[0].wait()
         copies[1].wait()
@@ -130,43 +137,41 @@
             if row == 0:
                 copies[2].wait()
             h3 = dot(k, w_ref[1])
-            sig = jax.nn.sigmoid(h1)
+            sig = sigmoid(h1)
             act = h1 * sig
             hidden[rows, :] = (act * h3).astype(bf16)
+            store(hidden.at[rows, :], factors_out.at[rows, width : 2 * width])
             if row == 0:
                 copies[3].wait()
             for part in range(row, row + ROWS, lanes):
                 rate = rate_columns[:, part // lanes : part // lanes + 1]
                 span = slice(part, part + lanes)
                 errors[span, :] = (-rate * v_ref[span, :].astype(f32)).astype(bf16)
+            store(errors.at[rows, kept], factors_out.at[rows, 2 * width :])
             if row == 0:
                 copies[4].wait()
             dz = dot_nt(errors[rows, :], w_ref[2])
-            g1 = (dz * h3 * (sig * (1.0 + h1 * (1.0 - sig)))).astype(bf16)
-            g3 = (dz * act).astype(bf16)
-            g_keep[rows, :] = jnp.where(first, g1, g3)
-            g_send[rows, :] = jnp.where(first, g3, g1)
-        left = errors[:, :half]
-        right = errors[:, half:]
-        factors[:, 2 * width :] = jnp.where(first, left, right)
-        stores[2].start()
-        own_send[...] = dot_tn(k_ref[...], g_send[...]).astype(bf16)
-        stores[0].start()
-        shared_send[...] = dot_tn(hidden[...], jnp.where(first, right, left)).astype(bf16)
-        stores[1].start()
-        for store in stores:
-            store.wait()
+            slope = sig + act * (1.0 - sig)
+            grads[core, rows, :] = (dz * h3 * slope).astype(bf16)
+            grads[1 - core, rows, :] = (dz * act).astype(bf16)
+            store(grads.at[0, rows, :], factors_out.at[rows, :width])
+        own_send[...] = dot_tn(k_ref[...], grads[1]).astype(bf16)
+        store(own_send, own_out)
+        shared_send[...] = dot_tn(hidden[...], errors[:, sent]).astype(bf16)
+        store(shared_send, shared_out)
+        for copy in stores:
+            copy.wait()
 
     results = [(width, width), (width, half), (tokens, 2 * width + half)]
+    wide = pltpu.VMEM((tokens, width), bf16)
     return call(
         body,
         [shape(*dims) for dims in results],
         [VMEM] + [HBM] * 3,
-        [pltpu.VMEM(dims, bf16) for dims in results]
-        + [pltpu.VMEM((tokens, width), bf16)] * 2
-        + [pltpu.VMEM((3, width, width), bf16)]
-        + [pltpu.VMEM((tokens, width), bf16)] * 2
-        + [pltpu.SemaphoreType.DMA((5,)), pltpu.SemaphoreType.DMA((3,))],
+        [wide, wide, pltpu.VMEM((3, width, width), bf16), wide, wide]
+        + [pltpu.VMEM((2, tokens, width), bf16)]
+        + [pltpu.VMEM(dims, bf16) for dims in results[:2]]
+        + [pltpu.SemaphoreType.DMA((5,)), pltpu.SemaphoreType.DMA((3 * parts + 2,))],
         60,
         9 * tokens * width * width,
         12 * width * width,
@@ -258,7 +263,7 @@
     )(*pieces)
 
 
-def newton_schulz(x_ref, w_ref, w_copy, outs, gram, poly, other):
+def newton_schulz(x_ref, w_ref, outs, gram, poly, other):
     width = x_ref.shape[0]
     blocks = [slice(row, row + ROWS) for row in range(0, width, ROWS)]
 
@@ -284,8 +289,6 @@
             squared = dot(gram[rows, :], gram[:, : rows.stop])
             linear = gram[rows, : rows.stop].astype(f32)
             store(poly, n, (ns_b * linear + ns_c * squared).astype(bf16))
-        if turn == NS_ITERS - 1:
-            w_copy.wait()
         for rows in blocks:
             new = ns_a * now[rows, :].astype(f32) + dot(poly[rows, :], now[...])
             if turn == 0:
@@ -308,17 +311,15 @@
 def own_step(summed, weights):
     width = weights.shape[-1]
 
-    def body(x_ref, w_hbm, top, bottom, gram, poly, other, w_ref, sem):
-        copy = pltpu.make_async_copy(w_hbm.at[0, own_core()], w_ref, sem)
-        copy.start()
-        newton_schulz(x_ref, w_ref, copy, (top, bottom), gram, poly, other)
+    def body(x_ref, w_ref, top, bottom, gram, poly, other):
+        newton_schulz(x_ref, w_ref.at[0, own_core()], (top, bottom), gram, poly, other)
 
     return call(
         body,
         [shape(width // 2, width)] * 2,
-        [VMEM, HBM],
-        [pltpu.VMEM((width, width), bf16)] * 4 + [pltpu.SemaphoreType.DMA],
-        20,
+        [VMEM] * 2,
+        [pltpu.VMEM((width, width), bf16)] * 3,
+        16,
         10 * width**3,
         6 * width * width,
         "own_step",
@@ -329,20 +330,18 @@
     width = weights.shape[-1]
     half = width // 2
 
-    def body(a_ref, b_ref, w_hbm, out_ref, gram, poly, other, x_ref, w_ref, sem):
-        copy = pltpu.make_async_copy(w_hbm.at[0, 2], w_ref, sem)
-        copy.start()
+    def body(a_ref, b_ref, w_ref, out_ref, gram, poly, other, x_ref):
         first = own_core() == 0
         x_ref[:, :half] = jnp.where(first, a_ref[...], b_ref[...])
         x_ref[:, half:] = jnp.where(first, b_ref[...], a_ref[...])
-        newton_schulz(x_ref, w_ref, copy, (out_ref,), gram, poly, other)
+        newton_schulz(x_ref, w_ref.at[0, 2], (out_ref,), gram, poly, other)
 
     return call(
         body,
         shape(width, width),
-        [VMEM, VMEM, HBM],
-        [pltpu.VMEM((width, width), bf16)] * 5 + [pltpu.SemaphoreType.DMA],
-        20,
+        [VMEM] * 3,
+        [pltpu.VMEM((width, width), bf16)] * 4,
+        16,
         10 * width**3,
         6 * width * width,
         "shared_step",
@@ -362,7 +361,7 @@
         q_other = dot(left, other_a[...]) + dot(right, other_b[...])
         q1 = jnp.where(first, q_own, q_other)
         q3 = jnp.where(first, q_other, q_own)
-        gated = (q1 * jax.nn.sigmoid(q1) * q3).astype(bf16)
+        gated = (q1 * sigmoid(q1) * q3).astype(bf16)
         outputs = dot(gated, shared_ref[...]).astype(bf16)
         cut = tokens // 2
         for step in range(heads):

time: 120 us -> 118 us (0.983)
  Pallas kernels: 23.5 us -> 21.9 us
    pallas_call x3, Pallas kernels: 18.2 us -> 16.6 us  [the longest x1 7.04 us: gradients(): call(body, [shape(*dims) for dims in results], [VMEM] + [HBM] * 3, [wide,...]
  transfers between devices with their start and end apart: 23 -> 23, of which waited for: 11 -> 11; matrix products, arithmetic and copies ran while one was open for 0% -> 0% of each run, Pallas kernels for 10% -> 9%
where the time goes in v6:
time: 118 us
  blocking collectives  35.3 us (30%)
  starting transfers between devices  30 us (25%)
  waiting for transfers between devices  28.4 us (24%)
  Pallas kernels  21.9 us (19%)
  local copies, waits for them, and re-layouts  1.64 us (1%)
    all_to_all x2, blocking collectives, exchange(): return lax.all_to_all(blocks, 'tok', 0, 0, axis_index_groups=groups)  35.3 us
    ppermute x18, waiting for transfers between devices, shift(): return lax.ppermute(array, axis, pairs)  27.7 us
    ppermute x18, starting transfers between devices, shift(): return lax.ppermute(array, axis, pairs)  21.3 us
    ppermute x5, starting transfers between devices, swap_cores(): return lax.ppermute(array, 'tok', CORE_SWAP)  8.7 us
    pallas_call x1, Pallas kernels, gradients(): call(body, [shape(*dims) for dims in results], [VMEM] + [HBM] * 3, [wide,...  7.04 us
    pallas_call x1, Pallas kernels, shared_step(): call(body, shape(width, width), [VMEM] * 3, [pltpu.VMEM((width, width), b...  4.79 us
    pallas_call x1, Pallas kernels, own_step(): call(body, [shape(width // 2, width)] * 2, [VMEM] * 2, [pltpu.VMEM((width...  4.78 us
    pallas_call x1, Pallas kernels, project(): call(body, [shape(tokens, width, dtype=f32)] + [shape(tokens // 2, width)...  2.69 us
  transfers between devices with their start and end apart: 23, of which 11 were waited for; matrix products, arithmetic and copies ran while one was open for 0% of the time, Pallas kernels for 9%

profile of v6, /device:TPU:1, one launch (start us, length us, event | category | flops | bytes accessed | tf_op | source)
XLA Modules:
  0.0 117.9 jit_solution(14716437361909588994)
XLA Ops:
  0.0 7.0 %gradients.1 = (bf16[768,768]{1,0:T(8,128)(2,1)}, bf16[768,384]{1,0:T(8,128)(2,1)}, bf16[512,1920]{1,0:T(8,128)(2,1)}) custom-call(f32[4,128]{1,0:T(4,128)} %bitcast.13, bf16[512,768]{1,0:T(8,128)(2,1)} %k_ref.1, bf16[512,768]{1,0:T(8,128)(2,1)} %v_hbm.1, bf16[1,3,768,768]{3,2,1,0:T(8,128)(2,1)} %w_ref.3), custom_call_target="tpu_custom_call" | custom-call | flops 2717908992 | bytes 7077888 | tf_op jit(solution)/shard_map/gradients/pallas_call | solution.py:167
  7.0 3.3 %collective-permute-start = (bf16[768,768]{1,0:T(8,128)(2,1)}, bf16[768,768]{1,0:T(8,128)(2,1)S(1)}, u32[]{:S(2)}, u32[]{:S(2)}) collective-permute-start(bf16[768,768]{1,0:T(8,128)(2,1)} %get-tuple-element.30), channel_id=1, source_target_pairs={{0,4},{4,0},{8,12},{12,8},{16,20},{20,16},{24,28},{28,24},{32,36},... | collective-permute-start | bytes 3538952 | tf_op jit(solution)/shard_map/ppermute | solution.py:40
  10.5 1.5 %copy-done.3 = bf16[512,1920]{1,0:T(8,128)(2,1)S(1)} copy-done((bf16[512,1920]{1,0:T(8,128)(2,1)S(1)}, bf16[512,1920]{1,0:T(8,128)(2,1)}, u32[]{:S(2)}) %copy-start.3) | copy-done | bytes 1966104
  14.3 2.7 %collective-permute-start.4 = (bf16[96,1152]{1,0:T(8,128)(2,1)S(1)}, bf16[96,1152]{1,0:T(8,128)(2,1)S(1)}, u32[]{:S(2)}, u32[]{:S(2)}) collective-permute-start(bf16[96,1152]{1,0:T(8,128)(2,1)S(1)} %get-tuple-element.36), channel_id=1, source_target_pairs={{64,0},{68,4},{72,8},{76,12},{80,16},{84,20},{88,24},{92,28},{96,3... | collective-permute-start | bytes 663560 | tf_op jit(solution)/shard_map/ppermute | solution.py:406
  17.0 1.4 %collective-permute-start.7 = (bf16[96,1152]{1,0:T(8,128)(2,1)S(1)}, bf16[96,1152]{1,0:T(8,128)(2,1)S(1)}, u32[]{:S(2)}, u32[]{:S(2)}) collective-permute-start(bf16[96,1152]{1,0:T(8,128)(2,1)S(1)} %get-tuple-element.38), channel_id=1, source_target_pairs={{0,64},{4,68},{8,72},{12,76},{16,80},{20,84},{24,88},{28,92},{32,9... | collective-permute-start | bytes 663560 | tf_op jit(solution)/shard_map/ppermute | solution.py:406
  18.4 3.7 %collective-permute-done.2 = bf16[96,1152]{1,0:T(8,128)(2,1)S(1)} collective-permute-done((bf16[96,1152]{1,0:T(8,128)(2,1)S(1)}, bf16[96,1152]{1,0:T(8,128)(2,1)S(1)}, u32[]{:S(2)}, u32[]{:S(2)}) %collective-permute-start.2) | collective-permute-done | bytes 221216 | tf_op jit(solution)/shard_map/ppermute | solution.py:406
  22.4 2.7 %collective-permute-start.5 = (bf16[96,1152]{1,0:T(8,128)(2,1)S(1)}, bf16[96,1152]{1,0:T(8,128)(2,1)S(1)}, u32[]{:S(2)}, u32[]{:S(2)}) collective-permute-start(bf16[96,1152]{1,0:T(8,128)(2,1)S(1)} %add_convert_fusion.1), channel_id=1, source_target_pairs={{64,0},{68,4},{72,8},{76,12},{80,16},{84,20},{88,24},{92,28},{96,3... | collective-permute-start | bytes 663560 | tf_op jit(solution)/shard_map/ppermute | solution.py:406
  26.9 4.5 %collective-permute-done.3 = bf16[96,1152]{1,0:T(8,128)(2,1)S(1)} collective-permute-done((bf16[96,1152]{1,0:T(8,128)(2,1)S(1)}, bf16[96,1152]{1,0:T(8,128)(2,1)S(1)}, u32[]{:S(2)}, u32[]{:S(2)}) %collective-permute-start.3) | collective-permute-done | bytes 221216 | tf_op jit(solution)/shard_map/ppermute | solution.py:406
  31.5 19.8 %all_to_all.10 = bf16[8,24,1152]{2,1,0:T(8,128)(2,1)S(1)} all-to-all(bf16[8,24,1152]{2,1,0:T(8,128)(2,1)S(1)} %bitcast.8), channel_id=1, replica_groups={{0,8,16,24,32,40,48,56},{4,12,20,28,36,44,52,60},{64,72,80,88,96,104,11..., dimensions={0} | all-to-all | bytes 884736 | tf_op jit(solution)/shard_map/all_to_all | solution.py:44
  51.4 15.5 %all_to_all.11 = bf16[8,24,1152]{2,1,0:T(8,128)(2,1)S(1)} all-to-all(bf16[8,24,1152]{2,1,0:T(8,128)(2,1)S(1)} %broadcast_in_dim.2), channel_id=1, replica_groups={{0,8,16,24,32,40,48,56},{4,12,20,28,36,44,52,60},{64,72,80,88,96,104,11..., dimensions={0} | all-to-all | bytes 884736 | tf_op jit(solution)/shard_map/all_to_all | solution.py:44
  67.0 1.4 %collective-permute-start.10 = (bf16[96,1152]{1,0:T(8,128)(2,1)S(1)}, bf16[96,1152]{1,0:T(8,128)(2,1)S(1)}, u32[]{:S(2)}, u32[]{:S(2)}) collective-permute-start(bf16[96,1152]{1,0:T(8,128)(2,1)S(1)} %bitcast.11), channel_id=1, source_target_pairs={{0,64},{4,68},{8,72},{12,76},{16,80},{20,84},{24,88},{28,92},{32,9... | collective-permute-start | bytes 663560 | tf_op jit(solution)/shard_map/ppermute | solution.py:406
  68.4 1.6 %collective-permute-start.9 = (bf16[96,1152]{1,0:T(8,128)(2,1)S(1)}, bf16[96,1152]{1,0:T(8,128)(2,1)S(1)}, u32[]{:S(2)}, u32[]{:S(2)}) collective-permute-start(bf16[96,1152]{1,0:T(8,128)(2,1)S(1)} %bitcast.9), channel_id=1, source_target_pairs={{64,0},{68,4},{72,8},{76,12},{80,16},{84,20},{88,24},{92,28},{96,3... | collective-permute-start | bytes 663560 | tf_op jit(solution)/shard_map/ppermute | solution.py:406
  71.4 1.7 %collective-permute-done.10.rest_4_ = bf16[96,1152]{1,0:T(8,128)(2,1)S(1)} collective-permute-done((bf16[96,1152]{1,0:T(8,128)(2,1)S(1)}, bf16[96,1152]{1,0:T(8,128)(2,1)S(1)}, u32[]{:S(2)}, u32[]{:S(2)}) %collective-permute-start.10) | collective-permute-done | bytes 221216 | tf_op jit(solution)/shard_map/ppermute | solution.py:406
  73.2 2.8 %collective-permute-start.12 = (bf16[96,1152]{1,0:T(8,128)(2,1)S(1)}, bf16[96,1152]{1,0:T(8,128)(2,1)S(1)}, u32[]{:S(2)}, u32[]{:S(2)}) collective-permute-start(bf16[96,1152]{1,0:T(8,128)(2,1)S(1)} %collective-permute-done.9.rest_1_), channel_id=1, source_target_pairs={{64,0},{68,4},{72,8},{76,12},{80,16},{84,20},{88,24},{92,28},{96,3... | collective-permute-start | bytes 663560 | tf_op jit(solution)/shard_map/ppermute | solution.py:406
  76.0 3.1 %collective-permute-done.13.rest_5_ = bf16[96,1152]{1,0:T(8,128)(2,1)S(1)} collective-permute-done((bf16[96,1152]{1,0:T(8,128)(2,1)S(1)}, bf16[96,1152]{1,0:T(8,128)(2,1)S(1)}, u32[]{:S(2)}, u32[]{:S(2)}) %collective-permute-start.13) | collective-permute-done | bytes 221216 | tf_op jit(solution)/shard_map/ppermute | solution.py:406
  79.0 4.4 %collective-permute-done.11.rest_2_ = bf16[96,1152]{1,0:T(8,128)(2,1)S(1)} collective-permute-done((bf16[96,1152]{1,0:T(8,128)(2,1)S(1)}, bf16[96,1152]{1,0:T(8,128)(2,1)S(1)}, u32[]{:S(2)}, u32[]{:S(2)}) %collective-permute-start.11) | collective-permute-done | bytes 221216 | tf_op jit(solution)/shard_map/ppermute | solution.py:406
  83.6 4.7 %collective-permute-start.16 = (bf16[768,384]{1,0:T(8,128)(2,1)S(1)}, bf16[768,384]{1,0:T(8,128)(2,1)S(1)}, u32[]{:S(2)}, u32[]{:S(2)}) collective-permute-start(bf16[768,384]{1,0:T(8,128)(2,1)S(1)} %get-tuple-element.43.a_ref), channel_id=1, source_target_pairs={{0,4},{4,0},{8,12},{12,8},{16,20},{20,16},{24,28},{28,24},{32,36},... | collective-permute-start | bytes 1769480 | tf_op jit(solution)/shard_map/ppermute | solution.py:40
  88.3 4.8 %own_step.1 = (bf16[384,768]{1,0:T(8,128)(2,1)S(1)}, bf16[384,768]{1,0:T(8,128)(2,1)S(1)}) custom-call(bf16[768,768]{1,0:T(8,128)(2,1)S(1)} %get-tuple-element.40.x_ref, bf16[1,3,768,768]{3,2,1,0:T(8,128)(2,1)S(1)} %copy-done.1), custom_call_target="tpu_custom_call" | custom-call | flops 4529848320 | bytes 3538944 | tf_op jit(solution)/shard_map/own_step/pallas_call | solution.py:317
  93.7 4.8 %shared_step.1.shared_ref = bf16[768,768]{1,0:T(8,128)(2,1)S(1)} custom-call(bf16[768,384]{1,0:T(8,128)(2,1)S(1)} %get-tuple-element.43.a_ref, bf16[768,384]{1,0:T(8,128)(2,1)S(1)} %collective-permute-done.16.b_ref, bf16[1,3,768,768]{3,2,1,0:T(8,128)(2,1)S(1)} %copy-done.1), custom_call_target="tpu_custom_call" | custom-call | flops 4529848320 | bytes 3538944 | tf_op jit(solution)/shard_map/shared_step/pallas_call | solution.py:339
  98.6 2.7 %project.1 = (f32[256,768]{1,0:T(8,128)S(1)}, bf16[128,768]{1,0:T(8,128)(2,1)S(1)}, bf16[128,768]{1,0:T(8,128)(2,1)S(1)}, bf16[128,768]{1,0:T(8,128)(2,1)S(1)}, ...) custom-call(bf16[256,768]{1,0:T(8,128)(2,1)S(1)} %copy-done, ...), custom_call_target="tpu_custom_call" | custom-call | flops 2113929216 | bytes 9437184 | tf_op jit(solution)/shard_map/project/pallas_call | solution.py:377
  102.6 1.5 %collective-permute-start.19 = (bf16[128,768]{1,0:T(8,128)(2,1)S(1)}, bf16[128,768]{1,0:T(8,128)(2,1)S(1)}, u32[]{:S(2)}, u32[]{:S(2)}) collective-permute-start(bf16[128,768]{1,0:T(8,128)(2,1)S(1)} %get-tuple-element.47), channel_id=1, source_target_pairs={{0,3},{1,0},{2,1},{3,2},{4,7},{5,4},{6,5},{7,6},{8,11},{9,8},{10,9... | collective-permute-start | bytes 589832 | tf_op jit(solution)/shard_map/ppermute | solution.py:406
  105.5 3.2 %collective-permute-done.17 = bf16[128,768]{1,0:T(8,128)(2,1)S(1)} collective-permute-done((bf16[128,768]{1,0:T(8,128)(2,1)S(1)}, bf16[128,768]{1,0:T(8,128)(2,1)S(1)}, u32[]{:S(2)}, u32[]{:S(2)}) %collective-permute-start.17) | collective-permute-done | bytes 196640 | tf_op jit(solution)/shard_map/ppermute | solution.py:406
  108.9 2.7 %collective-permute-start.20 = (bf16[128,768]{1,0:T(8,128)(2,1)S(1)}, bf16[128,768]{1,0:T(8,128)(2,1)S(1)}, u32[]{:S(2)}, u32[]{:S(2)}) collective-permute-start(bf16[128,768]{1,0:T(8,128)(2,1)S(1)} %add_convert_fusion.3), channel_id=1, source_target_pairs={{0,3},{1,0},{2,1},{3,2},{4,7},{5,4},{6,5},{7,6},{8,11},{9,8},{10,9... | collective-permute-start | bytes 589832 | tf_op jit(solution)/shard_map/ppermute | solution.py:406
  112.6 4.4 %collective-permute-done.18.sum_a_ref = bf16[128,768]{1,0:T(8,128)(2,1)S(1)} collective-permute-done((bf16[128,768]{1,0:T(8,128)(2,1)S(1)}, bf16[128,768]{1,0:T(8,128)(2,1)S(1)}, u32[]{:S(2)}, u32[]{:S(2)}) %collective-permute-start.18) | collective-permute-done | bytes 196640 | tf_op jit(solution)/shard_map/ppermute | solution.py:406
  (53 shorter events, 11.8 us)
Async XLA Ops:
  7.0 6.9 %collective-permute-start = (bf16[768,768]{1,0:T(8,128)(2,1)}, bf16[768,768]{1,0:T(8,128)(2,1)S(1)}, u32[]{:S(2)}, u32[]{:S(2)}) collective-permute-start(bf16[768,768]{1,0:T(8,128)(2,1)} %get-tuple-element.30), channel_id=1, source_target_pairs={{0,4},{4,0},{8,12},{12,8},{16,20},{20,16},{24,28},{28,24},{32,36},... | collective-permute-start | bytes 3538952 | tf_op jit(solution)/shard_map/ppermute | solution.py:40
  10.4 3.5 %collective-permute-start.1 = (bf16[768,384]{1,0:T(8,128)(2,1)}, bf16[768,384]{1,0:T(8,128)(2,1)S(1)}, u32[]{:S(2)}, u32[]{:S(2)}) collective-permute-start(bf16[768,384]{1,0:T(8,128)(2,1)} %get-tuple-element.32), channel_id=1, source_target_pairs={{0,4},{4,0},{8,12},{12,8},{16,20},{20,16},{24,28},{28,24},{32,36},... | collective-permute-start | bytes 1769480 | tf_op jit(solution)/shard_map/ppermute | solution.py:40
  14.2 7.9 %collective-permute-start.2 = (bf16[96,1152]{1,0:T(8,128)(2,1)S(1)}, bf16[96,1152]{1,0:T(8,128)(2,1)S(1)}, u32[]{:S(2)}, u32[]{:S(2)}) collective-permute-start(bf16[96,1152]{1,0:T(8,128)(2,1)S(1)} %get-tuple-element.34), channel_id=1, source_target_pairs={{0,64},{4,68},{8,72},{12,76},{16,80},{20,84},{24,88},{28,92},{32,9... | collective-permute-start | bytes 663560 | tf_op jit(solution)/shard_map/ppermute | solution.py:406
  14.3 8.0 %collective-permute-start.4 = (bf16[96,1152]{1,0:T(8,128)(2,1)S(1)}, bf16[96,1152]{1,0:T(8,128)(2,1)S(1)}, u32[]{:S(2)}, u32[]{:S(2)}) collective-permute-start(bf16[96,1152]{1,0:T(8,128)(2,1)S(1)} %get-tuple-element.36), channel_id=1, source_target_pairs={{64,0},{68,4},{72,8},{76,12},{80,16},{84,20},{88,24},{92,28},{96,3... | collective-permute-start | bytes 663560 | tf_op jit(solution)/shard_map/ppermute | solution.py:406
  17.0 8.9 %collective-permute-start.6 = (bf16[96,1152]{1,0:T(8,128)(2,1)S(1)}, bf16[96,1152]{1,0:T(8,128)(2,1)S(1)}, u32[]{:S(2)}, u32[]{:S(2)}) collective-permute-start(bf16[96,1152]{1,0:T(8,128)(2,1)S(1)} %get-tuple-element.37), channel_id=1, source_target_pairs={{64,0},{68,4},{72,8},{76,12},{80,16},{84,20},{88,24},{92,28},{96,3... | collective-permute-start | bytes 663560 | tf_op jit(solution)/shard_map/ppermute | solution.py:406
  17.0 9.9 %collective-permute-start.7 = (bf16[96,1152]{1,0:T(8,128)(2,1)S(1)}, bf16[96,1152]{1,0:T(8,128)(2,1)S(1)}, u32[]{:S(2)}, u32[]{:S(2)}) collective-permute-start(bf16[96,1152]{1,0:T(8,128)(2,1)S(1)} %get-tuple-element.38), channel_id=1, source_target_pairs={{0,64},{4,68},{8,72},{12,76},{16,80},{20,84},{24,88},{28,92},{32,9... | collective-permute-start | bytes 663560 | tf_op jit(solution)/shard_map/ppermute | solution.py:406
  22.2 9.2 %collective-permute-start.3 = (bf16[96,1152]{1,0:T(8,128)(2,1)S(1)}, bf16[96,1152]{1,0:T(8,128)(2,1)S(1)}, u32[]{:S(2)}, u32[]{:S(2)}) collective-permute-start(bf16[96,1152]{1,0:T(8,128)(2,1)S(1)} %add_convert_fusion.2), channel_id=1, source_target_pairs={{0,64},{4,68},{8,72},{12,76},{16,80},{20,84},{24,88},{28,92},{32,9... | collective-permute-start | bytes 663560 | tf_op jit(solution)/shard_map/ppermute | solution.py:406
  22.4 9.0 %collective-permute-start.5 = (bf16[96,1152]{1,0:T(8,128)(2,1)S(1)}, bf16[96,1152]{1,0:T(8,128)(2,1)S(1)}, u32[]{:S(2)}, u32[]{:S(2)}) collective-permute-start(bf16[96,1152]{1,0:T(8,128)(2,1)S(1)} %add_convert_fusion.1), channel_id=1, source_target_pairs={{64,0},{68,4},{72,8},{76,12},{80,16},{84,20},{88,24},{92,28},{96,3... | collective-permute-start | bytes 663560 | tf_op jit(solution)/shard_map/ppermute | solution.py:406
  51.4 36.9 %copy-start.1 = (bf16[1,3,768,768]{3,2,1,0:T(8,128)(2,1)S(1)}, bf16[1,3,768,768]{3,2,1,0:T(8,128)(2,1)}, u32[]{:S(2)}) copy-start(bf16[1,3,768,768]{3,2,1,0:T(8,128)(2,1)} %w_ref.3) | copy-start | bytes 10616836
  67.0 6.1 %collective-permute-start.10 = (bf16[96,1152]{1,0:T(8,128)(2,1)S(1)}, bf16[96,1152]{1,0:T(8,128)(2,1)S(1)}, u32[]{:S(2)}, u32[]{:S(2)}) collective-permute-start(bf16[96,1152]{1,0:T(8,128)(2,1)S(1)} %bitcast.11), channel_id=1, source_target_pairs={{0,64},{4,68},{8,72},{12,76},{16,80},{20,84},{24,88},{28,92},{32,9... | collective-permute-start | bytes 663560 | tf_op jit(solution)/shard_map/ppermute | solution.py:406
  68.4 4.8 %collective-permute-start.9 = (bf16[96,1152]{1,0:T(8,128)(2,1)S(1)}, bf16[96,1152]{1,0:T(8,128)(2,1)S(1)}, u32[]{:S(2)}, u32[]{:S(2)}) collective-permute-start(bf16[96,1152]{1,0:T(8,128)(2,1)S(1)} %bitcast.9), channel_id=1, source_target_pairs={{64,0},{68,4},{72,8},{76,12},{80,16},{84,20},{88,24},{92,28},{96,3... | collective-permute-start | bytes 663560 | tf_op jit(solution)/shard_map/ppermute | solution.py:406
  70.0 6.0 %collective-permute-start.8 = (bf16[96,1152]{1,0:T(8,128)(2,1)S(1)}, bf16[96,1152]{1,0:T(8,128)(2,1)S(1)}, u32[]{:S(2)}, u32[]{:S(2)}) collective-permute-start(bf16[96,1152]{1,0:T(8,128)(2,1)S(1)} %bitcast.12), channel_id=1, source_target_pairs={{64,0},{68,4},{72,8},{76,12},{80,16},{84,20},{88,24},{92,28},{96,3... | collective-permute-start | bytes 663560 | tf_op jit(solution)/shard_map/ppermute | solution.py:406
  71.1 7.9 %collective-permute-start.13 = (bf16[96,1152]{1,0:T(8,128)(2,1)S(1)}, bf16[96,1152]{1,0:T(8,128)(2,1)S(1)}, u32[]{:S(2)}, u32[]{:S(2)}) collective-permute-start(bf16[96,1152]{1,0:T(8,128)(2,1)S(1)} %bitcast.10), channel_id=1, source_target_pairs={{0,64},{4,68},{8,72},{12,76},{16,80},{20,84},{24,88},{28,92},{32,9... | collective-permute-start | bytes 663560 | tf_op jit(solution)/shard_map/ppermute | solution.py:406
  73.1 10.4 %collective-permute-start.11 = (bf16[96,1152]{1,0:T(8,128)(2,1)S(1)}, bf16[96,1152]{1,0:T(8,128)(2,1)S(1)}, u32[]{:S(2)}, u32[]{:S(2)}) collective-permute-start(bf16[96,1152]{1,0:T(8,128)(2,1)S(1)} %collective-permute-done.10.rest_4_), channel_id=1, source_target_pairs={{0,64},{4,68},{8,72},{12,76},{16,80},{20,84},{24,88},{28,92},{32,9... | collective-permute-start | bytes 663560 | tf_op jit(solution)/shard_map/ppermute | solution.py:406
  73.2 10.3 %collective-permute-start.12 = (bf16[96,1152]{1,0:T(8,128)(2,1)S(1)}, bf16[96,1152]{1,0:T(8,128)(2,1)S(1)}, u32[]{:S(2)}, u32[]{:S(2)}) collective-permute-start(bf16[96,1152]{1,0:T(8,128)(2,1)S(1)} %collective-permute-done.9.rest_1_), channel_id=1, source_target_pairs={{64,0},{68,4},{72,8},{76,12},{80,16},{84,20},{88,24},{92,28},{96,3... | collective-permute-start | bytes 663560 | tf_op jit(solution)/shard_map/ppermute | solution.py:406
  83.6 10.1 %collective-permute-start.16 = (bf16[768,384]{1,0:T(8,128)(2,1)S(1)}, bf16[768,384]{1,0:T(8,128)(2,1)S(1)}, u32[]{:S(2)}, u32[]{:S(2)}) collective-permute-start(bf16[768,384]{1,0:T(8,128)(2,1)S(1)} %get-tuple-element.43.a_ref), channel_id=1, source_target_pairs={{0,4},{4,0},{8,12},{12,8},{16,20},{20,16},{24,28},{28,24},{32,36},... | collective-permute-start | bytes 1769480 | tf_op jit(solution)/shard_map/ppermute | solution.py:40
  93.1 5.4 %collective-permute-start.14 = (bf16[384,768]{1,0:T(8,128)(2,1)S(1)}, bf16[384,768]{1,0:T(8,128)(2,1)S(1)}, u32[]{:S(2)}, u32[]{:S(2)}) collective-permute-start(bf16[384,768]{1,0:T(8,128)(2,1)S(1)} %get-tuple-element.41.own_a), channel_id=1, source_target_pairs={{0,4},{4,0},{8,12},{12,8},{16,20},{20,16},{24,28},{28,24},{32,36},... | collective-permute-start | bytes 1769480 | tf_op jit(solution)/shard_map/ppermute | solution.py:40
  93.3 5.3 %collective-permute-start.15 = (bf16[384,768]{1,0:T(8,128)(2,1)S(1)}, bf16[384,768]{1,0:T(8,128)(2,1)S(1)}, u32[]{:S(2)}, u32[]{:S(2)}) collective-permute-start(bf16[384,768]{1,0:T(8,128)(2,1)S(1)} %get-tuple-element.42.own_b), channel_id=1, source_target_pairs={{0,4},{4,0},{8,12},{12,8},{16,20},{20,16},{24,28},{28,24},{32,36},... | collective-permute-start | bytes 1769480 | tf_op jit(solution)/shard_map/ppermute | solution.py:40
  101.3 7.4 %collective-permute-start.17 = (bf16[128,768]{1,0:T(8,128)(2,1)S(1)}, bf16[128,768]{1,0:T(8,128)(2,1)S(1)}, u32[]{:S(2)}, u32[]{:S(2)}) collective-permute-start(bf16[128,768]{1,0:T(8,128)(2,1)S(1)} %get-tuple-element.45), channel_id=1, source_target_pairs={{0,1},{1,2},{2,3},{3,0},{4,5},{5,6},{6,7},{7,4},{8,9},{9,10},{10,1... | collective-permute-start | bytes 589832 | tf_op jit(solution)/shard_map/ppermute | solution.py:406
  102.6 6.3 %collective-permute-start.19 = (bf16[128,768]{1,0:T(8,128)(2,1)S(1)}, bf16[128,768]{1,0:T(8,128)(2,1)S(1)}, u32[]{:S(2)}, u32[]{:S(2)}) collective-permute-start(bf16[128,768]{1,0:T(8,128)(2,1)S(1)} %get-tuple-element.47), channel_id=1, source_target_pairs={{0,3},{1,0},{2,1},{3,2},{4,7},{5,4},{6,5},{7,6},{8,11},{9,8},{10,9... | collective-permute-start | bytes 589832 | tf_op jit(solution)/shard_map/ppermute | solution.py:406
  104.0 8.5 %collective-permute-start.21 = (bf16[128,768]{1,0:T(8,128)(2,1)S(1)}, bf16[128,768]{1,0:T(8,128)(2,1)S(1)}, u32[]{:S(2)}, u32[]{:S(2)}) collective-permute-start(bf16[128,768]{1,0:T(8,128)(2,1)S(1)} %get-tuple-element.48), channel_id=1, source_target_pairs={{0,3},{1,0},{2,1},{3,2},{4,7},{5,4},{6,5},{7,6},{8,11},{9,8},{10,9... | collective-permute-start | bytes 589832 | tf_op jit(solution)/shard_map/ppermute | solution.py:406
  105.3 7.3 %collective-permute-start.22 = (bf16[128,768]{1,0:T(8,128)(2,1)S(1)}, bf16[128,768]{1,0:T(8,128)(2,1)S(1)}, u32[]{:S(2)}, u32[]{:S(2)}) collective-permute-start(bf16[128,768]{1,0:T(8,128)(2,1)S(1)} %get-tuple-element.49), channel_id=1, source_target_pairs={{0,1},{1,2},{2,3},{3,0},{4,5},{5,6},{6,7},{7,4},{8,9},{9,10},{10,1... | collective-permute-start | bytes 589832 | tf_op jit(solution)/shard_map/ppermute | solution.py:406
  108.8 8.2 %collective-permute-start.18 = (bf16[128,768]{1,0:T(8,128)(2,1)S(1)}, bf16[128,768]{1,0:T(8,128)(2,1)S(1)}, u32[]{:S(2)}, u32[]{:S(2)}) collective-permute-start(bf16[128,768]{1,0:T(8,128)(2,1)S(1)} %add_convert_fusion.4), channel_id=1, source_target_pairs={{0,1},{1,2},{2,3},{3,0},{4,5},{5,6},{6,7},{7,4},{8,9},{9,10},{10,1... | collective-permute-start | bytes 589832 | tf_op jit(solution)/shard_map/ppermute | solution.py:406
  108.9 8.0 %collective-permute-start.20 = (bf16[128,768]{1,0:T(8,128)(2,1)S(1)}, bf16[128,768]{1,0:T(8,128)(2,1)S(1)}, u32[]{:S(2)}, u32[]{:S(2)}) collective-permute-start(bf16[128,768]{1,0:T(8,128)(2,1)S(1)} %add_convert_fusion.3), channel_id=1, source_target_pairs={{0,3},{1,0},{2,1},{3,2},{4,7},{5,4},{6,5},{7,6},{8,11},{9,8},{10,9... | collective-permute-start | bytes 589832 | tf_op jit(solution)/shard_map/ppermute | solution.py:406
  (5 other events, 28.0 us)

commit v7 on v6

--- a/solution.py
+++ b/solution.py
@@ -26,10 +26,27 @@
 
 
 Z_GROUPS = [
-    [chip_index(y, z, core) for z in range(NZ)] for y in range(NY) for core in range(NC)
+    [chip_index(y, z, core) for parity in range(2) for z in range(parity, NZ, 2)]
+    for y in range(NY)
+    for core in range(NC)
 ]
-Y_UP = [(d, (d + NZ * NC) % (NY * NZ * NC)) for d in range(NY * NZ * NC)]
-Y_DOWN = [(there, here) for here, there in Y_UP]
+PARITY_GROUPS = [
+    [chip_index(y, z, core) for z in range(parity, NZ, 2)]
+    for y in range(NY)
+    for parity in range(2)
+    for core in range(NC)
+]
+
+
+def moved(up, flip):
+    return [
+        (chip_index(y, z, core), chip_index((y + up) % NY, z ^ flip, core))
+        for y in range(NY)
+        for z in range(NZ)
+        for core in range(NC)
+    ]
+
+
 CORE_SWAP = [(device, device ^ 1) for device in range(NY * NZ * NC)]
 
 VMEM = pl.BlockSpec(memory_space=pltpu.VMEM)
@@ -42,16 +59,6 @@
 
 def exchange(blocks, groups):
     return lax.all_to_all(blocks, "tok", 0, 0, axis_index_groups=groups)
-
-
-def sum_shares(blocks, groups):
-    return jnp.sum(exchange(blocks, groups).astype(f32), axis=0).astype(bf16)
-
-
-def gather_rows(rows, groups):
-    size = len(groups[0])
-    gathered = exchange(jnp.broadcast_to(rows[None], (size,) + rows.shape), groups)
-    return gathered.reshape(-1, rows.shape[1])
 
 
 def dot(left, right):
@@ -87,6 +94,10 @@
 
 def own_core():
     return lax.rem(lax.axis_index("tok"), NC)
+
+
+def own_parity():
+    return lax.rem(lax.div(lax.axis_index("tok"), NC), 2)
 
 
 def own_y():
@@ -155,10 +166,12 @@
             grads[core, rows, :] = (dz * h3 * slope).astype(bf16)
             grads[1 - core, rows, :] = (dz * act).astype(bf16)
             store(grads.at[0, rows, :], factors_out.at[rows, :width])
-        own_send[...] = dot_tn(k_ref[...], grads[1]).astype(bf16)
-        store(own_send, own_out)
         shared_send[...] = dot_tn(hidden[...], errors[:, sent]).astype(bf16)
         store(shared_send, shared_out)
+        for row in range(0, width, ROWS):
+            rows = slice(row, row + ROWS)
+            own_send[rows, :] = dot_tn(k_ref[:, rows], grads[1]).astype(bf16)
+            store(own_send.at[rows, :], own_out.at[rows, :])
         for copy in stores:
             copy.wait()
 
@@ -171,7 +184,7 @@
         [wide, wide, pltpu.VMEM((3, width, width), bf16), wide, wide]
         + [pltpu.VMEM((2, tokens, width), bf16)]
         + [pltpu.VMEM(dims, bf16) for dims in results[:2]]
-        + [pltpu.SemaphoreType.DMA((5,)), pltpu.SemaphoreType.DMA((3 * parts + 2,))],
+        + [pltpu.SemaphoreType.DMA((5,)), pltpu.SemaphoreType.DMA((3 * parts + 1 + width // ROWS,))],
         60,
         9 * tokens * width * width,
         12 * width * width,
@@ -202,28 +215,22 @@
 
 def chip_sum(own_keep, own_got, shared_keep, shared_got):
     width, half = shared_keep.shape
-    rows = width // NY
+    cut = width // NY // 2
     wide = width + half
 
-    def body(ok_ref, og_ref, sk_ref, sg_ref, mine, *outs):
-        for step in range(NY):
-            start = lax.rem(own_y() + step, NY) * rows
-            for part in range(2):
-                cut = rows // 2
-                span = pl.ds(pl.multiple_of(start + part * cut, cut), cut)
-                own = ok_ref[span, :] + og_ref[span, :].astype(f32)
-                shared = sk_ref[span, :] + sg_ref[span, :].astype(f32)
-                if step == 0:
-                    mine[part * cut : (part + 1) * cut, :width] = own
-                    mine[part * cut : (part + 1) * cut, width:] = shared
-                else:
-                    out = outs[2 * (step - 1) + part]
-                    out[:, :width] = own.astype(bf16)
-                    out[:, width:] = shared.astype(bf16)
-
-    return call(
-        body,
-        [shape(rows, wide, dtype=f32)] + [shape(rows // 2, wide)] * (2 * NY - 2),
+    def body(ok_ref, og_ref, sk_ref, sg_ref, *outs):
+        for n, out in enumerate(outs):
+            block = lax.rem(own_y() + n // 2, NY) * 2
+            side = own_parity() if n % 2 == 0 else 1 - own_parity()
+            span = pl.ds(pl.multiple_of((block + side) * cut, cut), cut)
+            own = ok_ref[span, :] + og_ref[span, :].astype(f32)
+            shared = sk_ref[span, :] + sg_ref[span, :].astype(f32)
+            out[:, :width] = own.astype(out.dtype)
+            out[:, width:] = shared.astype(out.dtype)
+
+    return call(
+        body,
+        [shape(cut, wide, dtype=f32)] + [shape(cut, wide)] * (2 * NY - 1),
         [VMEM] * 4,
         [],
         16,
@@ -421,6 +428,31 @@
     return from_down_a, from_up_b, from_up_a, from_down_b
 
 
+def y_parity_sum(mine, mine_z, next_x, next_z, far_x, far_z, previous_x, previous_z):
+    relay_x = shift(far_x, "tok", moved(1, 0))
+    relay_z = shift(far_z, "tok", moved(-1, 0))
+    sum_x = shift(add(next_x, relay_x), "tok", moved(1, 0))
+    sum_z = shift(add(previous_z, relay_z), "tok", moved(-1, 1))
+    direct_x = shift(previous_x, "tok", moved(-1, 0))
+    beside = shift(mine_z, "tok", moved(0, 1))
+    direct_z = shift(next_z, "tok", moved(1, 1))
+    total = sum_x.astype(f32) + sum_z.astype(f32)
+    total = total + direct_x.astype(f32) + beside.astype(f32)
+    return (total + direct_z.astype(f32) + mine).astype(bf16)
+
+
+def sum_and_spread(blocks, times):
+    def body(in_ref, out_ref):
+        total = in_ref[0].astype(f32)
+        for n in range(1, blocks.shape[0]):
+            total = total + in_ref[n].astype(f32)
+        for n in range(times):
+            out_ref[n] = total.astype(bf16)
+
+    spread = shape(times, *blocks.shape[1:])
+    return call(body, spread, [VMEM], [], 16, 0, 6 * blocks.size, "sum_and_spread")(blocks)
+
+
 def ring_gather(block, axis, up, down):
     cut = block.shape[0] // 2
     block_a, block_b = block[:cut], block[cut:]
@@ -443,16 +475,13 @@
     own_got = swap_cores(own_send)
     shared_got = swap_cores(shared_send)
     own_keep, shared_keep = keep(keys, factors)
-    mine, *shares = chip_sum(own_keep, own_got, shared_keep, shared_got)
-
-    sum_a, sum_b, direct_a, direct_b = ring_sum(shares, "tok", Y_UP, Y_DOWN)
-    relayed = jnp.concatenate([sum_a, sum_b]).astype(f32)
-    direct = jnp.concatenate([direct_a, direct_b]).astype(f32)
-    y_sum = (relayed + direct + mine).astype(bf16)
-    z_sum = sum_shares(y_sum.reshape(NZ, width // NY // NZ, -1), Z_GROUPS)
-    y_rows = gather_rows(z_sum, Z_GROUPS)
-    previous, following, far = ring_gather(y_rows, "tok", Y_UP, Y_DOWN)
-    own_sum, shared_part = assemble(y_rows, previous, following, far)
+    shares = chip_sum(own_keep, own_got, shared_keep, shared_got)
+
+    y_sum = y_parity_sum(*shares)
+    shares = exchange(y_sum.reshape(NZ // 2, width // NY // NZ, -1), PARITY_GROUPS)
+    rows = exchange(sum_and_spread(shares, NZ), Z_GROUPS).reshape(width // NY, -1)
+    previous, following, far = ring_gather(rows, "tok", moved(1, 0), moved(-1, 0))
+    own_sum, shared_part = assemble(rows, previous, following, far)
 
     shared_other = swap_cores(shared_part)
     own_fresh = own_step(own_sum, fast_weights)

time: 118 us -> 114 us (0.966)
  blocking collectives: 35.3 us -> 27.4 us
  starting transfers between devices: 30 us -> 33.4 us
    all_to_all x2, blocking collectives: 35.3 us -> 27.4 us  [exchange(): return lax.all_to_all(blocks, 'tok', 0, 0, axis_index_groups=groups)]
    ppermute x5, starting transfers between devices: 8.7 us -> 11.3 us  [swap_cores(): return lax.ppermute(array, 'tok', CORE_SWAP)]
    ppermute x18 -> x19, starting transfers between devices: 21.3 us -> 22.1 us  [shift(): return lax.ppermute(array, axis, pairs)]
    ppermute x18 -> x19, waiting for transfers between devices: 27.7 us -> 28 us  [shift(): return lax.ppermute(array, axis, pairs)]
  transfers between devices with their start and end apart: 23 -> 24, of which waited for: 11 -> 11; matrix products, arithmetic and copies ran while one was open for 0% -> 0% of each run, Pallas kernels for 9% -> 9%
where the time goes in v7:
time: 114 us
  starting transfers between devices  33.4 us (29%)
  waiting for transfers between devices  28.6 us (25%)
  blocking collectives  27.4 us (24%)
  Pallas kernels  21.9 us (19%)
  local copies, waits for them, and re-layouts  1.6 us (1%)
    ppermute x19, waiting for transfers between devices, shift(): return lax.ppermute(array, axis, pairs)  28 us
    all_to_all x2, blocking collectives, exchange(): return lax.all_to_all(blocks, 'tok', 0, 0, axis_index_groups=groups)  27.4 us
    ppermute x19, starting transfers between devices, shift(): return lax.ppermute(array, axis, pairs)  22.1 us
    ppermute x5, starting transfers between devices, swap_cores(): return lax.ppermute(array, 'tok', CORE_SWAP)  11.3 us
    pallas_call x1, Pallas kernels, gradients(): call(body, [shape(*dims) for dims in results], [VMEM] + [HBM] * 3, [wide,...  7.02 us
    pallas_call x1, Pallas kernels, shared_step(): call(body, shape(width, width), [VMEM] * 3, [pltpu.VMEM((width, width), b...  4.79 us
    pallas_call x1, Pallas kernels, own_step(): call(body, [shape(width // 2, width)] * 2, [VMEM] * 2, [pltpu.VMEM((width...  4.78 us
    pallas_call x1, Pallas kernels, project(): call(body, [shape(tokens, width, dtype=f32)] + [shape(tokens // 2, width)...  2.69 us
  transfers between devices with their start and end apart: 24, of which 11 were waited for; matrix products, arithmetic and copies ran while one was open for 0% of the time, Pallas kernels for 9%

profile of v7, /device:TPU:1, one launch (start us, length us, event | category | flops | bytes accessed | tf_op | source)
XLA Modules:
  0.0 113.6 jit_solution(3973437941874320995)
XLA Ops:
  0.0 7.0 %gradients.1 = (bf16[768,768]{1,0:T(8,128)(2,1)}, bf16[768,384]{1,0:T(8,128)(2,1)}, bf16[512,1920]{1,0:T(8,128)(2,1)}) custom-call(f32[4,128]{1,0:T(4,128)} %bitcast.13, bf16[512,768]{1,0:T(8,128)(2,1)} %k_ref.1, bf16[512,768]{1,0:T(8,128)(2,1)} %v_hbm.1, bf16[1,3,768,768]{3,2,1,0:T(8,128)(2,1)} %w_ref.3), custom_call_target="tpu_custom_call" | custom-call | flops 2717908992 | bytes 7077888 | tf_op jit(solution)/shard_map/gradients/pallas_call | solution.py:180
  7.0 3.3 %collective-permute-start = (bf16[768,768]{1,0:T(8,128)(2,1)}, bf16[768,768]{1,0:T(8,128)(2,1)S(1)}, u32[]{:S(2)}, u32[]{:S(2)}) collective-permute-start(bf16[768,768]{1,0:T(8,128)(2,1)} %get-tuple-element.31), channel_id=1, source_target_pairs={{0,4},{4,0},{8,12},{12,8},{16,20},{20,16},{24,28},{28,24},{32,36},... | collective-permute-start | bytes 3538952 | tf_op jit(solution)/shard_map/ppermute | solution.py:57
  10.5 1.5 %copy-done.3 = bf16[512,1920]{1,0:T(8,128)(2,1)S(1)} copy-done((bf16[512,1920]{1,0:T(8,128)(2,1)S(1)}, bf16[512,1920]{1,0:T(8,128)(2,1)}, u32[]{:S(2)}) %copy-start.3) | copy-done | bytes 1966104
  14.3 2.7 %collective-permute-start.4 = (bf16[96,1152]{1,0:T(8,128)(2,1)S(1)}, bf16[96,1152]{1,0:T(8,128)(2,1)S(1)}, u32[]{:S(2)}, u32[]{:S(2)}) collective-permute-start(bf16[96,1152]{1,0:T(8,128)(2,1)S(1)} %get-tuple-element.37), channel_id=1, source_target_pairs={{0,192},{4,196},{8,200},{12,204},{16,208},{20,212},{24,216},{28,22... | collective-permute-start | bytes 663560 | tf_op jit(solution)/shard_map/ppermute | solution.py:413
  17.0 1.4 %collective-permute-start.7 = (bf16[96,1152]{1,0:T(8,128)(2,1)S(1)}, bf16[96,1152]{1,0:T(8,128)(2,1)S(1)}, u32[]{:S(2)}, u32[]{:S(2)}) collective-permute-start(bf16[96,1152]{1,0:T(8,128)(2,1)S(1)} %get-tuple-element.39), channel_id=1, source_target_pairs={{0,8},{4,12},{8,0},{12,4},{16,24},{20,28},{24,16},{28,20},{32,40},... | collective-permute-start | bytes 663560 | tf_op jit(solution)/shard_map/ppermute | solution.py:413
  19.6 2.5 %collective-permute-done.2 = bf16[96,1152]{1,0:T(8,128)(2,1)S(1)} collective-permute-done((bf16[96,1152]{1,0:T(8,128)(2,1)S(1)}, bf16[96,1152]{1,0:T(8,128)(2,1)S(1)}, u32[]{:S(2)}, u32[]{:S(2)}) %collective-permute-start.2) | collective-permute-done | bytes 221216 | tf_op jit(solution)/shard_map/ppermute | solution.py:413
  22.4 2.5 %collective-permute-start.5 = (bf16[96,1152]{1,0:T(8,128)(2,1)S(1)}, bf16[96,1152]{1,0:T(8,128)(2,1)S(1)}, u32[]{:S(2)}, u32[]{:S(2)}) collective-permute-start(bf16[96,1152]{1,0:T(8,128)(2,1)S(1)} %add_convert_fusion.1), channel_id=1, source_target_pairs={{0,200},{4,204},{8,192},{12,196},{16,216},{20,220},{24,208},{28,21... | collective-permute-start | bytes 663560 | tf_op jit(solution)/shard_map/ppermute | solution.py:413
  25.8 2.2 %collective-permute-done.8 = bf16[96,1152]{1,0:T(8,128)(2,1)S(1)} collective-permute-done((bf16[96,1152]{1,0:T(8,128)(2,1)S(1)}, bf16[96,1152]{1,0:T(8,128)(2,1)S(1)}, u32[]{:S(2)}, u32[]{:S(2)}) %collective-permute-start.8) | collective-permute-done | bytes 221216 | tf_op jit(solution)/shard_map/ppermute | solution.py:413
  28.1 5.9 %collective-permute-done.3 = bf16[96,1152]{1,0:T(8,128)(2,1)S(1)} collective-permute-done((bf16[96,1152]{1,0:T(8,128)(2,1)S(1)}, bf16[96,1152]{1,0:T(8,128)(2,1)S(1)}, u32[]{:S(2)}, u32[]{:S(2)}) %collective-permute-start.3) | collective-permute-done | bytes 221216 | tf_op jit(solution)/shard_map/ppermute | solution.py:413
  34.1 14.6 %all_to_all.10.in_ref = bf16[4,24,1152]{2,1,0:T(8,128)(2,1)S(1)} all-to-all(bf16[4,24,1152]{2,1,0:T(8,128)(2,1)S(1)} %bitcast.8), channel_id=1, replica_groups={{0,16,32,48},{4,20,36,52},{8,24,40,56},{12,28,44,60},{64,80,96,112},{68..., dimensions={0} | all-to-all | bytes 442368 | tf_op jit(solution)/shard_map/all_to_all | solution.py:61
  48.7 12.8 %all_to_all.11 = bf16[8,24,1152]{2,1,0:T(8,128)(2,1)S(1)} all-to-all(bf16[8,24,1152]{2,1,0:T(8,128)(2,1)S(1)} %sum_and_spread.1), channel_id=1, replica_groups={{0,16,32,48,8,24,40,56},{4,20,36,52,12,28,44,60},{64,80,96,112,72,88,10..., dimensions={0} | all-to-all | bytes 884736 | tf_op jit(solution)/shard_map/all_to_all | solution.py:61
  61.9 2.7 %collective-permute-start.10 = (bf16[96,1152]{1,0:T(8,128)(2,1)S(1)}, bf16[96,1152]{1,0:T(8,128)(2,1)S(1)}, u32[]{:S(2)}, u32[]{:S(2)}) collective-permute-start(bf16[96,1152]{1,0:T(8,128)(2,1)S(1)} %bitcast.9), channel_id=1, source_target_pairs={{0,192},{4,196},{8,200},{12,204},{16,208},{20,212},{24,216},{28,22... | collective-permute-start | bytes 663560 | tf_op jit(solution)/shard_map/ppermute | solution.py:413
  66.0 1.9 %collective-permute-done.11.rest_4_ = bf16[96,1152]{1,0:T(8,128)(2,1)S(1)} collective-permute-done((bf16[96,1152]{1,0:T(8,128)(2,1)S(1)}, bf16[96,1152]{1,0:T(8,128)(2,1)S(1)}, u32[]{:S(2)}, u32[]{:S(2)}) %collective-permute-start.11) | collective-permute-done | bytes 221216 | tf_op jit(solution)/shard_map/ppermute | solution.py:413
  67.9 2.7 %collective-permute-start.13 = (bf16[96,1152]{1,0:T(8,128)(2,1)S(1)}, bf16[96,1152]{1,0:T(8,128)(2,1)S(1)}, u32[]{:S(2)}, u32[]{:S(2)}) collective-permute-start(bf16[96,1152]{1,0:T(8,128)(2,1)S(1)} %collective-permute-done.10.rest_1_), channel_id=1, source_target_pairs={{0,192},{4,196},{8,200},{12,204},{16,208},{20,212},{24,216},{28,22... | collective-permute-start | bytes 663560 | tf_op jit(solution)/shard_map/ppermute | solution.py:413
  71.3 5.2 %collective-permute-done.12.rest_2_ = bf16[96,1152]{1,0:T(8,128)(2,1)S(1)} collective-permute-done((bf16[96,1152]{1,0:T(8,128)(2,1)S(1)}, bf16[96,1152]{1,0:T(8,128)(2,1)S(1)}, u32[]{:S(2)}, u32[]{:S(2)}) %collective-permute-start.12) | collective-permute-done | bytes 221216 | tf_op jit(solution)/shard_map/ppermute | solution.py:413
  76.7 7.3 %collective-permute-start.17 = (bf16[768,384]{1,0:T(8,128)(2,1)S(1)}, bf16[768,384]{1,0:T(8,128)(2,1)S(1)}, u32[]{:S(2)}, u32[]{:S(2)}) collective-permute-start(bf16[768,384]{1,0:T(8,128)(2,1)S(1)} %get-tuple-element.45.a_ref), channel_id=1, source_target_pairs={{0,4},{4,0},{8,12},{12,8},{16,20},{20,16},{24,28},{28,24},{32,36},... | collective-permute-start | bytes 1769480 | tf_op jit(solution)/shard_map/ppermute | solution.py:57
  84.0 4.8 %own_step.1 = (bf16[384,768]{1,0:T(8,128)(2,1)S(1)}, bf16[384,768]{1,0:T(8,128)(2,1)S(1)}) custom-call(bf16[768,768]{1,0:T(8,128)(2,1)S(1)} %get-tuple-element.42.x_ref, bf16[1,3,768,768]{3,2,1,0:T(8,128)(2,1)S(1)} %copy-done.1), custom_call_target="tpu_custom_call" | custom-call | flops 4529848320 | bytes 3538944 | tf_op jit(solution)/shard_map/own_step/pallas_call | solution.py:324
  89.4 4.8 %shared_step.1.shared_ref = bf16[768,768]{1,0:T(8,128)(2,1)S(1)} custom-call(bf16[768,384]{1,0:T(8,128)(2,1)S(1)} %get-tuple-element.45.a_ref, bf16[768,384]{1,0:T(8,128)(2,1)S(1)} %collective-permute-done.17.b_ref, bf16[1,3,768,768]{3,2,1,0:T(8,128)(2,1)S(1)} %copy-done.1), custom_call_target="tpu_custom_call" | custom-call | flops 4529848320 | bytes 3538944 | tf_op jit(solution)/shard_map/shared_step/pallas_call | solution.py:346
  94.2 2.7 %project.1 = (f32[256,768]{1,0:T(8,128)S(1)}, bf16[128,768]{1,0:T(8,128)(2,1)S(1)}, bf16[128,768]{1,0:T(8,128)(2,1)S(1)}, bf16[128,768]{1,0:T(8,128)(2,1)S(1)}, ...) custom-call(bf16[256,768]{1,0:T(8,128)(2,1)S(1)} %copy-done, ...), custom_call_target="tpu_custom_call" | custom-call | flops 2113929216 | bytes 9437184 | tf_op jit(solution)/shard_map/project/pallas_call | solution.py:384
  96.9 1.3 %collective-permute-start.18 = (bf16[128,768]{1,0:T(8,128)(2,1)S(1)}, bf16[128,768]{1,0:T(8,128)(2,1)S(1)}, u32[]{:S(2)}, u32[]{:S(2)}) collective-permute-start(bf16[128,768]{1,0:T(8,128)(2,1)S(1)} %get-tuple-element.47), channel_id=1, source_target_pairs={{0,1},{1,2},{2,3},{3,0},{4,5},{5,6},{6,7},{7,4},{8,9},{9,10},{10,1... | collective-permute-start | bytes 589832 | tf_op jit(solution)/shard_map/ppermute | solution.py:413
  98.2 1.5 %collective-permute-start.20 = (bf16[128,768]{1,0:T(8,128)(2,1)S(1)}, bf16[128,768]{1,0:T(8,128)(2,1)S(1)}, u32[]{:S(2)}, u32[]{:S(2)}) collective-permute-start(bf16[128,768]{1,0:T(8,128)(2,1)S(1)} %get-tuple-element.49), channel_id=1, source_target_pairs={{0,3},{1,0},{2,1},{3,2},{4,7},{5,4},{6,5},{7,6},{8,11},{9,8},{10,9... | collective-permute-start | bytes 589832 | tf_op jit(solution)/shard_map/ppermute | solution.py:413
  101.2 3.2 %collective-permute-done.18 = bf16[128,768]{1,0:T(8,128)(2,1)S(1)} collective-permute-done((bf16[128,768]{1,0:T(8,128)(2,1)S(1)}, bf16[128,768]{1,0:T(8,128)(2,1)S(1)}, u32[]{:S(2)}, u32[]{:S(2)}) %collective-permute-start.18) | collective-permute-done | bytes 196640 | tf_op jit(solution)/shard_map/ppermute | solution.py:413
  104.6 2.7 %collective-permute-start.21 = (bf16[128,768]{1,0:T(8,128)(2,1)S(1)}, bf16[128,768]{1,0:T(8,128)(2,1)S(1)}, u32[]{:S(2)}, u32[]{:S(2)}) collective-permute-start(bf16[128,768]{1,0:T(8,128)(2,1)S(1)} %add_convert_fusion.3), channel_id=1, source_target_pairs={{0,3},{1,0},{2,1},{3,2},{4,7},{5,4},{6,5},{7,6},{8,11},{9,8},{10,9... | collective-permute-start | bytes 589832 | tf_op jit(solution)/shard_map/ppermute | solution.py:413
  108.2 4.4 %collective-permute-done.19.sum_a_ref = bf16[128,768]{1,0:T(8,128)(2,1)S(1)} collective-permute-done((bf16[128,768]{1,0:T(8,128)(2,1)S(1)}, bf16[128,768]{1,0:T(8,128)(2,1)S(1)}, u32[]{:S(2)}, u32[]{:S(2)}) %collective-permute-start.19) | collective-permute-done | bytes 196640 | tf_op jit(solution)/shard_map/ppermute | solution.py:413
  (54 shorter events, 11.9 us)
Async XLA Ops:
  7.0 6.9 %collective-permute-start = (bf16[768,768]{1,0:T(8,128)(2,1)}, bf16[768,768]{1,0:T(8,128)(2,1)S(1)}, u32[]{:S(2)}, u32[]{:S(2)}) collective-permute-start(bf16[768,768]{1,0:T(8,128)(2,1)} %get-tuple-element.31), channel_id=1, source_target_pairs={{0,4},{4,0},{8,12},{12,8},{16,20},{20,16},{24,28},{28,24},{32,36},... | collective-permute-start | bytes 3538952 | tf_op jit(solution)/shard_map/ppermute | solution.py:57
  10.4 3.5 %collective-permute-start.1 = (bf16[768,384]{1,0:T(8,128)(2,1)}, bf16[768,384]{1,0:T(8,128)(2,1)S(1)}, u32[]{:S(2)}, u32[]{:S(2)}) collective-permute-start(bf16[768,384]{1,0:T(8,128)(2,1)} %get-tuple-element.33), channel_id=1, source_target_pairs={{0,4},{4,0},{8,12},{12,8},{16,20},{20,16},{24,28},{28,24},{32,36},... | collective-permute-start | bytes 1769480 | tf_op jit(solution)/shard_map/ppermute | solution.py:57
  14.2 7.9 %collective-permute-start.2 = (bf16[96,1152]{1,0:T(8,128)(2,1)S(1)}, bf16[96,1152]{1,0:T(8,128)(2,1)S(1)}, u32[]{:S(2)}, u32[]{:S(2)}) collective-permute-start(bf16[96,1152]{1,0:T(8,128)(2,1)S(1)} %get-tuple-element.35), channel_id=1, source_target_pairs={{0,64},{4,68},{8,72},{12,76},{16,80},{20,84},{24,88},{28,92},{32,9... | collective-permute-start | bytes 663560 | tf_op jit(solution)/shard_map/ppermute | solution.py:413
  14.3 8.0 %collective-permute-start.4 = (bf16[96,1152]{1,0:T(8,128)(2,1)S(1)}, bf16[96,1152]{1,0:T(8,128)(2,1)S(1)}, u32[]{:S(2)}, u32[]{:S(2)}) collective-permute-start(bf16[96,1152]{1,0:T(8,128)(2,1)S(1)} %get-tuple-element.37), channel_id=1, source_target_pairs={{0,192},{4,196},{8,200},{12,204},{16,208},{20,212},{24,216},{28,22... | collective-permute-start | bytes 663560 | tf_op jit(solution)/shard_map/ppermute | solution.py:413
  17.0 8.9 %collective-permute-start.6 = (bf16[96,1152]{1,0:T(8,128)(2,1)S(1)}, bf16[96,1152]{1,0:T(8,128)(2,1)S(1)}, u32[]{:S(2)}, u32[]{:S(2)}) collective-permute-start(bf16[96,1152]{1,0:T(8,128)(2,1)S(1)} %get-tuple-element.38), channel_id=1, source_target_pairs={{0,192},{4,196},{8,200},{12,204},{16,208},{20,212},{24,216},{28,22... | collective-permute-start | bytes 663560 | tf_op jit(solution)/shard_map/ppermute | solution.py:413
  17.0 8.8 %collective-permute-start.7 = (bf16[96,1152]{1,0:T(8,128)(2,1)S(1)}, bf16[96,1152]{1,0:T(8,128)(2,1)S(1)}, u32[]{:S(2)}, u32[]{:S(2)}) collective-permute-start(bf16[96,1152]{1,0:T(8,128)(2,1)S(1)} %get-tuple-element.39), channel_id=1, source_target_pairs={{0,8},{4,12},{8,0},{12,4},{16,24},{20,28},{24,16},{28,20},{32,40},... | collective-permute-start | bytes 663560 | tf_op jit(solution)/shard_map/ppermute | solution.py:413
  18.4 9.7 %collective-permute-start.8 = (bf16[96,1152]{1,0:T(8,128)(2,1)S(1)}, bf16[96,1152]{1,0:T(8,128)(2,1)S(1)}, u32[]{:S(2)}, u32[]{:S(2)}) collective-permute-start(bf16[96,1152]{1,0:T(8,128)(2,1)S(1)} %get-tuple-element.40), channel_id=1, source_target_pairs={{0,72},{4,76},{8,64},{12,68},{16,88},{20,92},{24,80},{28,84},{32,1... | collective-permute-start | bytes 663560 | tf_op jit(solution)/shard_map/ppermute | solution.py:413
  22.2 11.7 %collective-permute-start.3 = (bf16[96,1152]{1,0:T(8,128)(2,1)S(1)}, bf16[96,1152]{1,0:T(8,128)(2,1)S(1)}, u32[]{:S(2)}, u32[]{:S(2)}) collective-permute-start(bf16[96,1152]{1,0:T(8,128)(2,1)S(1)} %add_convert_fusion.2), channel_id=1, source_target_pairs={{0,64},{4,68},{8,72},{12,76},{16,80},{20,84},{24,88},{28,92},{32,9... | collective-permute-start | bytes 663560 | tf_op jit(solution)/shard_map/ppermute | solution.py:413
  22.4 11.6 %collective-permute-start.5 = (bf16[96,1152]{1,0:T(8,128)(2,1)S(1)}, bf16[96,1152]{1,0:T(8,128)(2,1)S(1)}, u32[]{:S(2)}, u32[]{:S(2)}) collective-permute-start(bf16[96,1152]{1,0:T(8,128)(2,1)S(1)} %add_convert_fusion.1), channel_id=1, source_target_pairs={{0,200},{4,204},{8,192},{12,196},{16,216},{20,220},{24,208},{28,21... | collective-permute-start | bytes 663560 | tf_op jit(solution)/shard_map/ppermute | solution.py:413
  61.6 6.3 %collective-permute-start.11 = (bf16[96,1152]{1,0:T(8,128)(2,1)S(1)}, bf16[96,1152]{1,0:T(8,128)(2,1)S(1)}, u32[]{:S(2)}, u32[]{:S(2)}) collective-permute-start(bf16[96,1152]{1,0:T(8,128)(2,1)S(1)} %bitcast.11), channel_id=1, source_target_pairs={{0,64},{4,68},{8,72},{12,76},{16,80},{20,84},{24,88},{28,92},{32,9... | collective-permute-start | bytes 663560 | tf_op jit(solution)/shard_map/ppermute | solution.py:413
  61.9 6.0 %collective-permute-start.10 = (bf16[96,1152]{1,0:T(8,128)(2,1)S(1)}, bf16[96,1152]{1,0:T(8,128)(2,1)S(1)}, u32[]{:S(2)}, u32[]{:S(2)}) collective-permute-start(bf16[96,1152]{1,0:T(8,128)(2,1)S(1)} %bitcast.9), channel_id=1, source_target_pairs={{0,192},{4,196},{8,200},{12,204},{16,208},{20,212},{24,216},{28,22... | collective-permute-start | bytes 663560 | tf_op jit(solution)/shard_map/ppermute | solution.py:413
  64.6 6.0 %collective-permute-start.9 = (bf16[96,1152]{1,0:T(8,128)(2,1)S(1)}, bf16[96,1152]{1,0:T(8,128)(2,1)S(1)}, u32[]{:S(2)}, u32[]{:S(2)}) collective-permute-start(bf16[96,1152]{1,0:T(8,128)(2,1)S(1)} %bitcast.12), channel_id=1, source_target_pairs={{0,192},{4,196},{8,200},{12,204},{16,208},{20,212},{24,216},{28,22... | collective-permute-start | bytes 663560 | tf_op jit(solution)/shard_map/ppermute | solution.py:413
  65.3 6.0 %collective-permute-start.14 = (bf16[96,1152]{1,0:T(8,128)(2,1)S(1)}, bf16[96,1152]{1,0:T(8,128)(2,1)S(1)}, u32[]{:S(2)}, u32[]{:S(2)}) collective-permute-start(bf16[96,1152]{1,0:T(8,128)(2,1)S(1)} %bitcast.10), channel_id=1, source_target_pairs={{0,64},{4,68},{8,72},{12,76},{16,80},{20,84},{24,88},{28,92},{32,9... | collective-permute-start | bytes 663560 | tf_op jit(solution)/shard_map/ppermute | solution.py:413
  67.9 8.7 %collective-permute-start.12 = (bf16[96,1152]{1,0:T(8,128)(2,1)S(1)}, bf16[96,1152]{1,0:T(8,128)(2,1)S(1)}, u32[]{:S(2)}, u32[]{:S(2)}) collective-permute-start(bf16[96,1152]{1,0:T(8,128)(2,1)S(1)} %collective-permute-done.11.rest_4_), channel_id=1, source_target_pairs={{0,64},{4,68},{8,72},{12,76},{16,80},{20,84},{24,88},{28,92},{32,9... | collective-permute-start | bytes 663560 | tf_op jit(solution)/shard_map/ppermute | solution.py:413
  67.9 8.7 %collective-permute-start.13 = (bf16[96,1152]{1,0:T(8,128)(2,1)S(1)}, bf16[96,1152]{1,0:T(8,128)(2,1)S(1)}, u32[]{:S(2)}, u32[]{:S(2)}) collective-permute-start(bf16[96,1152]{1,0:T(8,128)(2,1)S(1)} %collective-permute-done.10.rest_1_), channel_id=1, source_target_pairs={{0,192},{4,196},{8,200},{12,204},{16,208},{20,212},{24,216},{28,22... | collective-permute-start | bytes 663560 | tf_op jit(solution)/shard_map/ppermute | solution.py:413
  76.7 12.7 %collective-permute-start.17 = (bf16[768,384]{1,0:T(8,128)(2,1)S(1)}, bf16[768,384]{1,0:T(8,128)(2,1)S(1)}, u32[]{:S(2)}, u32[]{:S(2)}) collective-permute-start(bf16[768,384]{1,0:T(8,128)(2,1)S(1)} %get-tuple-element.45.a_ref), channel_id=1, source_target_pairs={{0,4},{4,0},{8,12},{12,8},{16,20},{20,16},{24,28},{28,24},{32,36},... | collective-permute-start | bytes 1769480 | tf_op jit(solution)/shard_map/ppermute | solution.py:57
  88.8 5.4 %collective-permute-start.15 = (bf16[384,768]{1,0:T(8,128)(2,1)S(1)}, bf16[384,768]{1,0:T(8,128)(2,1)S(1)}, u32[]{:S(2)}, u32[]{:S(2)}) collective-permute-start(bf16[384,768]{1,0:T(8,128)(2,1)S(1)} %get-tuple-element.43.own_a), channel_id=1, source_target_pairs={{0,4},{4,0},{8,12},{12,8},{16,20},{20,16},{24,28},{28,24},{32,36},... | collective-permute-start | bytes 1769480 | tf_op jit(solution)/shard_map/ppermute | solution.py:57
  88.9 5.3 %collective-permute-start.16 = (bf16[384,768]{1,0:T(8,128)(2,1)S(1)}, bf16[384,768]{1,0:T(8,128)(2,1)S(1)}, u32[]{:S(2)}, u32[]{:S(2)}) collective-permute-start(bf16[384,768]{1,0:T(8,128)(2,1)S(1)} %get-tuple-element.44.own_b), channel_id=1, source_target_pairs={{0,4},{4,0},{8,12},{12,8},{16,20},{20,16},{24,28},{28,24},{32,36},... | collective-permute-start | bytes 1769480 | tf_op jit(solution)/shard_map/ppermute | solution.py:57
  96.9 7.4 %collective-permute-start.18 = (bf16[128,768]{1,0:T(8,128)(2,1)S(1)}, bf16[128,768]{1,0:T(8,128)(2,1)S(1)}, u32[]{:S(2)}, u32[]{:S(2)}) collective-permute-start(bf16[128,768]{1,0:T(8,128)(2,1)S(1)} %get-tuple-element.47), channel_id=1, source_target_pairs={{0,1},{1,2},{2,3},{3,0},{4,5},{5,6},{6,7},{7,4},{8,9},{9,10},{10,1... | collective-permute-start | bytes 589832 | tf_op jit(solution)/shard_map/ppermute | solution.py:413
  98.2 6.3 %collective-permute-start.20 = (bf16[128,768]{1,0:T(8,128)(2,1)S(1)}, bf16[128,768]{1,0:T(8,128)(2,1)S(1)}, u32[]{:S(2)}, u32[]{:S(2)}) collective-permute-start(bf16[128,768]{1,0:T(8,128)(2,1)S(1)} %get-tuple-element.49), channel_id=1, source_target_pairs={{0,3},{1,0},{2,1},{3,2},{4,7},{5,4},{6,5},{7,6},{8,11},{9,8},{10,9... | collective-permute-start | bytes 589832 | tf_op jit(solution)/shard_map/ppermute | solution.py:413
  99.7 8.6 %collective-permute-start.22 = (bf16[128,768]{1,0:T(8,128)(2,1)S(1)}, bf16[128,768]{1,0:T(8,128)(2,1)S(1)}, u32[]{:S(2)}, u32[]{:S(2)}) collective-permute-start(bf16[128,768]{1,0:T(8,128)(2,1)S(1)} %get-tuple-element.50), channel_id=1, source_target_pairs={{0,3},{1,0},{2,1},{3,2},{4,7},{5,4},{6,5},{7,6},{8,11},{9,8},{10,9... | collective-permute-start | bytes 589832 | tf_op jit(solution)/shard_map/ppermute | solution.py:413
  100.9 7.3 %collective-permute-start.23 = (bf16[128,768]{1,0:T(8,128)(2,1)S(1)}, bf16[128,768]{1,0:T(8,128)(2,1)S(1)}, u32[]{:S(2)}, u32[]{:S(2)}) collective-permute-start(bf16[128,768]{1,0:T(8,128)(2,1)S(1)} %get-tuple-element.51), channel_id=1, source_target_pairs={{0,1},{1,2},{2,3},{3,0},{4,5},{5,6},{6,7},{7,4},{8,9},{9,10},{10,1... | collective-permute-start | bytes 589832 | tf_op jit(solution)/shard_map/ppermute | solution.py:413
  104.4 8.2 %collective-permute-start.19 = (bf16[128,768]{1,0:T(8,128)(2,1)S(1)}, bf16[128,768]{1,0:T(8,128)(2,1)S(1)}, u32[]{:S(2)}, u32[]{:S(2)}) collective-permute-start(bf16[128,768]{1,0:T(8,128)(2,1)S(1)} %add_convert_fusion.4), channel_id=1, source_target_pairs={{0,1},{1,2},{2,3},{3,0},{4,5},{5,6},{6,7},{7,4},{8,9},{9,10},{10,1... | collective-permute-start | bytes 589832 | tf_op jit(solution)/shard_map/ppermute | solution.py:413
  104.6 8.0 %collective-permute-start.21 = (bf16[128,768]{1,0:T(8,128)(2,1)S(1)}, bf16[128,768]{1,0:T(8,128)(2,1)S(1)}, u32[]{:S(2)}, u32[]{:S(2)}) collective-permute-start(bf16[128,768]{1,0:T(8,128)(2,1)S(1)} %add_convert_fusion.3), channel_id=1, source_target_pairs={{0,3},{1,0},{2,1},{3,2},{4,7},{5,4},{6,5},{7,6},{8,11},{9,8},{10,9... | collective-permute-start | bytes 589832 | tf_op jit(solution)/shard_map/ppermute | solution.py:413
  (6 other events, 63.3 us)

commit v8 on v7

--- a/solution.py
+++ b/solution.py
@@ -26,12 +26,12 @@
 
 
 Z_GROUPS = [
-    [chip_index(y, z, core) for parity in range(2) for z in range(parity, NZ, 2)]
+    [chip_index(y, z, core) for parity in range(2) for z in reversed(range(parity, NZ, 2))]
     for y in range(NY)
     for core in range(NC)
 ]
 PARITY_GROUPS = [
-    [chip_index(y, z, core) for z in range(parity, NZ, 2)]
+    [chip_index(y, z, core) for z in reversed(range(parity, NZ, 2))]
     for y in range(NY)
     for parity in range(2)
     for core in range(NC)

time: 114 us -> 113 us (level)
  starting transfers between devices: 33.4 us -> 29.2 us
  waiting for transfers between devices: 28.6 us -> 30.3 us
  blocking collectives: 27.4 us -> 28.7 us
    ppermute x5, starting transfers between devices: 11.3 us -> 7.17 us  [swap_cores(): return lax.ppermute(array, 'tok', CORE_SWAP)]
    ppermute x19, waiting for transfers between devices: 28 us -> 29.7 us  [shift(): return lax.ppermute(array, axis, pairs)]
    all_to_all x2, blocking collectives: 27.4 us -> 28.7 us  [exchange(): return lax.all_to_all(blocks, 'tok', 0, 0, axis_index_groups=groups)]
  transfers between devices with their start and end apart: 24 -> 24, of which waited for: 11 -> 12; matrix products, arithmetic and copies ran while one was open for 0% -> 0% of each run, Pallas kernels for 9% -> 10%
where the time goes in v8:
time: 113 us; the launch traced here: 112 us
  waiting for transfers between devices  30.3 us (27%)
  starting transfers between devices  29.2 us (26%)
  blocking collectives  28.7 us (25%)
  Pallas kernels  21.9 us (19%)
  local copies, waits for them, and re-layouts  1.61 us (1%)
    ppermute x19, waiting for transfers between devices, shift(): return lax.ppermute(array, axis, pairs)  29.7 us
    all_to_all x2, blocking collectives, exchange(): return lax.all_to_all(blocks, 'tok', 0, 0, axis_index_groups=groups)  28.7 us
    ppermute x19, starting transfers between devices, shift(): return lax.ppermute(array, axis, pairs)  22.1 us
    ppermute x5, starting transfers between devices, swap_cores(): return lax.ppermute(array, 'tok', CORE_SWAP)  7.17 us
    pallas_call x1, Pallas kernels, gradients(): call(body, [shape(*dims) for dims in results], [VMEM] + [HBM] * 3, [wide,...  7.02 us
    pallas_call x1, Pallas kernels, shared_step(): call(body, shape(width, width), [VMEM] * 3, [pltpu.VMEM((width, width), b...  4.79 us
    pallas_call x1, Pallas kernels, own_step(): call(body, [shape(width // 2, width)] * 2, [VMEM] * 2, [pltpu.VMEM((width...  4.78 us
    pallas_call x1, Pallas kernels, project(): call(body, [shape(tokens, width, dtype=f32)] + [shape(tokens // 2, width)...  2.69 us
  transfers between devices with their start and end apart: 24, of which 12 were waited for; matrix products, arithmetic and copies ran while one was open for 0% of the time, Pallas kernels for 10%

profile of v8, /device:TPU:1, one launch (start us, length us, event | category | flops | bytes accessed | tf_op | source)
XLA Modules:
  0.0 112.4 jit_solution(17536439452659569967)
XLA Ops:
  0.0 7.0 %gradients.1 = (bf16[768,768]{1,0:T(8,128)(2,1)}, bf16[768,384]{1,0:T(8,128)(2,1)}, bf16[512,1920]{1,0:T(8,128)(2,1)}) custom-call(f32[4,128]{1,0:T(4,128)} %bitcast.13, bf16[512,768]{1,0:T(8,128)(2,1)} %k_ref.1, bf16[512,768]{1,0:T(8,128)(2,1)} %v_hbm.1, bf16[1,3,768,768]{3,2,1,0:T(8,128)(2,1)} %w_ref.3), custom_call_target="tpu_custom_call" | custom-call | flops 2717908992 | bytes 7077888 | tf_op jit(solution)/shard_map/gradients/pallas_call | solution.py:180
  7.0 3.3 %collective-permute-start = (bf16[768,768]{1,0:T(8,128)(2,1)}, bf16[768,768]{1,0:T(8,128)(2,1)S(1)}, u32[]{:S(2)}, u32[]{:S(2)}) collective-permute-start(bf16[768,768]{1,0:T(8,128)(2,1)} %get-tuple-element.31), channel_id=1, source_target_pairs={{0,4},{4,0},{8,12},{12,8},{16,20},{20,16},{24,28},{28,24},{32,36},... | collective-permute-start | bytes 3538952 | tf_op jit(solution)/shard_map/ppermute | solution.py:57
  10.5 1.5 %copy-done.3 = bf16[512,1920]{1,0:T(8,128)(2,1)S(1)} copy-done((bf16[512,1920]{1,0:T(8,128)(2,1)S(1)}, bf16[512,1920]{1,0:T(8,128)(2,1)}, u32[]{:S(2)}) %copy-start.3) | copy-done | bytes 1966104
  14.3 2.7 %collective-permute-start.4 = (bf16[96,1152]{1,0:T(8,128)(2,1)S(1)}, bf16[96,1152]{1,0:T(8,128)(2,1)S(1)}, u32[]{:S(2)}, u32[]{:S(2)}) collective-permute-start(bf16[96,1152]{1,0:T(8,128)(2,1)S(1)} %get-tuple-element.37), channel_id=1, source_target_pairs={{0,192},{4,196},{8,200},{12,204},{16,208},{20,212},{24,216},{28,22... | collective-permute-start | bytes 663560 | tf_op jit(solution)/shard_map/ppermute | solution.py:413
  17.0 1.4 %collective-permute-start.7 = (bf16[96,1152]{1,0:T(8,128)(2,1)S(1)}, bf16[96,1152]{1,0:T(8,128)(2,1)S(1)}, u32[]{:S(2)}, u32[]{:S(2)}) collective-permute-start(bf16[96,1152]{1,0:T(8,128)(2,1)S(1)} %get-tuple-element.39), channel_id=1, source_target_pairs={{0,8},{4,12},{8,0},{12,4},{16,24},{20,28},{24,16},{28,20},{32,40},... | collective-permute-start | bytes 663560 | tf_op jit(solution)/shard_map/ppermute | solution.py:413
  19.6 2.5 %collective-permute-done.2 = bf16[96,1152]{1,0:T(8,128)(2,1)S(1)} collective-permute-done((bf16[96,1152]{1,0:T(8,128)(2,1)S(1)}, bf16[96,1152]{1,0:T(8,128)(2,1)S(1)}, u32[]{:S(2)}, u32[]{:S(2)}) %collective-permute-start.2) | collective-permute-done | bytes 221216 | tf_op jit(solution)/shard_map/ppermute | solution.py:413
  22.4 2.5 %collective-permute-start.5 = (bf16[96,1152]{1,0:T(8,128)(2,1)S(1)}, bf16[96,1152]{1,0:T(8,128)(2,1)S(1)}, u32[]{:S(2)}, u32[]{:S(2)}) collective-permute-start(bf16[96,1152]{1,0:T(8,128)(2,1)S(1)} %add_convert_fusion.1), channel_id=1, source_target_pairs={{0,200},{4,204},{8,192},{12,196},{16,216},{20,220},{24,208},{28,21... | collective-permute-start | bytes 663560 | tf_op jit(solution)/shard_map/ppermute | solution.py:413
  25.8 2.2 %collective-permute-done.8 = bf16[96,1152]{1,0:T(8,128)(2,1)S(1)} collective-permute-done((bf16[96,1152]{1,0:T(8,128)(2,1)S(1)}, bf16[96,1152]{1,0:T(8,128)(2,1)S(1)}, u32[]{:S(2)}, u32[]{:S(2)}) %collective-permute-start.8) | collective-permute-done | bytes 221216 | tf_op jit(solution)/shard_map/ppermute | solution.py:413
  28.1 5.9 %collective-permute-done.3 = bf16[96,1152]{1,0:T(8,128)(2,1)S(1)} collective-permute-done((bf16[96,1152]{1,0:T(8,128)(2,1)S(1)}, bf16[96,1152]{1,0:T(8,128)(2,1)S(1)}, u32[]{:S(2)}, u32[]{:S(2)}) %collective-permute-start.3) | collective-permute-done | bytes 221216 | tf_op jit(solution)/shard_map/ppermute | solution.py:413
  34.1 11.9 %all_to_all.10.in_ref = bf16[4,24,1152]{2,1,0:T(8,128)(2,1)S(1)} all-to-all(bf16[4,24,1152]{2,1,0:T(8,128)(2,1)S(1)} %bitcast.8), channel_id=1, replica_groups={{48,32,16,0},{52,36,20,4},{56,40,24,8},{60,44,28,12},{112,96,80,64},{11..., dimensions={0} | all-to-all | bytes 442368 | tf_op jit(solution)/shard_map/all_to_all | solution.py:61
  46.1 16.9 %all_to_all.11 = bf16[8,24,1152]{2,1,0:T(8,128)(2,1)S(1)} all-to-all(bf16[8,24,1152]{2,1,0:T(8,128)(2,1)S(1)} %sum_and_spread.1), channel_id=1, replica_groups={{48,32,16,0,56,40,24,8},{52,36,20,4,60,44,28,12},{112,96,80,64,120,104,..., dimensions={0} | all-to-all | bytes 884736 | tf_op jit(solution)/shard_map/all_to_all | solution.py:61
  63.2 2.7 %collective-permute-start.10 = (bf16[96,1152]{1,0:T(8,128)(2,1)S(1)}, bf16[96,1152]{1,0:T(8,128)(2,1)S(1)}, u32[]{:S(2)}, u32[]{:S(2)}) collective-permute-start(bf16[96,1152]{1,0:T(8,128)(2,1)S(1)} %bitcast.9), channel_id=1, source_target_pairs={{0,192},{4,196},{8,200},{12,204},{16,208},{20,212},{24,216},{28,22... | collective-permute-start | bytes 663560 | tf_op jit(solution)/shard_map/ppermute | solution.py:413
  67.4 1.9 %collective-permute-done.11.rest_4_ = bf16[96,1152]{1,0:T(8,128)(2,1)S(1)} collective-permute-done((bf16[96,1152]{1,0:T(8,128)(2,1)S(1)}, bf16[96,1152]{1,0:T(8,128)(2,1)S(1)}, u32[]{:S(2)}, u32[]{:S(2)}) %collective-permute-start.11) | collective-permute-done | bytes 221216 | tf_op jit(solution)/shard_map/ppermute | solution.py:413
  69.2 2.7 %collective-permute-start.13 = (bf16[96,1152]{1,0:T(8,128)(2,1)S(1)}, bf16[96,1152]{1,0:T(8,128)(2,1)S(1)}, u32[]{:S(2)}, u32[]{:S(2)}) collective-permute-start(bf16[96,1152]{1,0:T(8,128)(2,1)S(1)} %collective-permute-done.10.rest_1_), channel_id=1, source_target_pairs={{0,192},{4,196},{8,200},{12,204},{16,208},{20,212},{24,216},{28,22... | collective-permute-start | bytes 663560 | tf_op jit(solution)/shard_map/ppermute | solution.py:413
  72.8 2.1 %collective-permute-done.14.rest_5_ = bf16[96,1152]{1,0:T(8,128)(2,1)S(1)} collective-permute-done((bf16[96,1152]{1,0:T(8,128)(2,1)S(1)}, bf16[96,1152]{1,0:T(8,128)(2,1)S(1)}, u32[]{:S(2)}, u32[]{:S(2)}) %collective-permute-start.14) | collective-permute-done | bytes 221216 | tf_op jit(solution)/shard_map/ppermute | solution.py:413
  74.8 4.7 %collective-permute-done.12.rest_2_ = bf16[96,1152]{1,0:T(8,128)(2,1)S(1)} collective-permute-done((bf16[96,1152]{1,0:T(8,128)(2,1)S(1)}, bf16[96,1152]{1,0:T(8,128)(2,1)S(1)}, u32[]{:S(2)}, u32[]{:S(2)}) %collective-permute-start.12) | collective-permute-done | bytes 221216 | tf_op jit(solution)/shard_map/ppermute | solution.py:413
  79.7 3.2 %collective-permute-start.17 = (bf16[768,384]{1,0:T(8,128)(2,1)S(1)}, bf16[768,384]{1,0:T(8,128)(2,1)S(1)}, u32[]{:S(2)}, u32[]{:S(2)}) collective-permute-start(bf16[768,384]{1,0:T(8,128)(2,1)S(1)} %get-tuple-element.45.a_ref), channel_id=1, source_target_pairs={{0,4},{4,0},{8,12},{12,8},{16,20},{20,16},{24,28},{28,24},{32,36},... | collective-permute-start | bytes 1769480 | tf_op jit(solution)/shard_map/ppermute | solution.py:57
  82.9 4.8 %own_step.1 = (bf16[384,768]{1,0:T(8,128)(2,1)S(1)}, bf16[384,768]{1,0:T(8,128)(2,1)S(1)}) custom-call(bf16[768,768]{1,0:T(8,128)(2,1)S(1)} %get-tuple-element.42.x_ref, bf16[1,3,768,768]{3,2,1,0:T(8,128)(2,1)S(1)} %copy-done.1), custom_call_target="tpu_custom_call" | custom-call | flops 4529848320 | bytes 3538944 | tf_op jit(solution)/shard_map/own_step/pallas_call | solution.py:324
  88.3 4.8 %shared_step.1.shared_ref = bf16[768,768]{1,0:T(8,128)(2,1)S(1)} custom-call(bf16[768,384]{1,0:T(8,128)(2,1)S(1)} %get-tuple-element.45.a_ref, bf16[768,384]{1,0:T(8,128)(2,1)S(1)} %collective-permute-done.17.b_ref, bf16[1,3,768,768]{3,2,1,0:T(8,128)(2,1)S(1)} %copy-done.1), custom_call_target="tpu_custom_call" | custom-call | flops 4529848320 | bytes 3538944 | tf_op jit(solution)/shard_map/shared_step/pallas_call | solution.py:346
  93.1 2.7 %project.1 = (f32[256,768]{1,0:T(8,128)S(1)}, bf16[128,768]{1,0:T(8,128)(2,1)S(1)}, bf16[128,768]{1,0:T(8,128)(2,1)S(1)}, bf16[128,768]{1,0:T(8,128)(2,1)S(1)}, ...) custom-call(bf16[256,768]{1,0:T(8,128)(2,1)S(1)} %copy-done, ...), custom_call_target="tpu_custom_call" | custom-call | flops 2113929216 | bytes 9437184 | tf_op jit(solution)/shard_map/project/pallas_call | solution.py:384
  97.1 1.5 %collective-permute-start.20 = (bf16[128,768]{1,0:T(8,128)(2,1)S(1)}, bf16[128,768]{1,0:T(8,128)(2,1)S(1)}, u32[]{:S(2)}, u32[]{:S(2)}) collective-permute-start(bf16[128,768]{1,0:T(8,128)(2,1)S(1)} %get-tuple-element.49), channel_id=1, source_target_pairs={{0,3},{1,0},{2,1},{3,2},{4,7},{5,4},{6,5},{7,6},{8,11},{9,8},{10,9... | collective-permute-start | bytes 589832 | tf_op jit(solution)/shard_map/ppermute | solution.py:413
  100.1 3.2 %collective-permute-done.18 = bf16[128,768]{1,0:T(8,128)(2,1)S(1)} collective-permute-done((bf16[128,768]{1,0:T(8,128)(2,1)S(1)}, bf16[128,768]{1,0:T(8,128)(2,1)S(1)}, u32[]{:S(2)}, u32[]{:S(2)}) %collective-permute-start.18) | collective-permute-done | bytes 196640 | tf_op jit(solution)/shard_map/ppermute | solution.py:413
  103.5 2.7 %collective-permute-start.21 = (bf16[128,768]{1,0:T(8,128)(2,1)S(1)}, bf16[128,768]{1,0:T(8,128)(2,1)S(1)}, u32[]{:S(2)}, u32[]{:S(2)}) collective-permute-start(bf16[128,768]{1,0:T(8,128)(2,1)S(1)} %add_convert_fusion.3), channel_id=1, source_target_pairs={{0,3},{1,0},{2,1},{3,2},{4,7},{5,4},{6,5},{7,6},{8,11},{9,8},{10,9... | collective-permute-start | bytes 589832 | tf_op jit(solution)/shard_map/ppermute | solution.py:413
  107.1 4.3 %collective-permute-done.19.sum_a_ref = bf16[128,768]{1,0:T(8,128)(2,1)S(1)} collective-permute-done((bf16[128,768]{1,0:T(8,128)(2,1)S(1)}, bf16[128,768]{1,0:T(8,128)(2,1)S(1)}, u32[]{:S(2)}, u32[]{:S(2)}) %collective-permute-start.19) | collective-permute-done | bytes 196640 | tf_op jit(solution)/shard_map/ppermute | solution.py:413
  (54 shorter events, 13.2 us)
Async XLA Ops:
  7.0 6.9 %collective-permute-start = (bf16[768,768]{1,0:T(8,128)(2,1)}, bf16[768,768]{1,0:T(8,128)(2,1)S(1)}, u32[]{:S(2)}, u32[]{:S(2)}) collective-permute-start(bf16[768,768]{1,0:T(8,128)(2,1)} %get-tuple-element.31), channel_id=1, source_target_pairs={{0,4},{4,0},{8,12},{12,8},{16,20},{20,16},{24,28},{28,24},{32,36},... | collective-permute-start | bytes 3538952 | tf_op jit(solution)/shard_map/ppermute | solution.py:57
  10.4 3.5 %collective-permute-start.1 = (bf16[768,384]{1,0:T(8,128)(2,1)}, bf16[768,384]{1,0:T(8,128)(2,1)S(1)}, u32[]{:S(2)}, u32[]{:S(2)}) collective-permute-start(bf16[768,384]{1,0:T(8,128)(2,1)} %get-tuple-element.33), channel_id=1, source_target_pairs={{0,4},{4,0},{8,12},{12,8},{16,20},{20,16},{24,28},{28,24},{32,36},... | collective-permute-start | bytes 1769480 | tf_op jit(solution)/shard_map/ppermute | solution.py:57
  14.2 7.9 %collective-permute-start.2 = (bf16[96,1152]{1,0:T(8,128)(2,1)S(1)}, bf16[96,1152]{1,0:T(8,128)(2,1)S(1)}, u32[]{:S(2)}, u32[]{:S(2)}) collective-permute-start(bf16[96,1152]{1,0:T(8,128)(2,1)S(1)} %get-tuple-element.35), channel_id=1, source_target_pairs={{0,64},{4,68},{8,72},{12,76},{16,80},{20,84},{24,88},{28,92},{32,9... | collective-permute-start | bytes 663560 | tf_op jit(solution)/shard_map/ppermute | solution.py:413
  14.3 8.0 %collective-permute-start.4 = (bf16[96,1152]{1,0:T(8,128)(2,1)S(1)}, bf16[96,1152]{1,0:T(8,128)(2,1)S(1)}, u32[]{:S(2)}, u32[]{:S(2)}) collective-permute-start(bf16[96,1152]{1,0:T(8,128)(2,1)S(1)} %get-tuple-element.37), channel_id=1, source_target_pairs={{0,192},{4,196},{8,200},{12,204},{16,208},{20,212},{24,216},{28,22... | collective-permute-start | bytes 663560 | tf_op jit(solution)/shard_map/ppermute | solution.py:413
  17.0 8.9 %collective-permute-start.6 = (bf16[96,1152]{1,0:T(8,128)(2,1)S(1)}, bf16[96,1152]{1,0:T(8,128)(2,1)S(1)}, u32[]{:S(2)}, u32[]{:S(2)}) collective-permute-start(bf16[96,1152]{1,0:T(8,128)(2,1)S(1)} %get-tuple-element.38), channel_id=1, source_target_pairs={{0,192},{4,196},{8,200},{12,204},{16,208},{20,212},{24,216},{28,22... | collective-permute-start | bytes 663560 | tf_op jit(solution)/shard_map/ppermute | solution.py:413
  17.0 8.8 %collective-permute-start.7 = (bf16[96,1152]{1,0:T(8,128)(2,1)S(1)}, bf16[96,1152]{1,0:T(8,128)(2,1)S(1)}, u32[]{:S(2)}, u32[]{:S(2)}) collective-permute-start(bf16[96,1152]{1,0:T(8,128)(2,1)S(1)} %get-tuple-element.39), channel_id=1, source_target_pairs={{0,8},{4,12},{8,0},{12,4},{16,24},{20,28},{24,16},{28,20},{32,40},... | collective-permute-start | bytes 663560 | tf_op jit(solution)/shard_map/ppermute | solution.py:413
  18.4 9.7 %collective-permute-start.8 = (bf16[96,1152]{1,0:T(8,128)(2,1)S(1)}, bf16[96,1152]{1,0:T(8,128)(2,1)S(1)}, u32[]{:S(2)}, u32[]{:S(2)}) collective-permute-start(bf16[96,1152]{1,0:T(8,128)(2,1)S(1)} %get-tuple-element.40), channel_id=1, source_target_pairs={{0,72},{4,76},{8,64},{12,68},{16,88},{20,92},{24,80},{28,84},{32,1... | collective-permute-start | bytes 663560 | tf_op jit(solution)/shard_map/ppermute | solution.py:413
  22.2 11.7 %collective-permute-start.3 = (bf16[96,1152]{1,0:T(8,128)(2,1)S(1)}, bf16[96,1152]{1,0:T(8,128)(2,1)S(1)}, u32[]{:S(2)}, u32[]{:S(2)}) collective-permute-start(bf16[96,1152]{1,0:T(8,128)(2,1)S(1)} %add_convert_fusion.2), channel_id=1, source_target_pairs={{0,64},{4,68},{8,72},{12,76},{16,80},{20,84},{24,88},{28,92},{32,9... | collective-permute-start | bytes 663560 | tf_op jit(solution)/shard_map/ppermute | solution.py:413
  22.4 11.6 %collective-permute-start.5 = (bf16[96,1152]{1,0:T(8,128)(2,1)S(1)}, bf16[96,1152]{1,0:T(8,128)(2,1)S(1)}, u32[]{:S(2)}, u32[]{:S(2)}) collective-permute-start(bf16[96,1152]{1,0:T(8,128)(2,1)S(1)} %add_convert_fusion.1), channel_id=1, source_target_pairs={{0,200},{4,204},{8,192},{12,196},{16,216},{20,220},{24,208},{28,21... | collective-permute-start | bytes 663560 | tf_op jit(solution)/shard_map/ppermute | solution.py:413
  63.0 6.3 %collective-permute-start.11 = (bf16[96,1152]{1,0:T(8,128)(2,1)S(1)}, bf16[96,1152]{1,0:T(8,128)(2,1)S(1)}, u32[]{:S(2)}, u32[]{:S(2)}) collective-permute-start(bf16[96,1152]{1,0:T(8,128)(2,1)S(1)} %bitcast.11), channel_id=1, source_target_pairs={{0,64},{4,68},{8,72},{12,76},{16,80},{20,84},{24,88},{28,92},{32,9... | collective-permute-start | bytes 663560 | tf_op jit(solution)/shard_map/ppermute | solution.py:413
  63.2 6.0 %collective-permute-start.10 = (bf16[96,1152]{1,0:T(8,128)(2,1)S(1)}, bf16[96,1152]{1,0:T(8,128)(2,1)S(1)}, u32[]{:S(2)}, u32[]{:S(2)}) collective-permute-start(bf16[96,1152]{1,0:T(8,128)(2,1)S(1)} %bitcast.9), channel_id=1, source_target_pairs={{0,192},{4,196},{8,200},{12,204},{16,208},{20,212},{24,216},{28,22... | collective-permute-start | bytes 663560 | tf_op jit(solution)/shard_map/ppermute | solution.py:413
  65.9 6.9 %collective-permute-start.9 = (bf16[96,1152]{1,0:T(8,128)(2,1)S(1)}, bf16[96,1152]{1,0:T(8,128)(2,1)S(1)}, u32[]{:S(2)}, u32[]{:S(2)}) collective-permute-start(bf16[96,1152]{1,0:T(8,128)(2,1)S(1)} %bitcast.12), channel_id=1, source_target_pairs={{0,192},{4,196},{8,200},{12,204},{16,208},{20,212},{24,216},{28,22... | collective-permute-start | bytes 663560 | tf_op jit(solution)/shard_map/ppermute | solution.py:413
  66.3 8.5 %collective-permute-start.14 = (bf16[96,1152]{1,0:T(8,128)(2,1)S(1)}, bf16[96,1152]{1,0:T(8,128)(2,1)S(1)}, u32[]{:S(2)}, u32[]{:S(2)}) collective-permute-start(bf16[96,1152]{1,0:T(8,128)(2,1)S(1)} %bitcast.10), channel_id=1, source_target_pairs={{0,64},{4,68},{8,72},{12,76},{16,80},{20,84},{24,88},{28,92},{32,9... | collective-permute-start | bytes 663560 | tf_op jit(solution)/shard_map/ppermute | solution.py:413
  69.2 10.4 %collective-permute-start.12 = (bf16[96,1152]{1,0:T(8,128)(2,1)S(1)}, bf16[96,1152]{1,0:T(8,128)(2,1)S(1)}, u32[]{:S(2)}, u32[]{:S(2)}) collective-permute-start(bf16[96,1152]{1,0:T(8,128)(2,1)S(1)} %collective-permute-done.11.rest_4_), channel_id=1, source_target_pairs={{0,64},{4,68},{8,72},{12,76},{16,80},{20,84},{24,88},{28,92},{32,9... | collective-permute-start | bytes 663560 | tf_op jit(solution)/shard_map/ppermute | solution.py:413
  69.2 10.4 %collective-permute-start.13 = (bf16[96,1152]{1,0:T(8,128)(2,1)S(1)}, bf16[96,1152]{1,0:T(8,128)(2,1)S(1)}, u32[]{:S(2)}, u32[]{:S(2)}) collective-permute-start(bf16[96,1152]{1,0:T(8,128)(2,1)S(1)} %collective-permute-done.10.rest_1_), channel_id=1, source_target_pairs={{0,192},{4,196},{8,200},{12,204},{16,208},{20,212},{24,216},{28,22... | collective-permute-start | bytes 663560 | tf_op jit(solution)/shard_map/ppermute | solution.py:413
  79.7 8.6 %collective-permute-start.17 = (bf16[768,384]{1,0:T(8,128)(2,1)S(1)}, bf16[768,384]{1,0:T(8,128)(2,1)S(1)}, u32[]{:S(2)}, u32[]{:S(2)}) collective-permute-start(bf16[768,384]{1,0:T(8,128)(2,1)S(1)} %get-tuple-element.45.a_ref), channel_id=1, source_target_pairs={{0,4},{4,0},{8,12},{12,8},{16,20},{20,16},{24,28},{28,24},{32,36},... | collective-permute-start | bytes 1769480 | tf_op jit(solution)/shard_map/ppermute | solution.py:57
  87.7 5.4 %collective-permute-start.15 = (bf16[384,768]{1,0:T(8,128)(2,1)S(1)}, bf16[384,768]{1,0:T(8,128)(2,1)S(1)}, u32[]{:S(2)}, u32[]{:S(2)}) collective-permute-start(bf16[384,768]{1,0:T(8,128)(2,1)S(1)} %get-tuple-element.43.own_a), channel_id=1, source_target_pairs={{0,4},{4,0},{8,12},{12,8},{16,20},{20,16},{24,28},{28,24},{32,36},... | collective-permute-start | bytes 1769480 | tf_op jit(solution)/shard_map/ppermute | solution.py:57
  87.8 5.3 %collective-permute-start.16 = (bf16[384,768]{1,0:T(8,128)(2,1)S(1)}, bf16[384,768]{1,0:T(8,128)(2,1)S(1)}, u32[]{:S(2)}, u32[]{:S(2)}) collective-permute-start(bf16[384,768]{1,0:T(8,128)(2,1)S(1)} %get-tuple-element.44.own_b), channel_id=1, source_target_pairs={{0,4},{4,0},{8,12},{12,8},{16,20},{20,16},{24,28},{28,24},{32,36},... | collective-permute-start | bytes 1769480 | tf_op jit(solution)/shard_map/ppermute | solution.py:57
  95.8 7.4 %collective-permute-start.18 = (bf16[128,768]{1,0:T(8,128)(2,1)S(1)}, bf16[128,768]{1,0:T(8,128)(2,1)S(1)}, u32[]{:S(2)}, u32[]{:S(2)}) collective-permute-start(bf16[128,768]{1,0:T(8,128)(2,1)S(1)} %get-tuple-element.47), channel_id=1, source_target_pairs={{0,1},{1,2},{2,3},{3,0},{4,5},{5,6},{6,7},{7,4},{8,9},{9,10},{10,1... | collective-permute-start | bytes 589832 | tf_op jit(solution)/shard_map/ppermute | solution.py:413
  97.1 6.3 %collective-permute-start.20 = (bf16[128,768]{1,0:T(8,128)(2,1)S(1)}, bf16[128,768]{1,0:T(8,128)(2,1)S(1)}, u32[]{:S(2)}, u32[]{:S(2)}) collective-permute-start(bf16[128,768]{1,0:T(8,128)(2,1)S(1)} %get-tuple-element.49), channel_id=1, source_target_pairs={{0,3},{1,0},{2,1},{3,2},{4,7},{5,4},{6,5},{7,6},{8,11},{9,8},{10,9... | collective-permute-start | bytes 589832 | tf_op jit(solution)/shard_map/ppermute | solution.py:413
  98.6 8.6 %collective-permute-start.22 = (bf16[128,768]{1,0:T(8,128)(2,1)S(1)}, bf16[128,768]{1,0:T(8,128)(2,1)S(1)}, u32[]{:S(2)}, u32[]{:S(2)}) collective-permute-start(bf16[128,768]{1,0:T(8,128)(2,1)S(1)} %get-tuple-element.50), channel_id=1, source_target_pairs={{0,3},{1,0},{2,1},{3,2},{4,7},{5,4},{6,5},{7,6},{8,11},{9,8},{10,9... | collective-permute-start | bytes 589832 | tf_op jit(solution)/shard_map/ppermute | solution.py:413
  99.8 7.3 %collective-permute-start.23 = (bf16[128,768]{1,0:T(8,128)(2,1)S(1)}, bf16[128,768]{1,0:T(8,128)(2,1)S(1)}, u32[]{:S(2)}, u32[]{:S(2)}) collective-permute-start(bf16[128,768]{1,0:T(8,128)(2,1)S(1)} %get-tuple-element.51), channel_id=1, source_target_pairs={{0,1},{1,2},{2,3},{3,0},{4,5},{5,6},{6,7},{7,4},{8,9},{9,10},{10,1... | collective-permute-start | bytes 589832 | tf_op jit(solution)/shard_map/ppermute | solution.py:413
  103.3 8.2 %collective-permute-start.19 = (bf16[128,768]{1,0:T(8,128)(2,1)S(1)}, bf16[128,768]{1,0:T(8,128)(2,1)S(1)}, u32[]{:S(2)}, u32[]{:S(2)}) collective-permute-start(bf16[128,768]{1,0:T(8,128)(2,1)S(1)} %add_convert_fusion.4), channel_id=1, source_target_pairs={{0,1},{1,2},{2,3},{3,0},{4,5},{5,6},{6,7},{7,4},{8,9},{9,10},{10,1... | collective-permute-start | bytes 589832 | tf_op jit(solution)/shard_map/ppermute | solution.py:413
  103.5 8.0 %collective-permute-start.21 = (bf16[128,768]{1,0:T(8,128)(2,1)S(1)}, bf16[128,768]{1,0:T(8,128)(2,1)S(1)}, u32[]{:S(2)}, u32[]{:S(2)}) collective-permute-start(bf16[128,768]{1,0:T(8,128)(2,1)S(1)} %add_convert_fusion.3), channel_id=1, source_target_pairs={{0,3},{1,0},{2,1},{3,2},{4,7},{5,4},{6,5},{7,6},{8,11},{9,8},{10,9... | collective-permute-start | bytes 589832 | tf_op jit(solution)/shard_map/ppermute | solution.py:413
  (6 other events, 64.8 us)

commit v9 on v8

--- a/solution.py
+++ b/solution.py
@@ -355,13 +355,20 @@
     )(mine, partners, weights)
 
 
-def project(queries, own, other, shared, out_proj):
+def projected(outputs, p_ref, step, heads):
+    width = p_ref.shape[0]
+    head = lax.rem(lax.axis_index("head") + step, heads)
+    start = pl.multiple_of(head * width, width)
+    return dot(outputs, p_ref[:, pl.ds(start, width)])
+
+
+def target_outputs(queries, own, other, shared, out_proj):
     tokens, width = queries.shape
     heads = out_proj.shape[1] // width
-
     half = width // 2
-
-    def body(q_ref, own_a, own_b, other_a, other_b, shared_ref, p_ref, *outs):
+    cut = tokens // 2
+
+    def body(q_ref, own_a, own_b, other_a, other_b, shared_ref, p_ref, out, far_a, far_b):
         first = own_core() == 0
         left, right = q_ref[:, :half], q_ref[:, half:]
         q_own = dot(left, own_a[...]) + dot(right, own_b[...])
@@ -370,27 +377,45 @@
         q3 = jnp.where(first, q_other, q_own)
         gated = (q1 * sigmoid(q1) * q3).astype(bf16)
         outputs = dot(gated, shared_ref[...]).astype(bf16)
-        cut = tokens // 2
-        for step in range(heads):
-            head = lax.rem(lax.axis_index("head") + step, heads)
-            start = pl.multiple_of(head * width, width)
-            product = dot(outputs, p_ref[:, pl.ds(start, width)])
-            if step == 0:
-                outs[0][...] = product
-            else:
-                outs[2 * step - 1][...] = product[:cut].astype(bf16)
-                outs[2 * step][...] = product[cut:].astype(bf16)
-
-    return call(
-        body,
-        [shape(tokens, width, dtype=f32)] + [shape(tokens // 2, width)] * (2 * heads - 2),
+        out[...] = outputs
+        product = projected(outputs, p_ref, 2, heads).astype(bf16)
+        far_a[...] = product[:cut]
+        far_b[...] = product[cut:]
+
+    return call(
+        body,
+        [shape(tokens, width), shape(cut, width), shape(cut, width)],
         [VMEM] * 7,
         [],
         20,
-        2 * tokens * width * width * (3 + heads),
+        8 * tokens * width * width,
         16 * width * width,
-        "project",
+        "target_outputs",
     )(queries, *own, *other, shared, out_proj)
+
+
+def project_near(outputs, out_proj):
+    tokens, width = outputs.shape
+    heads = out_proj.shape[1] // width
+    cut = tokens // 2
+
+    def body(o_ref, p_ref, mine, next_a, next_b, previous_a, previous_b):
+        for step, top, bottom in ((1, next_a, next_b), (3, previous_a, previous_b)):
+            product = projected(o_ref[...], p_ref, step, heads).astype(bf16)
+            top[...] = product[:cut]
+            bottom[...] = product[cut:]
+        mine[...] = projected(o_ref[...], p_ref, 0, heads)
+
+    return call(
+        body,
+        [shape(tokens, width, dtype=f32)] + [shape(cut, width)] * 4,
+        [VMEM] * 2,
+        [],
+        16,
+        6 * tokens * width * width,
+        8 * width * width,
+        "project_near",
+    )(outputs, out_proj)
 
 
 def mix(own, sum_a, sum_b, direct_a, direct_b):
@@ -488,7 +513,11 @@
     other_fresh = [swap_cores(rows) for rows in own_fresh]
     shared_fresh = shared_step(shared_part, shared_other, fast_weights)
 
-    mixed, *shares = project(queries, own_fresh, other_fresh, shared_fresh, out_proj)
+    outputs, far_a, far_b = target_outputs(
+        queries, own_fresh, other_fresh, shared_fresh, out_proj
+    )
+    mixed, next_a, next_b, previous_a, previous_b = project_near(outputs, out_proj)
+    shares = [next_a, next_b, far_a, far_b, previous_a, previous_b]
     up = [(i, (i + 1) % heads) for i in range(heads)]
     down = [(i, (i - 1) % heads) for i in range(heads)]
     return mix(mixed, *ring_sum(shares, "head", up, down))

time: 113 us -> 114 us (level)
  starting transfers between devices: 29.2 us -> 31.1 us
    ppermute x19, starting transfers between devices: 22.1 us -> 23.9 us  [shift(): return lax.ppermute(array, axis, pairs)]
    pallas_call x1 -> x2, Pallas kernels: 2.69 us -> 2.91 us  [the longest x1 1.8 us: target_outputs(): call(body, [shape(tokens, width), shape(cut, width), shape(cut, width)],...]
  transfers between devices with their start and end apart: 24 -> 24, of which waited for: 12 -> 14; matrix products, arithmetic and copies ran while one was open for 0% -> 0% of each run, Pallas kernels for 10% -> 10%
where the time goes in v9:
time: 114 us; the launch traced here: 113 us
  starting transfers between devices  31.1 us (27%)
  waiting for transfers between devices  29.4 us (26%)
  blocking collectives  28.7 us (25%)
  Pallas kernels  22 us (19%)
  local copies, waits for them, and re-layouts  1.61 us (1%)
    all_to_all x2, blocking collectives, exchange(): return lax.all_to_all(blocks, 'tok', 0, 0, axis_index_groups=groups)  28.7 us
    ppermute x19, waiting for transfers between devices, shift(): return lax.ppermute(array, axis, pairs)  28.7 us
    ppermute x19, starting transfers between devices, shift(): return lax.ppermute(array, axis, pairs)  23.9 us
    ppermute x5, starting transfers between devices, swap_cores(): return lax.ppermute(array, 'tok', CORE_SWAP)  7.2 us
    pallas_call x1, Pallas kernels, gradients(): call(body, [shape(*dims) for dims in results], [VMEM] + [HBM] * 3, [wide,...  7.01 us
    pallas_call x1, Pallas kernels, shared_step(): call(body, shape(width, width), [VMEM] * 3, [pltpu.VMEM((width, width), b...  4.77 us
    pallas_call x1, Pallas kernels, own_step(): call(body, [shape(width // 2, width)] * 2, [VMEM] * 2, [pltpu.VMEM((width...  4.69 us
  transfers between devices with their start and end apart: 24, of which 14 were waited for; matrix products, arithmetic and copies ran while one was open for 0% of the time, Pallas kernels for 10%

profile of v9, /device:TPU:1, one launch (start us, length us, event | category | flops | bytes accessed | tf_op | source)
XLA Modules:
  0.0 113.5 jit_solution(4084178915418964813)
XLA Ops:
  0.0 7.0 %gradients.1 = (bf16[768,768]{1,0:T(8,128)(2,1)}, bf16[768,384]{1,0:T(8,128)(2,1)}, bf16[512,1920]{1,0:T(8,128)(2,1)}) custom-call(f32[4,128]{1,0:T(4,128)} %bitcast.13, bf16[512,768]{1,0:T(8,128)(2,1)} %k_ref.1, bf16[512,768]{1,0:T(8,128)(2,1)} %v_hbm.1, bf16[1,3,768,768]{3,2,1,0:T(8,128)(2,1)} %w_ref.3), custom_call_target="tpu_custom_call" | custom-call | flops 2717908992 | bytes 7077888 | tf_op jit(solution)/shard_map/gradients/pallas_call | solution.py:180
  7.0 3.3 %collective-permute-start = (bf16[768,768]{1,0:T(8,128)(2,1)}, bf16[768,768]{1,0:T(8,128)(2,1)S(1)}, u32[]{:S(2)}, u32[]{:S(2)}) collective-permute-start(bf16[768,768]{1,0:T(8,128)(2,1)} %get-tuple-element.32), channel_id=1, source_target_pairs={{0,4},{4,0},{8,12},{12,8},{16,20},{20,16},{24,28},{28,24},{32,36},... | collective-permute-start | bytes 3538952 | tf_op jit(solution)/shard_map/ppermute | solution.py:57
  10.5 1.5 %copy-done.3 = bf16[512,1920]{1,0:T(8,128)(2,1)S(1)} copy-done((bf16[512,1920]{1,0:T(8,128)(2,1)S(1)}, bf16[512,1920]{1,0:T(8,128)(2,1)}, u32[]{:S(2)}) %copy-start.3) | copy-done | bytes 1966104
  14.3 2.7 %collective-permute-start.4 = (bf16[96,1152]{1,0:T(8,128)(2,1)S(1)}, bf16[96,1152]{1,0:T(8,128)(2,1)S(1)}, u32[]{:S(2)}, u32[]{:S(2)}) collective-permute-start(bf16[96,1152]{1,0:T(8,128)(2,1)S(1)} %get-tuple-element.38), channel_id=1, source_target_pairs={{0,192},{4,196},{8,200},{12,204},{16,208},{20,212},{24,216},{28,22... | collective-permute-start | bytes 663560 | tf_op jit(solution)/shard_map/ppermute | solution.py:438
  19.6 2.5 %collective-permute-done.2 = bf16[96,1152]{1,0:T(8,128)(2,1)S(1)} collective-permute-done((bf16[96,1152]{1,0:T(8,128)(2,1)S(1)}, bf16[96,1152]{1,0:T(8,128)(2,1)S(1)}, u32[]{:S(2)}, u32[]{:S(2)}) %collective-permute-start.2) | collective-permute-done | bytes 221216 | tf_op jit(solution)/shard_map/ppermute | solution.py:438
  22.4 2.5 %collective-permute-start.5 = (bf16[96,1152]{1,0:T(8,128)(2,1)S(1)}, bf16[96,1152]{1,0:T(8,128)(2,1)S(1)}, u32[]{:S(2)}, u32[]{:S(2)}) collective-permute-start(bf16[96,1152]{1,0:T(8,128)(2,1)S(1)} %add_convert_fusion.1), channel_id=1, source_target_pairs={{0,200},{4,204},{8,192},{12,196},{16,216},{20,220},{24,208},{28,21... | collective-permute-start | bytes 663560 | tf_op jit(solution)/shard_map/ppermute | solution.py:438
  25.8 2.2 %collective-permute-done.8 = bf16[96,1152]{1,0:T(8,128)(2,1)S(1)} collective-permute-done((bf16[96,1152]{1,0:T(8,128)(2,1)S(1)}, bf16[96,1152]{1,0:T(8,128)(2,1)S(1)}, u32[]{:S(2)}, u32[]{:S(2)}) %collective-permute-start.8) | collective-permute-done | bytes 221216 | tf_op jit(solution)/shard_map/ppermute | solution.py:438
  28.1 5.9 %collective-permute-done.3 = bf16[96,1152]{1,0:T(8,128)(2,1)S(1)} collective-permute-done((bf16[96,1152]{1,0:T(8,128)(2,1)S(1)}, bf16[96,1152]{1,0:T(8,128)(2,1)S(1)}, u32[]{:S(2)}, u32[]{:S(2)}) %collective-permute-start.3) | collective-permute-done | bytes 221216 | tf_op jit(solution)/shard_map/ppermute | solution.py:438
  34.1 11.9 %all_to_all.10.in_ref = bf16[4,24,1152]{2,1,0:T(8,128)(2,1)S(1)} all-to-all(bf16[4,24,1152]{2,1,0:T(8,128)(2,1)S(1)} %bitcast.8), channel_id=1, replica_groups={{48,32,16,0},{52,36,20,4},{56,40,24,8},{60,44,28,12},{112,96,80,64},{11..., dimensions={0} | all-to-all | bytes 442368 | tf_op jit(solution)/shard_map/all_to_all | solution.py:61
  46.0 16.9 %all_to_all.11 = bf16[8,24,1152]{2,1,0:T(8,128)(2,1)S(1)} all-to-all(bf16[8,24,1152]{2,1,0:T(8,128)(2,1)S(1)} %sum_and_spread.1), channel_id=1, replica_groups={{48,32,16,0,56,40,24,8},{52,36,20,4,60,44,28,12},{112,96,80,64,120,104,..., dimensions={0} | all-to-all | bytes 884736 | tf_op jit(solution)/shard_map/all_to_all | solution.py:61
  63.2 2.7 %collective-permute-start.10 = (bf16[96,1152]{1,0:T(8,128)(2,1)S(1)}, bf16[96,1152]{1,0:T(8,128)(2,1)S(1)}, u32[]{:S(2)}, u32[]{:S(2)}) collective-permute-start(bf16[96,1152]{1,0:T(8,128)(2,1)S(1)} %bitcast.9), channel_id=1, source_target_pairs={{0,192},{4,196},{8,200},{12,204},{16,208},{20,212},{24,216},{28,22... | collective-permute-start | bytes 663560 | tf_op jit(solution)/shard_map/ppermute | solution.py:438
  67.4 1.9 %collective-permute-done.11.rest_4_ = bf16[96,1152]{1,0:T(8,128)(2,1)S(1)} collective-permute-done((bf16[96,1152]{1,0:T(8,128)(2,1)S(1)}, bf16[96,1152]{1,0:T(8,128)(2,1)S(1)}, u32[]{:S(2)}, u32[]{:S(2)}) %collective-permute-start.11) | collective-permute-done | bytes 221216 | tf_op jit(solution)/shard_map/ppermute | solution.py:438
  69.2 2.7 %collective-permute-start.13 = (bf16[96,1152]{1,0:T(8,128)(2,1)S(1)}, bf16[96,1152]{1,0:T(8,128)(2,1)S(1)}, u32[]{:S(2)}, u32[]{:S(2)}) collective-permute-start(bf16[96,1152]{1,0:T(8,128)(2,1)S(1)} %collective-permute-done.10.rest_1_), channel_id=1, source_target_pairs={{0,192},{4,196},{8,200},{12,204},{16,208},{20,212},{24,216},{28,22... | collective-permute-start | bytes 663560 | tf_op jit(solution)/shard_map/ppermute | solution.py:438
  72.8 2.1 %collective-permute-done.14.rest_5_ = bf16[96,1152]{1,0:T(8,128)(2,1)S(1)} collective-permute-done((bf16[96,1152]{1,0:T(8,128)(2,1)S(1)}, bf16[96,1152]{1,0:T(8,128)(2,1)S(1)}, u32[]{:S(2)}, u32[]{:S(2)}) %collective-permute-start.14) | collective-permute-done | bytes 221216 | tf_op jit(solution)/shard_map/ppermute | solution.py:438
  74.8 4.7 %collective-permute-done.12.rest_2_ = bf16[96,1152]{1,0:T(8,128)(2,1)S(1)} collective-permute-done((bf16[96,1152]{1,0:T(8,128)(2,1)S(1)}, bf16[96,1152]{1,0:T(8,128)(2,1)S(1)}, u32[]{:S(2)}, u32[]{:S(2)}) %collective-permute-start.12) | collective-permute-done | bytes 221216 | tf_op jit(solution)/shard_map/ppermute | solution.py:438
  79.7 3.2 %collective-permute-start.17 = (bf16[768,384]{1,0:T(8,128)(2,1)S(1)}, bf16[768,384]{1,0:T(8,128)(2,1)S(1)}, u32[]{:S(2)}, u32[]{:S(2)}) collective-permute-start(bf16[768,384]{1,0:T(8,128)(2,1)S(1)} %get-tuple-element.46.a_ref), channel_id=1, source_target_pairs={{0,4},{4,0},{8,12},{12,8},{16,20},{20,16},{24,28},{28,24},{32,36},... | collective-permute-start | bytes 1769480 | tf_op jit(solution)/shard_map/ppermute | solution.py:57
  82.9 4.7 %own_step.1 = (bf16[384,768]{1,0:T(8,128)(2,1)S(1)}, bf16[384,768]{1,0:T(8,128)(2,1)S(1)}) custom-call(bf16[768,768]{1,0:T(8,128)(2,1)S(1)} %get-tuple-element.43.x_ref, bf16[1,3,768,768]{3,2,1,0:T(8,128)(2,1)S(1)} %copy-done.1), custom_call_target="tpu_custom_call" | custom-call | flops 4529848320 | bytes 3538944 | tf_op jit(solution)/shard_map/own_step/pallas_call | solution.py:324
  88.2 4.8 %shared_step.1.shared_ref = bf16[768,768]{1,0:T(8,128)(2,1)S(1)} custom-call(bf16[768,384]{1,0:T(8,128)(2,1)S(1)} %get-tuple-element.46.a_ref, bf16[768,384]{1,0:T(8,128)(2,1)S(1)} %collective-permute-done.17.b_ref, bf16[1,3,768,768]{3,2,1,0:T(8,128)(2,1)S(1)} %copy-done.1), custom_call_target="tpu_custom_call" | custom-call | flops 4529848320 | bytes 3538944 | tf_op jit(solution)/shard_map/shared_step/pallas_call | solution.py:346
  93.0 1.8 %target_outputs.1 = (bf16[256,768]{1,0:T(8,128)(2,1)S(1)}, bf16[128,768]{1,0:T(8,128)(2,1)S(1)}, bf16[128,768]{1,0:T(8,128)(2,1)S(1)}) custom-call(bf16[256,768]{1,0:T(8,128)(2,1)S(1)} %copy-done, bf16[384,768]{1,0:T(8,128)(2,1)S(1)} %get-tuple-element.44.own_a, bf16[384,768]{1,0:T(8,128)(2,1)S(1)} %get-tuple-element.45.own_b, ...), custom_call_target="tpu_custom_call" | custom-call | flops 1207959552 | bytes 9437184 | tf_op jit(solution)/shard_map/target_outputs/pallas_call | solution.py:385
  94.8 2.5 %collective-permute-start.20 = (bf16[128,768]{1,0:T(8,128)(2,1)S(1)}, bf16[128,768]{1,0:T(8,128)(2,1)S(1)}, u32[]{:S(2)}, u32[]{:S(2)}) collective-permute-start(bf16[128,768]{1,0:T(8,128)(2,1)S(1)} %get-tuple-element.51), channel_id=1, source_target_pairs={{0,3},{1,0},{2,1},{3,2},{4,7},{5,4},{6,5},{7,6},{8,11},{9,8},{10,9... | collective-permute-start | bytes 589832 | tf_op jit(solution)/shard_map/ppermute | solution.py:438
  98.5 2.8 %collective-permute-start.22 = (bf16[128,768]{1,0:T(8,128)(2,1)S(1)}, bf16[128,768]{1,0:T(8,128)(2,1)S(1)}, u32[]{:S(2)}, u32[]{:S(2)}) collective-permute-start(bf16[128,768]{1,0:T(8,128)(2,1)S(1)} %get-tuple-element.52), channel_id=1, source_target_pairs={{0,3},{1,0},{2,1},{3,2},{4,7},{5,4},{6,5},{7,6},{8,11},{9,8},{10,9... | collective-permute-start | bytes 589832 | tf_op jit(solution)/shard_map/ppermute | solution.py:438
  101.4 3.5 %collective-permute-start.21 = (bf16[128,768]{1,0:T(8,128)(2,1)S(1)}, bf16[128,768]{1,0:T(8,128)(2,1)S(1)}, u32[]{:S(2)}, u32[]{:S(2)}) collective-permute-start(bf16[128,768]{1,0:T(8,128)(2,1)S(1)} %add_convert_fusion.3), channel_id=1, source_target_pairs={{0,3},{1,0},{2,1},{3,2},{4,7},{5,4},{6,5},{7,6},{8,11},{9,8},{10,9... | collective-permute-start | bytes 589832 | tf_op jit(solution)/shard_map/ppermute | solution.py:438
  105.5 2.8 %collective-permute-done.23.direct_b_ref = bf16[128,768]{1,0:T(8,128)(2,1)S(1)} collective-permute-done((bf16[128,768]{1,0:T(8,128)(2,1)S(1)}, bf16[128,768]{1,0:T(8,128)(2,1)S(1)}, u32[]{:S(2)}, u32[]{:S(2)}) %collective-permute-start.23) | collective-permute-done | bytes 196640 | tf_op jit(solution)/shard_map/ppermute | solution.py:438
  109.7 2.8 %collective-permute-done.19.sum_a_ref = bf16[128,768]{1,0:T(8,128)(2,1)S(1)} collective-permute-done((bf16[128,768]{1,0:T(8,128)(2,1)S(1)}, bf16[128,768]{1,0:T(8,128)(2,1)S(1)}, u32[]{:S(2)}, u32[]{:S(2)}) %collective-permute-start.19) | collective-permute-done | bytes 196640 | tf_op jit(solution)/shard_map/ppermute | solution.py:438
  (55 shorter events, 14.0 us)
Async XLA Ops:
  7.0 6.9 %collective-permute-start = (bf16[768,768]{1,0:T(8,128)(2,1)}, bf16[768,768]{1,0:T(8,128)(2,1)S(1)}, u32[]{:S(2)}, u32[]{:S(2)}) collective-permute-start(bf16[768,768]{1,0:T(8,128)(2,1)} %get-tuple-element.32), channel_id=1, source_target_pairs={{0,4},{4,0},{8,12},{12,8},{16,20},{20,16},{24,28},{28,24},{32,36},... | collective-permute-start | bytes 3538952 | tf_op jit(solution)/shard_map/ppermute | solution.py:57
  10.4 3.5 %collective-permute-start.1 = (bf16[768,384]{1,0:T(8,128)(2,1)}, bf16[768,384]{1,0:T(8,128)(2,1)S(1)}, u32[]{:S(2)}, u32[]{:S(2)}) collective-permute-start(bf16[768,384]{1,0:T(8,128)(2,1)} %get-tuple-element.34), channel_id=1, source_target_pairs={{0,4},{4,0},{8,12},{12,8},{16,20},{20,16},{24,28},{28,24},{32,36},... | collective-permute-start | bytes 1769480 | tf_op jit(solution)/shard_map/ppermute | solution.py:57
  14.2 7.9 %collective-permute-start.2 = (bf16[96,1152]{1,0:T(8,128)(2,1)S(1)}, bf16[96,1152]{1,0:T(8,128)(2,1)S(1)}, u32[]{:S(2)}, u32[]{:S(2)}) collective-permute-start(bf16[96,1152]{1,0:T(8,128)(2,1)S(1)} %get-tuple-element.36), channel_id=1, source_target_pairs={{0,64},{4,68},{8,72},{12,76},{16,80},{20,84},{24,88},{28,92},{32,9... | collective-permute-start | bytes 663560 | tf_op jit(solution)/shard_map/ppermute | solution.py:438
  14.3 8.0 %collective-permute-start.4 = (bf16[96,1152]{1,0:T(8,128)(2,1)S(1)}, bf16[96,1152]{1,0:T(8,128)(2,1)S(1)}, u32[]{:S(2)}, u32[]{:S(2)}) collective-permute-start(bf16[96,1152]{1,0:T(8,128)(2,1)S(1)} %get-tuple-element.38), channel_id=1, source_target_pairs={{0,192},{4,196},{8,200},{12,204},{16,208},{20,212},{24,216},{28,22... | collective-permute-start | bytes 663560 | tf_op jit(solution)/shard_map/ppermute | solution.py:438
  17.0 8.9 %collective-permute-start.6 = (bf16[96,1152]{1,0:T(8,128)(2,1)S(1)}, bf16[96,1152]{1,0:T(8,128)(2,1)S(1)}, u32[]{:S(2)}, u32[]{:S(2)}) collective-permute-start(bf16[96,1152]{1,0:T(8,128)(2,1)S(1)} %get-tuple-element.39), channel_id=1, source_target_pairs={{0,192},{4,196},{8,200},{12,204},{16,208},{20,212},{24,216},{28,22... | collective-permute-start | bytes 663560 | tf_op jit(solution)/shard_map/ppermute | solution.py:438
  17.0 8.8 %collective-permute-start.7 = (bf16[96,1152]{1,0:T(8,128)(2,1)S(1)}, bf16[96,1152]{1,0:T(8,128)(2,1)S(1)}, u32[]{:S(2)}, u32[]{:S(2)}) collective-permute-start(bf16[96,1152]{1,0:T(8,128)(2,1)S(1)} %get-tuple-element.40), channel_id=1, source_target_pairs={{0,8},{4,12},{8,0},{12,4},{16,24},{20,28},{24,16},{28,20},{32,40},... | collective-permute-start | bytes 663560 | tf_op jit(solution)/shard_map/ppermute | solution.py:438
  18.4 9.7 %collective-permute-start.8 = (bf16[96,1152]{1,0:T(8,128)(2,1)S(1)}, bf16[96,1152]{1,0:T(8,128)(2,1)S(1)}, u32[]{:S(2)}, u32[]{:S(2)}) collective-permute-start(bf16[96,1152]{1,0:T(8,128)(2,1)S(1)} %get-tuple-element.41), channel_id=1, source_target_pairs={{0,72},{4,76},{8,64},{12,68},{16,88},{20,92},{24,80},{28,84},{32,1... | collective-permute-start | bytes 663560 | tf_op jit(solution)/shard_map/ppermute | solution.py:438
  22.2 11.7 %collective-permute-start.3 = (bf16[96,1152]{1,0:T(8,128)(2,1)S(1)}, bf16[96,1152]{1,0:T(8,128)(2,1)S(1)}, u32[]{:S(2)}, u32[]{:S(2)}) collective-permute-start(bf16[96,1152]{1,0:T(8,128)(2,1)S(1)} %add_convert_fusion.2), channel_id=1, source_target_pairs={{0,64},{4,68},{8,72},{12,76},{16,80},{20,84},{24,88},{28,92},{32,9... | collective-permute-start | bytes 663560 | tf_op jit(solution)/shard_map/ppermute | solution.py:438
  22.4 11.6 %collective-permute-start.5 = (bf16[96,1152]{1,0:T(8,128)(2,1)S(1)}, bf16[96,1152]{1,0:T(8,128)(2,1)S(1)}, u32[]{:S(2)}, u32[]{:S(2)}) collective-permute-start(bf16[96,1152]{1,0:T(8,128)(2,1)S(1)} %add_convert_fusion.1), channel_id=1, source_target_pairs={{0,200},{4,204},{8,192},{12,196},{16,216},{20,220},{24,208},{28,21... | collective-permute-start | bytes 663560 | tf_op jit(solution)/shard_map/ppermute | solution.py:438
  63.0 6.3 %collective-permute-start.11 = (bf16[96,1152]{1,0:T(8,128)(2,1)S(1)}, bf16[96,1152]{1,0:T(8,128)(2,1)S(1)}, u32[]{:S(2)}, u32[]{:S(2)}) collective-permute-start(bf16[96,1152]{1,0:T(8,128)(2,1)S(1)} %bitcast.11), channel_id=1, source_target_pairs={{0,64},{4,68},{8,72},{12,76},{16,80},{20,84},{24,88},{28,92},{32,9... | collective-permute-start | bytes 663560 | tf_op jit(solution)/shard_map/ppermute | solution.py:438
  63.2 6.0 %collective-permute-start.10 = (bf16[96,1152]{1,0:T(8,128)(2,1)S(1)}, bf16[96,1152]{1,0:T(8,128)(2,1)S(1)}, u32[]{:S(2)}, u32[]{:S(2)}) collective-permute-start(bf16[96,1152]{1,0:T(8,128)(2,1)S(1)} %bitcast.9), channel_id=1, source_target_pairs={{0,192},{4,196},{8,200},{12,204},{16,208},{20,212},{24,216},{28,22... | collective-permute-start | bytes 663560 | tf_op jit(solution)/shard_map/ppermute | solution.py:438
  65.9 6.9 %collective-permute-start.9 = (bf16[96,1152]{1,0:T(8,128)(2,1)S(1)}, bf16[96,1152]{1,0:T(8,128)(2,1)S(1)}, u32[]{:S(2)}, u32[]{:S(2)}) collective-permute-start(bf16[96,1152]{1,0:T(8,128)(2,1)S(1)} %bitcast.12), channel_id=1, source_target_pairs={{0,192},{4,196},{8,200},{12,204},{16,208},{20,212},{24,216},{28,22... | collective-permute-start | bytes 663560 | tf_op jit(solution)/shard_map/ppermute | solution.py:438
  66.3 8.5 %collective-permute-start.14 = (bf16[96,1152]{1,0:T(8,128)(2,1)S(1)}, bf16[96,1152]{1,0:T(8,128)(2,1)S(1)}, u32[]{:S(2)}, u32[]{:S(2)}) collective-permute-start(bf16[96,1152]{1,0:T(8,128)(2,1)S(1)} %bitcast.10), channel_id=1, source_target_pairs={{0,64},{4,68},{8,72},{12,76},{16,80},{20,84},{24,88},{28,92},{32,9... | collective-permute-start | bytes 663560 | tf_op jit(solution)/shard_map/ppermute | solution.py:438
  69.2 10.4 %collective-permute-start.12 = (bf16[96,1152]{1,0:T(8,128)(2,1)S(1)}, bf16[96,1152]{1,0:T(8,128)(2,1)S(1)}, u32[]{:S(2)}, u32[]{:S(2)}) collective-permute-start(bf16[96,1152]{1,0:T(8,128)(2,1)S(1)} %collective-permute-done.11.rest_4_), channel_id=1, source_target_pairs={{0,64},{4,68},{8,72},{12,76},{16,80},{20,84},{24,88},{28,92},{32,9... | collective-permute-start | bytes 663560 | tf_op jit(solution)/shard_map/ppermute | solution.py:438
  69.2 10.4 %collective-permute-start.13 = (bf16[96,1152]{1,0:T(8,128)(2,1)S(1)}, bf16[96,1152]{1,0:T(8,128)(2,1)S(1)}, u32[]{:S(2)}, u32[]{:S(2)}) collective-permute-start(bf16[96,1152]{1,0:T(8,128)(2,1)S(1)} %collective-permute-done.10.rest_1_), channel_id=1, source_target_pairs={{0,192},{4,196},{8,200},{12,204},{16,208},{20,212},{24,216},{28,22... | collective-permute-start | bytes 663560 | tf_op jit(solution)/shard_map/ppermute | solution.py:438
  79.7 8.5 %collective-permute-start.17 = (bf16[768,384]{1,0:T(8,128)(2,1)S(1)}, bf16[768,384]{1,0:T(8,128)(2,1)S(1)}, u32[]{:S(2)}, u32[]{:S(2)}) collective-permute-start(bf16[768,384]{1,0:T(8,128)(2,1)S(1)} %get-tuple-element.46.a_ref), channel_id=1, source_target_pairs={{0,4},{4,0},{8,12},{12,8},{16,20},{20,16},{24,28},{28,24},{32,36},... | collective-permute-start | bytes 1769480 | tf_op jit(solution)/shard_map/ppermute | solution.py:57
  87.6 5.4 %collective-permute-start.15 = (bf16[384,768]{1,0:T(8,128)(2,1)S(1)}, bf16[384,768]{1,0:T(8,128)(2,1)S(1)}, u32[]{:S(2)}, u32[]{:S(2)}) collective-permute-start(bf16[384,768]{1,0:T(8,128)(2,1)S(1)} %get-tuple-element.44.own_a), channel_id=1, source_target_pairs={{0,4},{4,0},{8,12},{12,8},{16,20},{20,16},{24,28},{28,24},{32,36},... | collective-permute-start | bytes 1769480 | tf_op jit(solution)/shard_map/ppermute | solution.py:57
  87.7 5.3 %collective-permute-start.16 = (bf16[384,768]{1,0:T(8,128)(2,1)S(1)}, bf16[384,768]{1,0:T(8,128)(2,1)S(1)}, u32[]{:S(2)}, u32[]{:S(2)}) collective-permute-start(bf16[384,768]{1,0:T(8,128)(2,1)S(1)} %get-tuple-element.45.own_b), channel_id=1, source_target_pairs={{0,4},{4,0},{8,12},{12,8},{16,20},{20,16},{24,28},{28,24},{32,36},... | collective-permute-start | bytes 1769480 | tf_op jit(solution)/shard_map/ppermute | solution.py:57
  94.8 6.5 %collective-permute-start.20 = (bf16[128,768]{1,0:T(8,128)(2,1)S(1)}, bf16[128,768]{1,0:T(8,128)(2,1)S(1)}, u32[]{:S(2)}, u32[]{:S(2)}) collective-permute-start(bf16[128,768]{1,0:T(8,128)(2,1)S(1)} %get-tuple-element.51), channel_id=1, source_target_pairs={{0,3},{1,0},{2,1},{3,2},{4,7},{5,4},{6,5},{7,6},{8,11},{9,8},{10,9... | collective-permute-start | bytes 589832 | tf_op jit(solution)/shard_map/ppermute | solution.py:438
  97.4 7.5 %collective-permute-start.18 = (bf16[128,768]{1,0:T(8,128)(2,1)S(1)}, bf16[128,768]{1,0:T(8,128)(2,1)S(1)}, u32[]{:S(2)}, u32[]{:S(2)}) collective-permute-start(bf16[128,768]{1,0:T(8,128)(2,1)S(1)} %get-tuple-element.49), channel_id=1, source_target_pairs={{0,1},{1,2},{2,3},{3,0},{4,5},{5,6},{6,7},{7,4},{8,9},{9,10},{10,1... | collective-permute-start | bytes 589832 | tf_op jit(solution)/shard_map/ppermute | solution.py:438
  98.5 7.0 %collective-permute-start.22 = (bf16[128,768]{1,0:T(8,128)(2,1)S(1)}, bf16[128,768]{1,0:T(8,128)(2,1)S(1)}, u32[]{:S(2)}, u32[]{:S(2)}) collective-permute-start(bf16[128,768]{1,0:T(8,128)(2,1)S(1)} %get-tuple-element.52), channel_id=1, source_target_pairs={{0,3},{1,0},{2,1},{3,2},{4,7},{5,4},{6,5},{7,6},{8,11},{9,8},{10,9... | collective-permute-start | bytes 589832 | tf_op jit(solution)/shard_map/ppermute | solution.py:438
  101.3 7.1 %collective-permute-start.23 = (bf16[128,768]{1,0:T(8,128)(2,1)S(1)}, bf16[128,768]{1,0:T(8,128)(2,1)S(1)}, u32[]{:S(2)}, u32[]{:S(2)}) collective-permute-start(bf16[128,768]{1,0:T(8,128)(2,1)S(1)} %get-tuple-element.53), channel_id=1, source_target_pairs={{0,1},{1,2},{2,3},{3,0},{4,5},{5,6},{6,7},{7,4},{8,9},{9,10},{10,1... | collective-permute-start | bytes 589832 | tf_op jit(solution)/shard_map/ppermute | solution.py:438
  101.4 8.3 %collective-permute-start.21 = (bf16[128,768]{1,0:T(8,128)(2,1)S(1)}, bf16[128,768]{1,0:T(8,128)(2,1)S(1)}, u32[]{:S(2)}, u32[]{:S(2)}) collective-permute-start(bf16[128,768]{1,0:T(8,128)(2,1)S(1)} %add_convert_fusion.3), channel_id=1, source_target_pairs={{0,3},{1,0},{2,1},{3,2},{4,7},{5,4},{6,5},{7,6},{8,11},{9,8},{10,9... | collective-permute-start | bytes 589832 | tf_op jit(solution)/shard_map/ppermute | solution.py:438
  104.9 7.6 %collective-permute-start.19 = (bf16[128,768]{1,0:T(8,128)(2,1)S(1)}, bf16[128,768]{1,0:T(8,128)(2,1)S(1)}, u32[]{:S(2)}, u32[]{:S(2)}) collective-permute-start(bf16[128,768]{1,0:T(8,128)(2,1)S(1)} %add_convert_fusion.4), channel_id=1, source_target_pairs={{0,1},{1,2},{2,3},{3,0},{4,5},{5,6},{6,7},{7,4},{8,9},{9,10},{10,1... | collective-permute-start | bytes 589832 | tf_op jit(solution)/shard_map/ppermute | solution.py:438
  (6 other events, 69.7 us)
